TPU v7x, 32 devices: a whole 2x2x4 slice. The times are simulated.
32 devices in a mesh: row: 8 (over z, y), col: 4 (over x, core).
Axes of the slice: x: 2, y: 2, z: 4, core: 2. Of those that a mesh axis runs over, the one named last changes fastest.
Arguments:
- covariance: float32 [12288, 12288], P('row', 'col'), may hold values from -6 to 6
- blocks: float32 [48, 5, 256, 256], P('col', None, 'row'), may hold values from -0.15625 to 0.15625
- present: int32 [48, 5], replicated, may hold values 0 or 1
- model_noise: float32 [12288, 12288], P('col', 'row'), may hold values from -6 to 6
Outputs:
- forecast: float32 [12288, 12288], P('col', 'row')
All inputs are finite; a program needn't handle non-finite values.
Results may differ from a plain program's by a relative error of at most 0.000057.
Values sent between devices are 32-bit elements; how exact they have to be, the bound alone decides.
No kernel may reach another device: no remote copies, remote signals or barrier semaphores. Data moves between devices by JAX's collectives and lax.ppermute only.
A program may use at most 320 MiB of HBM per device.

v0:
```python
import jax
import jax.numpy as jnp
from jax import lax
from jax.sharding import PartitionSpec as P


def spread(array, axis, root):
    mine = lax.axis_index(axis) == root
    return lax.psum(jnp.where(mine, array, jnp.zeros_like(array)), axis)


def padded_2(cells, sides, width):
    for axis, dim in sides:
        count = lax.axis_size(axis)
        ends = count - 1
        head = lax.slice_in_dim(cells, 0, width, axis=dim)
        tail = lax.slice_in_dim(cells, cells.shape[dim] - width, cells.shape[dim], axis=dim)
        cells = jnp.concatenate(
            [
                lax.ppermute(tail, axis, [(i, (i + 1) % count) for i in range(ends)]),
                cells,
                lax.ppermute(head, axis, [((i + 1) % count, i) for i in range(ends)]),
            ],
            axis=dim,
        )
    return cells


def band_apply(live_band, padded):
    blocks_here = live_band.shape[0]
    block_size = live_band.shape[2]
    columns = padded.shape[1]
    summed = None
    for diagonal in range(5):
        window = padded[diagonal * block_size : (diagonal + blocks_here) * block_size].reshape(
            blocks_here, block_size, columns
        )
        term = jnp.einsum(
            "bij,bjw->biw",
            live_band[:, diagonal],
            window,
            precision=lax.Precision.HIGHEST,
            preferred_element_type=jnp.float32,
        )
        summed = term if summed is None else summed + term
    return summed.reshape(blocks_here * block_size, columns)


def banded(live_band, field, halo_fn):
    return band_apply(live_band, halo_fn(field))


def body(covariance, blocks, present, model_noise):
    row_index = lax.axis_index("row")
    col_index = lax.axis_index("col")
    ratio = lax.axis_size("row") // lax.axis_size("col")
    column_band = lax.all_gather(blocks, "row", axis=2, tiled=True)
    col_blocks = column_band.shape[0]
    row_blocks = col_blocks // ratio
    own_part = lax.dynamic_slice_in_dim(column_band, row_index % ratio * row_blocks, row_blocks, 0)
    row_band = spread(own_part, "col", row_index // ratio)
    flags = present.astype(jnp.float32)
    col_flags = lax.dynamic_slice_in_dim(flags, col_index * col_blocks, col_blocks, 0)
    row_flags = lax.dynamic_slice_in_dim(flags, row_index * row_blocks, row_blocks, 0)
    live_col = column_band * col_flags[:, :, None, None]
    live_row = row_band * row_flags[:, :, None, None]
    margin = 2 * blocks.shape[3]

    def row_margin(field):
        return padded_2(field, (("row", 0),), margin)

    def col_margin(field):
        return padded_2(field, (("col", 0),), margin)

    mapped = banded(live_row, covariance, row_margin)
    second = banded(live_col, mapped.T, col_margin)
    return second + model_noise


def solution(mesh):
    in_specs = (P("row", "col"), P("col", None, "row", None), P(), P("col", "row"))
    out_specs = P("col", "row")
    return jax.shard_map(body, mesh=mesh, in_specs=in_specs, out_specs=out_specs, check_vma=False)
```

profile of v0, /device:TPU:24, one launch (start us, length us, event | category | flops | bytes accessed | tf_op | source)
XLA Modules:
  0.0 1051.5 jit_solution(14286111718665589921)
XLA Ops:
  6.5 0.0 all-gather.2.cloned.1.call-start
  6.5 3.1 copy.5
  9.6 0.0 all-gather.2.cloned.1.call-update
  9.6 0.0 all-reduce.2.cloned.1.call-start
  9.7 11.6 %fusion.14 = (f32[512,3072]{1,0:T(8,128)}, f32[512,3072]{1,0:T(8,128)}) fusion(f32[1536,3072]{1,0:T(8,128)} %param.4), kind=kLoop, calls=%fused_computation.42 | loop fusion | bytes 25165824 | tf_op jit(solution)/shard_map/slice | solution.py:17
  21.3 3.4 collective-permute-start
  24.8 3.3 collective-permute-start.1
  28.1 0.0 copy-start.1
  28.1 0.1 constant_dynamic-slice_fusion
  28.2 256.6 %collective-permute-done = f32[512,3072]{1,0:T(8,128)} collective-permute-done((f32[512,3072]{1,0:T(8,128)}, f32[512,3072]{1,0:T(8,128)}, u32[]{:S(2)}, u32[]{:S(2)}) %collective-permute-start) | collective-permute-done | bytes 6291488 | tf_op jit(solution)/shard_map/ppermute | solution.py:20
  284.8 6.2 constant_dynamic-update-slice_fusion.1
  291.0 18.5 %constant_dynamic-update-slice_fusion = (f32[2048,3072]{1,0:T(8,128)}, f32[2048,3072]{1,0:T(8,128)}) fusion(f32[2048,3072]{1,0:T(8,128)} %constant_dynamic-update-slice_fusion.1, f32[1536,3072]{1,0:T(8,128)} %param.4), kind=kLoop, calls=%fused_computation.33 | loop fusion | bytes 56623104 | tf_op jit(solution)/shard_map/concatenate | solution.py:18
  309.5 88.5 %collective-permute-done.1 = f32[512,3072]{1,0:T(8,128)} collective-permute-done((f32[512,3072]{1,0:T(8,128)}, f32[512,3072]{1,0:T(8,128)}, u32[]{:S(2)}, u32[]{:S(2)}) %collective-permute-start.1) | collective-permute-done | bytes 6291488 | tf_op jit(solution)/shard_map/ppermute | solution.py:22
  398.0 6.2 constant_dynamic-update-slice_fusion.2
  404.2 30.5 %all-gather.2.cloned.1.call-done = f32[12,5,256,256]{3,2,0,1:T(8,128)} async-done(((f32[12,5,32,256]{3,2,0,1:T(8,128)}), f32[12,5,256,256]{3,2,0,1:T(8,128)}) %all-gather.2.cloned.1.call-update) | async-done | bytes 15728656 | tf_op jit(solution)/shard_map/all_gather | solution.py:57
  434.7 7.2 dynamic-slice_select_fusion
  441.9 0.0 all-reduce.2.cloned.1.call-update
  441.9 26.8 %fusion.11 = (f32[1536,3072]{1,0:T(8,128)}, f32[1536,3072]{1,0:T(8,128)}) fusion(f32[2048,3072]{1,0:T(8,128)} %constant_dynamic-update-slice_fusion.2), kind=kLoop, calls=%fused_computation.39 | loop fusion | bytes 75497472 | tf_op jit(solution)/shard_map/slice | solution.py:35
  468.7 26.7 %fusion.12 = (f32[1536,3072]{1,0:T(8,128)}, f32[1536,3072]{1,0:T(8,128)}) fusion(f32[2048,3072]{1,0:T(8,128)} %get-tuple-element.17), kind=kLoop, calls=%fused_computation.40 | loop fusion | bytes 75497472 | tf_op jit(solution)/shard_map/slice | solution.py:35
  495.4 92.8 %all-reduce.2.cloned.1.call-done = f32[6,5,256,256]{3,2,0,1:T(8,128)} async-done(((f32[6,5,256,256]{3,2,0,1:T(8,128)}), f32[6,5,256,256]{3,2,0,1:T(8,128)}) %all-reduce.2.cloned.1.call-update) | async-done | bytes 7864336 | tf_op jit(solution)/shard_map/psum | solution.py:9
  588.2 4.1 broadcast_multiply_fusion.1
  592.3 25.3 %fusion.7 = f32[6,256,3072]{2,1,0:T(8,128)} fusion(f32[6,256,3072]{2,1,0:T(8,128)} %bitcast.69, f32[6,5,256,256]{3,2,0,1:T(8,128)S(1)} %broadcast_multiply_fusion.1), kind=kOutput, calls=%fused_computation.26 | convolution fusion | flops 14495514624 | bytes 39321600 | tf_op jit(solution)/shard_map/bij,bjw->biw/dot_general | solution.py:38
  617.6 0.0 slice-start.2
  617.7 23.0 %fusion.10 = f32[6,256,3072]{2,1,0:T(8,128)} fusion(f32[6,256,3072]{2,1,0:T(8,128)} %bitcast.71, f32[6,5,256,256]{3,2,0,1:T(8,128)S(1)} %broadcast_multiply_fusion.1), kind=kOutput, calls=%fused_computation.32 | convolution fusion | flops 14495514624 | bytes 39321600 | tf_op jit(solution)/shard_map/bij,bjw->biw/dot_general | solution.py:38
  640.7 23.3 %fusion.9 = f32[6,256,3072]{2,1,0:T(8,128)} fusion(f32[6,256,3072]{2,1,0:T(8,128)} %bitcast.70, f32[6,5,256,256]{3,2,0,1:T(8,128)} %copy-done), kind=kOutput, calls=%fused_computation.30 | convolution fusion | flops 14495514624 | bytes 39321600 | tf_op jit(solution)/shard_map/bij,bjw->biw/dot_general | solution.py:38
  664.0 0.0 slice-done
  664.0 0.0 slice-done.2
  664.0 21.3 %fusion.8 = f32[6,256,3072]{2,1,0:T(8,128)} fusion(f32[6,256,3072]{2,1,0:T(8,128)S(1)} %bitcast.62, f32[6,5,256,256]{3,2,0,1:T(8,128)} %copy-done), kind=kOutput, calls=%fused_computation.28 | convolution fusion | flops 14495514624 | bytes 39321600 | tf_op jit(solution)/shard_map/bij,bjw->biw/dot_general | solution.py:38
  685.3 38.6 %add_add_fusion.1 = f32[6,256,3072]{2,1,0:T(8,128)} fusion(f32[6,256,3072]{2,1,0:T(8,128)} %fusion.7, f32[6,256,3072]{2,1,0:T(8,128)} %fusion.8, f32[6,256,3072]{2,1,0:T(8,128)} %fusion.10, f32[6,256,3072]{2,1,0:T(8,128)} %fusion.9, f32[6,256,3072]{2,1,0:T(8,128)} %bitcast.68, f32[6,5,256,256]{3,2,0,1:T(8,128)} %copy-done), kind=kOutput, calls=%fused_computation.10 | convolution fusion | flops 14514388992 | bytes 114819072 | tf_op jit(solution)/shard_map/bij,bjw->biw/dot_general | solution.py:38
  723.9 6.3 fusion.13
  730.1 1.6 collective-permute-start.2
  731.8 1.3 collective-permute-start.3
  733.1 0.1 constant_dynamic-slice_fusion.1
  733.1 11.5 %broadcast_multiply_fusion = f32[12,5,256,256]{3,2,0,1:T(8,128)} fusion(f32[12,5,256,256]{3,2,0,1:T(8,128)} %all-gather.2.cloned.1.call-done, f32[12,5]{0,1:T(8,128)S(1)} %constant_dynamic-slice_fusion.1), kind=kLoop, calls=%fused_computation.12 | loop fusion | flops 3932160 | bytes 31457520 | tf_op jit(solution)/shard_map/mul | solution.py:65
  744.7 18.6 %copy.8 = f32[3072,1536]{1,0:T(8,128)} copy(f32[3072,1536]{0,1:T(8,128)} %bitcast.58) | data formatting | bytes 37748736 | tf_op jit(solution)/shard_map/transpose | solution.py:76
  763.3 24.4 %fusion.3 = f32[12,256,1536]{2,1,0:T(8,128)} fusion(f32[12,256,1536]{2,1,0:T(8,128)} %bitcast.66, f32[12,5,256,256]{3,2,0,1:T(8,128)} %broadcast_multiply_fusion), kind=kOutput, calls=%fused_computation.18 | convolution fusion | flops 14495514624 | bytes 40894464 | tf_op jit(solution)/shard_map/bij,bjw->biw/dot_general | solution.py:38
  787.7 0.0 collective-permute-done.2
  787.7 0.0 collective-permute-done.3
  787.7 48.1 %pad_maximum_fusion = (f32[3072,1536]{0,1:T(8,128)}, f32[3072,1536]{0,1:T(8,128)}, f32[3072,1536]{0,1:T(8,128)}, f32[3072,1536]{0,1:T(8,128)}) fusion(f32[512,1536]{0,1:T(8,128)} %collective-permute-done.3, f32[3072,1536]{0,1:T(8,128)} %bitcast.59, f32[512,1536]{0,1:T(8,128)S(1)} %collective-permute-done.2), kind=kLoop, calls=%fused_computation.6 | loop fusion | flops 18874368 | bytes 100663296 | tf_op jit(solution)/shard_map/concatenate | solution.py:18
  835.8 18.7 %copy.7 = f32[3072,1536]{1,0:T(8,128)} copy(f32[3072,1536]{0,1:T(8,128)} %get-tuple-element.14) | data formatting | bytes 37748736 | tf_op jit(solution)/shard_map/slice | solution.py:35
  854.5 24.4 %fusion.4 = f32[12,256,1536]{2,1,0:T(8,128)} fusion(f32[12,256,1536]{2,1,0:T(8,128)} %bitcast.63, f32[12,5,256,256]{3,2,0,1:T(8,128)} %broadcast_multiply_fusion), kind=kOutput, calls=%fused_computation.20 | convolution fusion | flops 14495514624 | bytes 40894464 | tf_op jit(solution)/shard_map/bij,bjw->biw/dot_general | solution.py:38
  878.9 18.7 %copy.6 = f32[3072,1536]{1,0:T(8,128)} copy(f32[3072,1536]{0,1:T(8,128)} %get-tuple-element.13) | data formatting | bytes 37748736 | tf_op jit(solution)/shard_map/slice | solution.py:35
  897.5 24.6 %fusion.5 = f32[12,256,1536]{2,1,0:T(8,128)} fusion(f32[12,256,1536]{2,1,0:T(8,128)} %bitcast.64, f32[12,5,256,256]{3,2,0,1:T(8,128)} %broadcast_multiply_fusion), kind=kOutput, calls=%fused_computation.22 | convolution fusion | flops 14495514624 | bytes 40894464 | tf_op jit(solution)/shard_map/bij,bjw->biw/dot_general | solution.py:38
  922.1 18.7 %copy.9 = f32[3072,1536]{1,0:T(8,128)} copy(f32[3072,1536]{0,1:T(8,128)} %get-tuple-element.10) | data formatting | bytes 37748736 | tf_op jit(solution)/shard_map/slice | solution.py:35
  940.7 24.7 %fusion.2 = f32[12,256,1536]{2,1,0:T(8,128)} fusion(f32[12,256,1536]{2,1,0:T(8,128)} %bitcast.65, f32[12,5,256,256]{3,2,0,1:T(8,128)} %broadcast_multiply_fusion), kind=kOutput, calls=%fused_computation.16 | convolution fusion | flops 14495514624 | bytes 40894464 | tf_op jit(solution)/shard_map/bij,bjw->biw/dot_general | solution.py:38
  965.4 18.6 %copy.10 = f32[3072,1536]{1,0:T(8,128)} copy(f32[3072,1536]{0,1:T(8,128)} %get-tuple-element.9) | data formatting | bytes 37748736 | tf_op jit(solution)/shard_map/slice | solution.py:35
  984.1 40.1 %add_add_fusion = f32[12,256,1536]{2,1,0:T(8,128)} fusion(f32[12,256,1536]{2,1,0:T(8,128)} %fusion.2, f32[12,256,1536]{2,1,0:T(8,128)} %fusion.3, f32[12,256,1536]{2,1,0:T(8,128)} %fusion.5, f32[12,256,1536]{2,1,0:T(8,128)} %fusion.4, f32[12,256,1536]{2,1,0:T(8,128)} %bitcast.67, f32[12,5,256,256]{3,2,0,1:T(8,128)} %broadcast_multiply_fusion), kind=kOutput, calls=%fused_computation.9 | convolution fusion | flops 14514388992 | bytes 116391936 | tf_op jit(solution)/shard_map/bij,bjw->biw/dot_general | solution.py:38
  1024.2 20.0 %bitcast_add_fusion = f32[3072,1536]{1,0:T(8,128)} fusion(f32[3072,1536]{1,0:T(8,128)} %param.7, f32[12,256,1536]{2,1,0:T(8,128)} %add_add_fusion), kind=kLoop, calls=%fused_computation.8 | loop fusion | flops 4718592 | bytes 56623104 | tf_op jit(solution)/shard_map/add | solution.py:77
  (16 shorter events, 0.0 us)
Async XLA Ops:
  6.5 21.6 %copy-start.3 = (s32[48,5]{0,1:T(8,128)S(1)}, s32[48,5]{0,1:T(8,128)}, u32[]{:S(2)}) copy-start(s32[48,5]{0,1:T(8,128)} %param.6) | copy-start | bytes 2884
  6.5 428.1 %all-gather.2.cloned.1.call-start = ((), (), s32[]{:S(2)}) async-start(), calls=%async_computation | async-start | bytes 17694720 | tf_op jit(solution)/shard_map/all_gather | solution.py:57
  9.6 578.5 %all-reduce.2.cloned.1.call-start = ((), (), s32[]{:S(2)}) async-start(), calls=%async_computation.1 | async-start | bytes 15728640 | tf_op jit(solution)/shard_map/psum | solution.py:9
  21.3 263.5 %collective-permute-start = (f32[512,3072]{1,0:T(8,128)}, f32[512,3072]{1,0:T(8,128)}, u32[]{:S(2)}, u32[]{:S(2)}) collective-permute-start(f32[512,3072]{1,0:T(8,128)} %get-tuple-element.19), channel_id=1, source_target_pairs={{0,4},{4,8},{8,12},{12,16},{16,20},{20,24},{24,28},{1,5},{5,9},{9,... | collective-permute-start | bytes 18874376 | tf_op jit(solution)/shard_map/ppermute | solution.py:20
  24.8 373.3 %collective-permute-start.1 = (f32[512,3072]{1,0:T(8,128)}, f32[512,3072]{1,0:T(8,128)}, u32[]{:S(2)}, u32[]{:S(2)}) collective-permute-start(f32[512,3072]{1,0:T(8,128)} %get-tuple-element.20), channel_id=1, source_target_pairs={{4,0},{8,4},{12,8},{16,12},{20,16},{24,20},{28,24},{5,1},{9,5},{13... | collective-permute-start | bytes 18874376 | tf_op jit(solution)/shard_map/ppermute | solution.py:22
  28.1 281.4 %copy-start.1 = (f32[48,5]{0,1:T(8,128)}, f32[48,5]{0,1:T(8,128)S(1)}, u32[]{:S(2)}) copy-start(f32[48,5]{0,1:T(8,128)S(1)} %convert_element_type.3) | copy-start | bytes 2884
  592.3 25.3 %copy-start = (f32[6,5,256,256]{3,2,0,1:T(8,128)}, f32[6,5,256,256]{3,2,0,1:T(8,128)S(1)}, u32[]{:S(2)}) copy-start(f32[6,5,256,256]{3,2,0,1:T(8,128)S(1)} %broadcast_multiply_fusion.1) | copy-start | bytes 23592964
  617.6 46.3 %slice-start = ((s8[18874368]{0:T(1024)(128)(4,1)}), s8[4194304]{0:T(1024)(128)(4,1)S(1)}, s32[]{:S(2)}) async-start(s8[18874368]{0:T(1024)(128)(4,1)} %bitcast.60), calls=%async_computation.2 | async-start | bytes 8388608
  617.6 46.3 %slice-start.1 = ((s8[18874368]{0:T(1024)(128)(4,1)}), s8[4194304]{0:T(1024)(128)(4,1)S(1)}, s32[]{:S(2)}) async-start(s8[18874368]{0:T(1024)(128)(4,1)} %bitcast.60), calls=%async_computation.3 | async-start | bytes 8388608
  617.6 46.3 %slice-start.2 = ((s8[18874368]{0:T(1024)(128)(4,1)}), s8[4194304]{0:T(1024)(128)(4,1)S(1)}, s32[]{:S(2)}) async-start(s8[18874368]{0:T(1024)(128)(4,1)} %bitcast.60), calls=%async_computation.4 | async-start | bytes 8388608
  640.7 23.3 %slice-start.3 = ((s8[18874368]{0:T(1024)(128)(4,1)}), s8[4194304]{0:T(1024)(128)(4,1)S(1)}, s32[]{:S(2)}) async-start(s8[18874368]{0:T(1024)(128)(4,1)} %bitcast.60), calls=%async_computation.5 | async-start | bytes 8388608
  640.7 23.3 %slice-start.4 = ((s8[18874368]{0:T(1024)(128)(4,1)}), s8[2097152]{0:T(1024)(128)(4,1)S(1)}, s32[]{:S(2)}) async-start(s8[18874368]{0:T(1024)(128)(4,1)} %bitcast.60), calls=%async_computation.6 | async-start | bytes 4194304
  685.3 47.8 %copy-start.2 = (f32[48,5]{0,1:T(8,128)S(1)}, f32[48,5]{0,1:T(8,128)}, u32[]{:S(2)}) copy-start(f32[48,5]{0,1:T(8,128)} %copy-done.1) | copy-start | bytes 2884
  730.1 57.6 %collective-permute-start.2 = (f32[512,1536]{0,1:T(8,128)}, f32[512,1536]{0,1:T(8,128)S(1)}, u32[]{:S(2)}, u32[]{:S(2)}) collective-permute-start(f32[512,1536]{0,1:T(8,128)} %get-tuple-element.15), channel_id=1, source_target_pairs={{0,1},{1,2},{2,3},{4,5},{5,6},{6,7},{8,9},{9,10},{10,11},{12,13},{... | collective-permute-start | bytes 9437192 | tf_op jit(solution)/shard_map/ppermute | solution.py:20
  731.8 56.0 %collective-permute-start.3 = (f32[512,1536]{0,1:T(8,128)}, f32[512,1536]{0,1:T(8,128)}, u32[]{:S(2)}, u32[]{:S(2)}) collective-permute-start(f32[512,1536]{0,1:T(8,128)} %get-tuple-element.16), channel_id=1, source_target_pairs={{1,0},{2,1},{3,2},{5,4},{6,5},{7,6},{9,8},{10,9},{11,10},{13,12},{... | collective-permute-start | bytes 9437192 | tf_op jit(solution)/shard_map/ppermute | solution.py:22
Sparse Core Ops, SparseCore 0:
  9.8 424.8 all-gather.1
  442.0 146.1 all-reduce.1
where the time goes:
time: 1060 us; the launch traced here: 1050 us
  waiting for transfers between devices  468 us (44%)
  matrix products  270 us (25%)
  local copies, waits for them, and re-layouts  199 us (19%)
  other arithmetic  90.9 us (9%)
  between operations  14.1 us (1%)
    dot_general x10, matrix products, band_apply(): jnp.einsum('bij,bjw->biw', live_band[:, diagonal], window, precision=lax....  270 us
    ppermute x2, waiting for transfers between devices, padded_2(): lax.ppermute(tail, axis, [(i, (i + 1) % count) for i in range(ends)])  257 us
    slice x6, local copies, waits for them, and re-layouts, band_apply(): padded[diagonal * block_size:(diagonal + blocks_here) * block_size]  128 us
    psum x1, waiting for transfers between devices, spread(): return lax.psum(jnp.where(mine, array, jnp.zeros_like(array)), axis)  92.8 us
    ppermute x2, waiting for transfers between devices, padded_2(): lax.ppermute(head, axis, [((i + 1) % count, i) for i in range(ends)])  88.5 us
    concatenate x1, other arithmetic, padded_2(): jnp.concatenate([lax.ppermute(tail, axis, [(i, (i + 1) % count) for i in...  48.1 us
    all_gather x1, waiting for transfers between devices, body(): column_band = lax.all_gather(blocks, 'row', axis=2, tiled=True)  30.5 us
    concatenate x2, local copies, waits for them, and re-layouts, padded_2(): jnp.concatenate([lax.ppermute(tail, axis, [(i, (i + 1) % count) for i in...  24.6 us
  transfers between devices with their start and end apart: 6, of which 4 were waited for; matrix products, arithmetic and copies ran while one was open for 14% of the time, Pallas kernels for 0%

commit v1 on v0

--- a/solution.py
+++ b/solution.py
@@ -1,7 +1,214 @@
+import functools
+
 import jax
 import jax.numpy as jnp
 from jax import lax
+from jax.experimental import pallas as pl
+from jax.experimental.pallas import tpu as pltpu
 from jax.sharding import PartitionSpec as P
+
+F32 = jnp.float32
+BF16 = jnp.bfloat16
+BS = 256
+MARGIN = 2 * BS
+WIDE = 5 * BS
+N = MARGIN
+VMEM_BYTES = 56 * 2**20
+
+
+def after(values, others):
+    return lax.optimization_barrier((tuple(values), tuple(others)))[0]
+
+
+def call(kernel, name, prefetch, grid, in_specs, out_specs, out_shape, scratch, args, flops, alias=None):
+    moved = sum(a.size * a.dtype.itemsize for a in args) // 2
+    return pl.pallas_call(
+        kernel,
+        grid_spec=pltpu.PrefetchScalarGridSpec(
+            num_scalar_prefetch=len(prefetch), grid=grid, in_specs=in_specs, out_specs=out_specs, scratch_shapes=scratch
+        ),
+        out_shape=out_shape,
+        input_output_aliases=alias or {},
+        compiler_params=pltpu.CompilerParams(vmem_limit_bytes=VMEM_BYTES),
+        cost_estimate=pl.CostEstimate(flops=flops, bytes_accessed=moved, transcendentals=0),
+        name=name,
+    )(*prefetch, *args)
+
+
+def split_into(high_ref, low_ref, rows, value):
+    high = value.astype(BF16)
+    high_ref[rows, :] = high
+    low_ref[rows, :] = (value - high.astype(F32)).astype(BF16)
+
+
+def dot3(a_high, a_low, b_high, b_low):
+    dot = functools.partial(jnp.dot, preferred_element_type=F32)
+    return dot(a_high, b_high) + (dot(a_high, b_low) + dot(a_low, b_high))
+
+
+def place_kernel(count, use, source, first, flags, *refs):
+    pieces, outs = refs[:count], refs[count:]
+    block = pl.program_id(0)
+    slab = pieces[0].shape[3]
+
+    for i, piece in enumerate(pieces):
+
+        @pl.when(use[i] != 0)
+        def _(i=i, piece=piece):
+            for slot in range(2):
+                side = first[i] if slot == 0 else 1 - first[i]
+                rows = pl.ds(pl.multiple_of((source[i] * 2 + side) * slab, slab), slab)
+                for d in range(5):
+                    value = piece[slot, 0, d]
+                    columns = pl.ds(d * BS, BS)
+                    live = value * flags[block * 5 + d].astype(F32)
+                    high = live.astype(BF16)
+                    outs[0][0, rows, columns] = high
+                    outs[1][0, rows, columns] = (live - high.astype(F32)).astype(BF16)
+
+
+def place(candidates, flags):
+    pieces = [a for a, _, _, _ in candidates]
+    table = [jnp.stack([jnp.asarray(c[k], jnp.int32) for c in candidates]) for k in (1, 2, 3)]
+    _, blocks, _, slab, _ = pieces[0].shape
+
+    def spec(i):
+        return pl.BlockSpec((2, 1, 5, slab, BS), lambda b, use, *_: (0, b * use[i], 0, 0, 0))
+
+    out = pl.BlockSpec((1, BS, WIDE), lambda b, *_: (b, 0, 0))
+    return call(
+        functools.partial(place_kernel, len(pieces)), "place_slabs", table + [flags], (blocks,),
+        [spec(i) for i in range(len(pieces))], [out] * 2,
+        [jax.ShapeDtypeStruct((blocks, BS, WIDE), BF16)] * 2, [], pieces, 0,
+    )
+
+
+def inner_kernel(count, y, own, *refs):
+    nears, (high_a, low_a, high_b, low_b, out, b_high, b_low) = refs[:count], refs[count:]
+    step = pl.program_id(0)
+    rows = own.shape[0]
+    split_into(b_high, b_low, pl.ds(pl.multiple_of(y[0] * MARGIN, MARGIN), rows), own[...])
+    at = pl.ds(pl.multiple_of((1 - y[0]) * rows, MARGIN), MARGIN)
+    for i, near in enumerate(nears):
+
+        @pl.when(step == i)
+        def _(near=near):
+            split_into(b_high, b_low, at, near[...])
+
+    for j in range(4):
+        high, low = (high_a, low_a) if j < 2 else (high_b, low_b)
+        window = pl.ds(j * BS, WIDE)
+        out[:, j * BS : (j + 1) * BS] = dot3(high[j % 2], low[j % 2], b_high[window, :], b_low[window, :]).T
+
+
+def map_inner(y, covariance, nears, row_high, row_low):
+    rows, columns = covariance.shape
+    pair_a = pl.BlockSpec((2, BS, WIDE), lambda s, y: (1 - y[0], 0, 0))
+    pair_b = pl.BlockSpec((2, BS, WIDE), lambda s, y: (2 - y[0], 0, 0))
+    return call(
+        functools.partial(inner_kernel, len(nears)), "map_inner", [y], (columns // N,),
+        [pl.BlockSpec((rows, N), lambda s, y: (0, s))]
+        + [pl.BlockSpec((MARGIN, N), lambda s, y: (0, 0))] * len(nears)
+        + [pair_a, pair_a, pair_b, pair_b],
+        pl.BlockSpec((N, 4 * BS), lambda s, y: (s + 1, 0)),
+        jax.ShapeDtypeStruct((columns + 2 * MARGIN, 4 * BS), F32),
+        [pltpu.VMEM((rows + MARGIN, N), BF16)] * 2,
+        [covariance, *nears, row_high, row_low, row_high, row_low], 6 * 4 * BS * WIDE * columns,
+    )
+
+
+def outer_kernel(y, own_a, own_b, far, high, low, out, b_high, b_low):
+    at = lambda k: pl.ds(pl.multiple_of(k * MARGIN, MARGIN), MARGIN)
+    split_into(b_high, b_low, at(1 - y[0]), own_a[...])
+    split_into(b_high, b_low, at(2 - y[0]), own_b[...])
+    split_into(b_high, b_low, at(2 * y[0]), far[...])
+    for j in range(2):
+        window = pl.ds(j * BS, WIDE)
+        out[:, j * BS : (j + 1) * BS] = dot3(high[j], low[j], b_high[window, :], b_low[window, :]).T
+
+
+def map_outer(y, covariance, far, row_high, row_low, chunk):
+    pair = pl.BlockSpec((2, BS, WIDE), lambda s, y: (2 * y[0], 0, 0))
+    return call(
+        outer_kernel, "map_outer", [y], (1,),
+        [
+            pl.BlockSpec((MARGIN, N), lambda s, y: (y[0], chunk)),
+            pl.BlockSpec((MARGIN, N), lambda s, y: (y[0] + 1, chunk)),
+            pl.BlockSpec((MARGIN, N), lambda s, y: (0, 0)),
+            pair, pair,
+        ],
+        pl.BlockSpec((N, 2 * BS), lambda s, y: (0, 0)),
+        jax.ShapeDtypeStruct((N, 2 * BS), F32),
+        [pltpu.VMEM((3 * MARGIN, N), BF16)] * 2,
+        [covariance, covariance, far, row_high, row_low], 6 * 2 * BS * WIDE * N,
+    )
+
+
+def cast_inner_kernel(aliased, table, padded, high, low, noise, *rest):
+    out, b_high, b_low = rest[aliased:]
+    step = pl.program_id(0)
+    split_into(b_high, b_low, pl.ds(pl.multiple_of(step * BS, BS), BS), padded[...])
+
+    @pl.when(step >= 4)
+    def _():
+        window = pl.ds(pl.multiple_of((step - 4) * BS, BS), WIDE)
+        out[...] = noise[...] + dot3(high[0], low[0], b_high[window, :], b_low[window, :])
+
+
+def cast_inner(table, padded, high, low, noise, forecast):
+    blocks, width = high.shape[0], padded.shape[1]
+    row = lambda s: jnp.maximum(s - 4, 0)
+    place = pl.BlockSpec(
+        (pl.Element(BS), pl.Element(width)), lambda s, t: (pl.multiple_of((t[0] + row(s)) * BS, BS), pl.multiple_of(t[1], N))
+    )
+    band = pl.BlockSpec((1, BS, WIDE), lambda s, t: (row(s), 0, 0))
+    aliased = forecast is not None
+    return call(
+        functools.partial(cast_inner_kernel, int(aliased)), "cast_inner", [table], (blocks + 4,),
+        [pl.BlockSpec((BS, width), lambda s, t: (t[0] + s, 0)), band, band, place]
+        + [pl.BlockSpec(memory_space=pl.ANY)] * aliased,
+        place, jax.ShapeDtypeStruct(noise.shape, F32), [pltpu.VMEM(((blocks + 4) * BS, width), BF16)] * 2,
+        [padded, high, low, noise] + [forecast] * aliased, 6 * blocks * BS * WIDE * width,
+        {5: 0} if aliased else None,
+    )
+
+
+def cast_outer_kernel(count, table, *refs):
+    parts, (high_a, low_a, high_b, low_b, noise, _, out, b_high, b_low) = refs[:count], refs[count:]
+    step = pl.program_id(0)
+
+    @pl.when(step == 0)
+    def _():
+        for i, part in enumerate(parts):
+            split_into(b_high, b_low, pl.ds(i * MARGIN, MARGIN), part[...])
+
+    window = pl.ds(pl.multiple_of(table[step, 1] * BS, BS), WIDE)
+
+    @pl.when(table[step, 2] == 0)
+    def _():
+        out[...] = noise[...] + dot3(high_a[0], low_a[0], b_high[window, :], b_low[window, :])
+
+    @pl.when(table[step, 2] != 0)
+    def _():
+        out[...] = noise[...] + dot3(high_b[0], low_b[0], b_high[window, :], b_low[window, :])
+
+
+def cast_outer(y, rows, starts, parts, bands, noise, forecast):
+    blocks = bands[0][0].shape[0]
+    table = jnp.array([[row, start, row // blocks, row % blocks] for row, start in zip(rows, starts)], jnp.int32)
+    table = table.at[:, 2].set((table[:, 2] + y) % 2)
+    column = jnp.broadcast_to(2 * y, (len(rows), 1))
+    table = jnp.concatenate([table, column], axis=1)
+    place = pl.BlockSpec((BS, N), lambda s, t: (t[s, 0], t[s, 4]))
+    band_a = pl.BlockSpec((1, BS, WIDE), lambda s, t: (t[s, 3] * (1 - t[s, 2]), 0, 0))
+    band_b = pl.BlockSpec((1, BS, WIDE), lambda s, t: (t[s, 3] * t[s, 2], 0, 0))
+    whole = pl.BlockSpec((MARGIN, N), lambda s, t: (0, 0))
+    return call(
+        functools.partial(cast_outer_kernel, len(parts)), "cast_outer", [table], (len(rows),),
+        [whole] * len(parts) + [band_a, band_a, band_b, band_b, place, pl.BlockSpec(memory_space=pl.ANY)],
+        place, jax.ShapeDtypeStruct(noise.shape, F32), [pltpu.VMEM((len(parts) * MARGIN, N), BF16)] * 2,
+        [*parts, *bands[0], *bands[1], noise, forecast], 6 * len(rows) * BS * WIDE * N, {len(parts) + 6: 0},
+    )
 
 
 def spread(array, axis, root):
@@ -50,7 +257,7 @@
     return band_apply(live_band, halo_fn(field))
 
 
-def body(covariance, blocks, present, model_noise):
+def plain_body(covariance, blocks, present, model_noise):
     row_index = lax.axis_index("row")
     col_index = lax.axis_index("col")
     ratio = lax.axis_size("row") // lax.axis_size("col")
@@ -77,7 +284,191 @@
     return second + model_noise
 
 
+def body(covariance, blocks, present, model_noise):
+    rows, cols = lax.axis_size("row"), lax.axis_size("col")
+    r, c = lax.axis_index("row"), lax.axis_index("col")
+    z, y = r // 2, r % 2
+    depth = rows // 2
+    col_blocks, _, slab, _ = blocks.shape
+    part_blocks = col_blocks // 2
+    swap = [(i, i ^ 1) for i in range(rows)]
+    permute = lax.ppermute
+    y_table = jnp.reshape(y, (1,)).astype(jnp.int32)
+
+    sliced = blocks.reshape(2, part_blocks, 5, slab, BS)
+    pick = lambda part: lax.dynamic_index_in_dim(sliced, part % 2, 0, False)
+
+    def along(k, long, ends=True):
+        hops = []
+        for i in range(k - 1, depth - 1):
+            hops.append((2 * i, 2 * i + 2) if long else (2 * i + 1, 2 * i + 3))
+        for i in range(0, depth - k):
+            hops.append((2 * i + 3, 2 * i + 1) if long else (2 * i + 2, 2 * i))
+        return [(a, b) for a, b in hops if ends or b not in (0, rows - 1)]
+
+    home = r // 2
+    bits = [1 << b for b in reversed(range(cols.bit_length() - 1))]
+
+    def senders(missing, bit, keep):
+        pairs_of = [(i, a) for i in range(rows) if keep(i) for a in range(cols) if ((a ^ (i // 2)) & missing) == 0]
+        return [(i * cols + a, i * cols + (a ^ bit)) for i, a in pairs_of]
+
+    def keeps(k, long):
+        def keep(i):
+            up = (i % 2 == 0) == long
+            return i // 2 >= k if up else i // 2 + k < depth
+
+        return keep
+
+    axes = ("row", "col")
+    at_home, at_mate = c == home, c == home ^ bits[0]
+
+    extra = covariance.shape[0] - MARGIN
+    count = covariance.shape[1] // N
+    chunks = sorted(range(count), key=lambda s: min(s, count - 1 - s))
+    hops = [(i, i + 1) for i in range(1, rows - 1, 2)] + [(i + 1, i) for i in range(1, rows - 1, 2)]
+    near_parts = [(lax.dynamic_slice(covariance, (extra * (1 - y), i * N), (MARGIN, N)), "row", swap) for i in range(count)]
+    far_parts = [(lax.dynamic_slice(covariance, (extra * y, i * N), (MARGIN, N)), "row", hops) for i in chunks]
+
+    def send(jobs, *others):
+        values = after([job[0] for job in jobs], others)
+        return [permute(value, axis, perm) for value, (_, axis, perm) in zip(values, jobs)]
+
+    trips = near_parts + far_parts
+    long0, short0, long1, short1 = ([] for _ in range(4))
+    passed = {}
+    trades = [permute(pick(1 - y), "row", swap)]
+    pair0 = jnp.stack([pick(y), trades[0]])
+    long0.append(pair0)
+    short0.append(pair0)
+    over = [None]
+
+    def relays(k):
+        jobs = [(long0[k], axes, senders(cols - 1, bits[0], keeps(k, True)))]
+        return jobs if k == 0 else jobs + [(short0[k], axes, senders(cols - 1, bits[0], keeps(k, False)))]
+
+    def climbed(k, up):
+        return jnp.where(up, z >= k, z + k < depth), jnp.where(up, z - k, z + k)
+
+    def entry(value, k, up, when, first=y):
+        held, source = climbed(k, up)
+        return value, held & when, jnp.clip(source, 0, depth - 1), first
+
+    end = ((y == 0) & (z == 0)) | ((y == 1) & (z == depth - 1))
+    always = z >= 0
+    row_flags = lax.dynamic_slice_in_dim(present, r * part_blocks, part_blocks, 0).reshape(-1)
+
+    def place_rows():
+        table = []
+        for k in range(depth):
+            for i, (long, value) in enumerate(((True, long0[k]), (False, short0[k]))):
+                if k == 0 and not long:
+                    continue
+                up = (y == 0) if long else (y == 1)
+                got = passed[k, i][0]
+                pairs_of = senders(cols - 1 - bits[0], bits[1], keeps(k, long))
+                beside = permute(jnp.where(at_mate, got, value), axes, pairs_of)
+                table += [entry(value, k, up, at_home), entry(got, k, up, at_mate), entry(beside, k, up, ~(at_home | at_mate))]
+        return place(table, row_flags)
+
+    def place_columns(phase):
+        table = [entry((pair0, pair1)[phase], 0, True, always)]
+        for k in range(1, depth):
+            if phase == 0:
+                table += [entry(long0[k], k, y == 0, always), entry(short0[k], k, y == 1, always)]
+            else:
+                table += [entry(long1[k], k, y == 0, always), entry(over[k], k, y == 1, end, 1 - y)]
+                if k < depth - 1:
+                    table.append(entry(short1[k], k, y == 1, ~end))
+        base = c * col_blocks + (y + phase) % 2 * part_blocks
+        return place(table, lax.dynamic_slice_in_dim(present, base, part_blocks, 0).reshape(-1))
+
+    def inner_table(phase):
+        return jnp.stack([(y + phase) % 2 * part_blocks, (1 - y) * N]).astype(jnp.int32)
+
+    def arrived(i):
+        return even[(i + 1) // 2] if i % 2 else odd[i // 2]
+
+    up, down = [(i, i + 1) for i in range(cols - 1)], [(i + 1, i) for i in range(cols - 1)]
+    mapped = {}
+    even, odd, stage = [], [], [trades[0]]
+    for s in range(1, count + 2):
+        jobs, sinks = [(pick(1 - y + 1), "row", swap) if s == 1 else trips[2 * s - 3]], [even]
+        if s < depth:
+            jobs += [(long0[s - 1], "row", along(s, True)), (short0[s - 1], "row", along(s, False))]
+            sinks += [long0, short0]
+        if s == depth - 1 or s == depth:
+            k = s - depth + 2
+            if k == 1:
+                short1.append(pair1)
+            jobs.append((short1[k - 1], "row", along(k, False, False)))
+            sinks.append(short1)
+        if depth <= s < 2 * depth - 1:
+            k = s - depth + 1
+            if k == 1:
+                long1.append(pair1)
+            jobs.append((long1[k - 1], "row", along(k, True)))
+            sinks.append(long1)
+        if depth < s < 2 * depth:
+            jobs.append((long0[s - depth], "row", [(1, 0), (rows - 2, rows - 1)]))
+            sinks.append(over)
+        if s <= depth:
+            jobs += relays(s - 1)
+            sinks += [passed.setdefault((s - 1, i), []) for i in range(1 if s == 1 else 2)]
+        results = send(jobs, *stage, *odd[-2:-1])
+        if 2 * s - 2 < len(trips):
+            odd += send([trips[2 * s - 2]], *stage, *odd[-1:])
+        for sink, result in zip(sinks, results):
+            sink.append(result)
+        stage = results
+        if s == 1:
+            pair1 = jnp.stack([pick(y + 1), even[0]])
+        if s == depth:
+            bands = [place_columns(0)]
+            row_high, row_low = place_rows()
+            stage = stage + [bands[0][0], row_high]
+        if s == depth + 1:
+            nears = [arrived(i) for i in range(count)]
+            padded = map_inner(y_table, covariance, nears, row_high, row_low)
+            stage = stage + [padded]
+        if s > depth + 1:
+            for i in range(2 * (s - depth - 2), 2 * (s - depth - 1)):
+                mapped[chunks[i]] = map_outer(y_table, covariance, arrived(count + i), row_high, row_low, chunks[i])
+                stage = stage + [mapped[chunks[i]]]
+        if s == depth + 2:
+            end_row = padded.shape[0] - MARGIN
+            below = permute(padded[end_row - MARGIN : end_row], "col", up)
+            above = permute(padded[MARGIN : 2 * MARGIN], "col", down)
+            padded = lax.dynamic_update_slice(padded, below, (0, 0))
+            padded = lax.dynamic_update_slice(padded, above, (end_row, 0))
+            mapped[-1] = permute(mapped[count - 1], "col", up)
+            mapped[count] = permute(mapped[0], "col", down)
+            forecast = cast_inner(inner_table(0), padded, *bands[0], model_noise, None)
+            stage = stage + [forecast]
+    for i in range(count - 2, count):
+        mapped[chunks[i]] = map_outer(y_table, covariance, arrived(count + i), row_high, row_low, chunks[i])
+    bands.append(place_columns(1))
+
+    forecast = cast_inner(inner_table(1), padded, *bands[1], model_noise, forecast)
+    late = chunks[-1]
+    tail_rows = range(2 * late - 2, 2 * late + 4)
+    tail_parts = range(late - 2, late + 3)
+    last = count - 1
+    head_rows = [b for b in range(col_blocks) if b not in tail_rows]
+    head_parts = [p for p in range(-1, last + 2) if p != late]
+    spot = {2 * p + i: 2 * k + i for k, p in enumerate(head_parts) for i in range(2)}
+    forecast = cast_outer(y, head_rows, [spot[b - 2] for b in head_rows], [mapped[p] for p in head_parts], bands, model_noise, forecast)
+    return cast_outer(y, tail_rows, range(6), [mapped[p] for p in tail_parts], bands, model_noise, forecast)
+
+
 def solution(mesh):
+    rows, cols = mesh.shape["row"], mesh.shape["col"]
     in_specs = (P("row", "col"), P("col", None, "row", None), P(), P("col", "row"))
-    out_specs = P("col", "row")
-    return jax.shard_map(body, mesh=mesh, in_specs=in_specs, out_specs=out_specs, check_vma=False)
+
+    def step(covariance, blocks, present, model_noise):
+        fits = rows == 2 * cols and rows == 8 and blocks.shape[0] == 12 * cols
+        chosen = body if fits and blocks.shape[3] == BS else plain_body
+        inner = jax.shard_map(chosen, mesh=mesh, in_specs=in_specs, out_specs=P("col", "row"), check_vma=False)
+        return inner(covariance, blocks, present, model_noise)
+
+    return step

time: 1060 us -> 566 us (0.53)
  matrix products: 270 us -> 0 us
  waiting for transfers between devices: 468 us -> 223 us
  Pallas kernels: 0 us -> 179 us
  local copies, waits for them, and re-layouts: 199 us -> 37.8 us
  starting transfers between devices: 9.68 us -> 97 us
  other arithmetic: 90.9 us -> 18.7 us
  between operations: 14.1 us -> 1.01 us
    dot_general x10 -> x0, matrix products: 270 us -> none  [band_apply(): jnp.einsum('bij,bjw->biw', live_band[:, diagonal], window, precision=lax....]
    pallas_call x0 -> x14, Pallas kernels: none -> 179 us  [call(): pl.pallas_call(kernel, grid_spec=pltpu.PrefetchScalarGridSpec(num_scalar_...]
    slice x8 -> x2, local copies, waits for them, and re-layouts: 146 us -> 8 us  [the longest x1 4.84 us: body(): above = permute(padded[MARGIN:2 * MARGIN], 'col', down)]
    ppermute x4 -> x46, waiting for transfers between devices: 345 us -> 223 us  [the longest x34 201 us: send(): permute(value, axis, perm)]
    psum x1 -> x0, waiting for transfers between devices: 92.8 us -> none  [spread(): return lax.psum(jnp.where(mine, array, jnp.zeros_like(array)), axis)]
    ppermute x4 -> x46, starting transfers between devices: 9.64 us -> 97 us  [the longest x34 74.4 us: send(): permute(value, axis, perm)]
    concatenate x1 -> x0, other arithmetic: 48.1 us -> none  [padded_2(): jnp.concatenate([lax.ppermute(tail, axis, [(i, (i + 1) % count) for i in...]
    all_gather x1 -> x0, waiting for transfers between devices: 30.5 us -> none  [body(): column_band = lax.all_gather(blocks, 'row', axis=2, tiled=True)]
  transfers between devices with their start and end apart: 6 -> 46, of which waited for: 4 -> 17; matrix products, arithmetic and copies ran while one was open for 14% -> 7% of each run, Pallas kernels for 0% -> 27%
where the time goes in v1:
time: 566 us; the launch traced here: 556 us
  waiting for transfers between devices  223 us (39%)
  Pallas kernels  179 us (32%)
  starting transfers between devices  97 us (17%)
  local copies, waits for them, and re-layouts  37.8 us (7%)
  other arithmetic  18.7 us (3%)
    ppermute x34, waiting for transfers between devices, send(): permute(value, axis, perm)  201 us
    pallas_call x14, Pallas kernels, call(): pl.pallas_call(kernel, grid_spec=pltpu.PrefetchScalarGridSpec(num_scalar_...  179 us
    ppermute x34, starting transfers between devices, send(): permute(value, axis, perm)  74.4 us
    ppermute x1, waiting for transfers between devices, body(): trades = [permute(pick(1 - y), 'row', swap)]  22 us
    select_n x7, other arithmetic, place_rows(): beside = permute(jnp.where(at_mate, got, value), axes, pairs_of)  12.7 us
  transfers between devices with their start and end apart: 46, of which 17 were waited for; matrix products, arithmetic and copies ran while one was open for 7% of the time, Pallas kernels for 27%

profile of v1, /device:TPU:24, one launch (start us, length us, event | category | flops | bytes accessed | tf_op | source)
XLA Modules:
  0.0 556.1 jit_solution(17849386337185681684)
XLA Ops:
  0.0 3.8 constant_dynamic-slice_fusion.5
  5.3 22.0 %collective-permute-done = f32[6,5,32,256]{3,2,1,0:T(8,128)S(1)} collective-permute-done((f32[6,5,32,256]{3,2,1,0:T(8,128)S(1)}, f32[6,5,32,256]{3,2,1,0:T(8,128)S(1)}, u32[]{:S(2)}, u32[]{:S(2)}) %collective-permute-start) | collective-permute-done | bytes 983072 | tf_op jit(solution)/shard_map/ppermute | solution.py:340
  30.2 5.9 %collective-permute-start.2 = (f32[2,6,5,32,256]{4,3,2,1,0:T(8,128)}, f32[2,6,5,32,256]{4,3,2,1,0:T(8,128)}, u32[]{:S(2)}, u32[]{:S(2)}) collective-permute-start(f32[2,6,5,32,256]{4,3,2,1,0:T(8,128)} %pad_maximum_fusion.refs_0_), channel_id=1, source_target_pairs={{4,12},{12,20},{20,28},{8,0},{16,8},{24,16},{5,13},{13,21},{21,29}... | collective-permute-start | bytes 5898248 | tf_op jit(solution)/shard_map/ppermute | solution.py:335
  38.0 8.7 %constant_dynamic-slice_fusion.7 = (f32[512,512]{1,0:T(8,128)}, f32[512,512]{1,0:T(8,128)}, f32[512,512]{1,0:T(8,128)}, f32[512,512]{1,0:T(8,128)}, f32[512,512]...) fusion(f32[1536,3072]{1,0:T(8,128)} %own_b.11, ...), kind=kLoop, calls=%fused_computation.35 | loop fusion | bytes 25165832 | tf_op jit(solution)/shard_map/dynamic_slice | solution.py:331
  48.7 14.3 %collective-permute-done.3 = f32[6,5,32,256]{3,2,1,0:T(8,128)} collective-permute-done((f32[6,5,32,256]{3,2,1,0:T(8,128)}, f32[6,5,32,256]{3,2,1,0:T(8,128)}, u32[]{:S(2)}, u32[]{:S(2)}) %collective-permute-start.3) | collective-permute-done | bytes 983072 | tf_op jit(solution)/shard_map/ppermute | solution.py:335
  63.0 11.7 %collective-permute-done.1.refs_1_.refs_3_ = f32[2,6,5,32,256]{4,3,2,1,0:T(8,128)S(1)} collective-permute-done((f32[2,6,5,32,256]{4,3,2,1,0:T(8,128)}, f32[2,6,5,32,256]{4,3,2,1,0:T(8,128)S(1)}, u32[]{:S(2)}, u32[]{:S(2)}) %collective-permute-start.1) | collective-permute-done | bytes 1966112 | tf_op jit(solution)/shard_map/ppermute | solution.py:335
  79.7 2.5 collective-permute-done.10.refs_0_
  84.9 20.4 %collective-permute-done.7.refs_1_ = f32[512,512]{1,0:T(8,128)S(1)} collective-permute-done((f32[512,512]{1,0:T(8,128)}, f32[512,512]{1,0:T(8,128)S(1)}, u32[]{:S(2)}, u32[]{:S(2)}) %collective-permute-start.7) | collective-permute-done | bytes 1048608 | tf_op jit(solution)/shard_map/ppermute | solution.py:335
  107.1 14.2 %collective-permute-done.5.refs_3_.refs_9_ = f32[2,6,5,32,256]{4,3,2,1,0:T(8,128)} collective-permute-done((f32[2,6,5,32,256]{4,3,2,1,0:T(8,128)S(1)}, f32[2,6,5,32,256]{4,3,2,1,0:T(8,128)}, u32[]{:S(2)}, u32[]{:S(2)}) %collective-permute-start.5) | collective-permute-done | bytes 1966112 | tf_op jit(solution)/shard_map/ppermute | solution.py:335
  121.3 4.0 collective-permute-start.14
  125.2 10.2 %collective-permute-start.11 = (f32[2,6,5,32,256]{4,3,2,1,0:T(8,128)S(1)}, f32[2,6,5,32,256]{4,3,2,1,0:T(8,128)S(1)}, u32[]{:S(2)}, u32[]{:S(2)}) collective-permute-start(f32[2,6,5,32,256]{4,3,2,1,0:T(8,128)S(1)} %pad_maximum_fusion.1.refs_0_), channel_id=1, source_target_pairs={{4,12},{12,20},{16,8},{24,16},{5,13},{13,21},{17,9},{25,17},{6,14}... | collective-permute-start | bytes 5898248 | tf_op jit(solution)/shard_map/ppermute | solution.py:335
  138.3 12.1 %collective-permute-done.14.refs_3_ = f32[512,512]{1,0:T(8,128)} collective-permute-done((f32[512,512]{1,0:T(8,128)S(1)}, f32[512,512]{1,0:T(8,128)}, u32[]{:S(2)}, u32[]{:S(2)}) %collective-permute-start.14) | collective-permute-done | bytes 1048608 | tf_op jit(solution)/shard_map/ppermute | solution.py:335
  151.1 16.3 %collective-permute-done.11.refs_3_ = f32[2,6,5,32,256]{4,3,2,1,0:T(8,128)S(1)} collective-permute-done((f32[2,6,5,32,256]{4,3,2,1,0:T(8,128)S(1)}, f32[2,6,5,32,256]{4,3,2,1,0:T(8,128)S(1)}, u32[]{:S(2)}, u32[]{:S(2)}) %collective-permute-start.11) | collective-permute-done | bytes 1966112 | tf_op jit(solution)/shard_map/ppermute | solution.py:335
  167.5 8.0 %collective-permute-done.12.refs_5_.refs_15_ = f32[2,6,5,32,256]{4,3,2,1,0:T(8,128)S(1)} collective-permute-done((f32[2,6,5,32,256]{4,3,2,1,0:T(8,128)}, f32[2,6,5,32,256]{4,3,2,1,0:T(8,128)S(1)}, u32[]{:S(2)}, u32[]{:S(2)}) %collective-permute-start.12) | collective-permute-done | bytes 1966112 | tf_op jit(solution)/shard_map/ppermute | solution.py:335
  186.1 2.1 broadcast_select_fusion.4
  188.2 3.4 broadcast_select_fusion.3
  197.3 14.4 %collective-permute-done.30.refs_4_ = f32[512,512]{1,0:T(8,128)S(1)} collective-permute-done((f32[512,512]{1,0:T(8,128)S(1)}, f32[512,512]{1,0:T(8,128)S(1)}, u32[]{:S(2)}, u32[]{:S(2)}) %collective-permute-start.30) | collective-permute-done | bytes 1048608 | tf_op jit(solution)/shard_map/ppermute | solution.py:335
  225.3 5.6 collective-permute-start.31
  231.5 10.7 %place_slabs.4 = (bf16[6,256,1280]{2,1,0:T(8,128)(2,1)}, bf16[6,256,1280]{2,1,0:T(8,128)(2,1)}) custom-call(s32[21]{0:T(128)} %stack.359.use, s32[21]{0:T(128)} %stack.360.source, s32[21]{0:T(128)} %stack.361.first, s32[30]{0:T(128)} %reshape.69.flags, f32[2,6,5,32,256]{4,3,2,1,0:T(8,128)} %pad_maximum_fusion.refs_0_, ...), custom_call_target="tpu_custom_call" | custom-call | bytes 20643840 | tf_op jit(solution)/shard_map/place_slabs/pallas_call | solution.py:25
  242.2 25.0 %collective-permute-done.18.refs_5_ = f32[512,512]{1,0:T(8,128)} collective-permute-done((f32[512,512]{1,0:T(8,128)}, f32[512,512]{1,0:T(8,128)}, u32[]{:S(2)}, u32[]{:S(2)}) %collective-permute-start.18) | collective-permute-done | bytes 1048608 | tf_op jit(solution)/shard_map/ppermute | solution.py:335
  267.2 36.9 %map_inner.1 = f32[4096,1024]{1,0:T(8,128)} custom-call(s32[1]{0:T(128)} %bitcast.y, f32[1536,3072]{1,0:T(8,128)} %own_b.11, f32[512,512]{1,0:T(8,128)} %copy-done.43, f32[512,512]{1,0:T(8,128)} %copy-done.44, f32[512,512]{1,0:T(8,128)} %collective-permute-done.17.refs_2_, f32[512,512]{1,0:T(8,128)} %collective-permute-done.14.refs_3_, ...), custom_call_target="tpu_custom_call" | custom-call | flops 24159191040 | bytes 20447232 | tf_op jit(solution)/shard_map/map_inner/pallas_call | solution.py:25
  304.2 3.2 slice.46
  307.3 4.9 collective-permute-start.40
  314.8 9.7 %place_slabs.3 = (bf16[6,256,1280]{2,1,0:T(8,128)(2,1)}, bf16[6,256,1280]{2,1,0:T(8,128)(2,1)}) custom-call(s32[7]{0:T(128)} %stack.327.use, s32[7]{0:T(128)} %stack.335.source, s32[7]{0:T(128)} %stack.336.first, s32[30]{0:T(128)} %reshape.68.flags, f32[2,6,5,32,256]{4,3,2,1,0:T(8,128)} %pad_maximum_fusion.refs_0_, f32[2,6,5,32,256]{4,3,2,1,0:T(8,128)} %copy-done.2, ...), custom_call_target="tpu_custom_call" | custom-call | bytes 6881280 | tf_op jit(solution)/shard_map/place_slabs/pallas_call | solution.py:25
  325.8 2.3 collective-permute-start.35
  328.1 2.1 collective-permute-start.32
  330.2 4.7 collective-permute-start.33
  334.9 22.1 %collective-permute-done.32.far = f32[512,512]{1,0:T(8,128)S(1)} collective-permute-done((f32[512,512]{1,0:T(8,128)S(1)}, f32[512,512]{1,0:T(8,128)S(1)}, u32[]{:S(2)}, u32[]{:S(2)}) %collective-permute-start.32) | collective-permute-done | bytes 1048608 | tf_op jit(solution)/shard_map/ppermute | solution.py:335
  357.0 20.8 %collective-permute-done.33.far = f32[512,512]{1,0:T(8,128)S(1)} collective-permute-done((f32[512,512]{1,0:T(8,128)S(1)}, f32[512,512]{1,0:T(8,128)S(1)}, u32[]{:S(2)}, u32[]{:S(2)}) %collective-permute-start.33) | collective-permute-done | bytes 1048608 | tf_op jit(solution)/shard_map/ppermute | solution.py:335
  379.1 4.8 fusion.4
  386.5 2.9 collective-permute-start.39
  390.1 6.7 %map_outer.8.refs_1_ = f32[512,512]{1,0:T(8,128)} custom-call(s32[1]{0:T(128)} %bitcast.y, f32[1536,3072]{1,0:T(8,128)} %own_b.11, f32[1536,3072]{1,0:T(8,128)} %own_b.11, f32[512,512]{1,0:T(8,128)} %collective-permute-done.31.far, bf16[6,256,1280]{2,1,0:T(8,128)(2,1)} %get-tuple-element.92.high.refs_6_.refs_8_, ...), custom_call_target="tpu_custom_call" | custom-call | flops 2013265920 | bytes 23330816 | tf_op jit(solution)/shard_map/map_outer/pallas_call | solution.py:25
  396.8 6.9 %map_outer.9.refs_5_.refs_4_ = f32[512,512]{1,0:T(8,128)} custom-call(s32[1]{0:T(128)} %bitcast.y, f32[1536,3072]{1,0:T(8,128)} %own_b.11, f32[1536,3072]{1,0:T(8,128)} %own_b.11, f32[512,512]{1,0:T(8,128)} %copy-done.37, bf16[6,256,1280]{2,1,0:T(8,128)(2,1)} %get-tuple-element.92.high.refs_6_.refs_8_, ...), custom_call_target="tpu_custom_call" | custom-call | flops 2013265920 | bytes 23330816 | tf_op jit(solution)/shard_map/map_outer/pallas_call | solution.py:25
  403.7 2.2 collective-permute-start.37
  407.4 21.1 %cast_inner.2.rest_0_ = f32[3072,1536]{1,0:T(8,128)} custom-call(s32[2]{0:T(128)} %pad_add_fusion.table, f32[4096,1024]{1,0:T(8,128)} %constant_dynamic-update-slice_fusion.padded, bf16[6,256,1280]{2,1,0:T(8,128)(2,1)} %get-tuple-element.91.high.refs_7_.refs_5_, bf16[6,256,1280]{2,1,0:T(8,128)(2,1)} %get-tuple-element.104.low.refs_8_.refs_6_, ...), custom_call_target="tpu_custom_call" | custom-call | flops 12079595520 | bytes 21757952 | tf_op jit(solution)/shard_map/cast_inner/pallas_call | solution.py:25
  428.5 3.8 collective-permute-done.37.far
  433.0 3.7 collective-permute-start.43
  438.6 4.8 collective-permute-start.42
  450.7 3.3 collective-permute-start.44
  454.0 6.7 %map_outer.6.refs_2_.refs_0_ = f32[512,512]{1,0:T(8,128)} custom-call(s32[1]{0:T(128)} %bitcast.y, f32[1536,3072]{1,0:T(8,128)} %own_b.11, f32[1536,3072]{1,0:T(8,128)} %own_b.11, f32[512,512]{1,0:T(8,128)} %copy-done.35, bf16[6,256,1280]{2,1,0:T(8,128)(2,1)} %get-tuple-element.92.high.refs_6_.refs_8_, ...), custom_call_target="tpu_custom_call" | custom-call | flops 2013265920 | bytes 23330816 | tf_op jit(solution)/shard_map/map_outer/pallas_call | solution.py:25
  460.7 6.7 %map_outer.11.refs_4_.refs_3_ = f32[512,512]{1,0:T(8,128)} custom-call(s32[1]{0:T(128)} %bitcast.y, f32[1536,3072]{1,0:T(8,128)} %own_b.11, f32[1536,3072]{1,0:T(8,128)} %own_b.11, f32[512,512]{1,0:T(8,128)} %copy-done.36, bf16[6,256,1280]{2,1,0:T(8,128)(2,1)} %get-tuple-element.92.high.refs_6_.refs_8_, ...), custom_call_target="tpu_custom_call" | custom-call | flops 2013265920 | bytes 23330816 | tf_op jit(solution)/shard_map/map_outer/pallas_call | solution.py:25
  467.4 6.7 %map_outer.7.refs_3_.refs_1_ = f32[512,512]{1,0:T(8,128)} custom-call(s32[1]{0:T(128)} %bitcast.y, f32[1536,3072]{1,0:T(8,128)} %own_b.11, f32[1536,3072]{1,0:T(8,128)} %own_b.11, f32[512,512]{1,0:T(8,128)} %collective-permute-done.36.far, bf16[6,256,1280]{2,1,0:T(8,128)(2,1)} %get-tuple-element.92.high.refs_6_.refs_8_, ...), custom_call_target="tpu_custom_call" | custom-call | flops 2013265920 | bytes 23330816 | tf_op jit(solution)/shard_map/map_outer/pallas_call | solution.py:25
  474.1 13.2 %collective-permute-done.42.far = f32[512,512]{1,0:T(8,128)} collective-permute-done((f32[512,512]{1,0:T(8,128)}, f32[512,512]{1,0:T(8,128)}, u32[]{:S(2)}, u32[]{:S(2)}) %collective-permute-start.42) | collective-permute-done | bytes 1048608 | tf_op jit(solution)/shard_map/ppermute | solution.py:335
  487.3 6.7 %map_outer.10.refs_2_ = f32[512,512]{1,0:T(8,128)} custom-call(s32[1]{0:T(128)} %bitcast.y, f32[1536,3072]{1,0:T(8,128)} %own_b.11, f32[1536,3072]{1,0:T(8,128)} %own_b.11, f32[512,512]{1,0:T(8,128)} %collective-permute-done.42.far, bf16[6,256,1280]{2,1,0:T(8,128)(2,1)} %get-tuple-element.92.high.refs_6_.refs_8_, ...), custom_call_target="tpu_custom_call" | custom-call | flops 2013265920 | bytes 23330816 | tf_op jit(solution)/shard_map/map_outer/pallas_call | solution.py:25
  493.9 9.7 %place_slabs.5 = (bf16[6,256,1280]{2,1,0:T(8,128)(2,1)}, bf16[6,256,1280]{2,1,0:T(8,128)(2,1)}) custom-call(s32[9]{0:T(128)} %stack.375.use, s32[9]{0:T(128)} %stack.376.source, s32[9]{0:T(128)} %stack.378.first, s32[30]{0:T(128)} %reshape.70.flags, f32[2,6,5,32,256]{4,3,2,1,0:T(8,128)} %copy-done.10, f32[2,6,5,32,256]{4,3,2,1,0:T(8,128)} %collective-permute-done.20.refs_1_, ...), custom_call_target="tpu_custom_call" | custom-call | bytes 8847360 | tf_op jit(solution)/shard_map/place_slabs/pallas_call | solution.py:25
  503.6 20.9 %cast_inner.3.refs_12_ = f32[3072,1536]{1,0:T(8,128)} custom-call(s32[2]{0:T(128)} %pad_add_fusion.1.table, f32[4096,1024]{1,0:T(8,128)} %constant_dynamic-update-slice_fusion.padded, bf16[6,256,1280]{2,1,0:T(8,128)(2,1)} %get-tuple-element.107.high.refs_9_.refs_7_, ...), custom_call_target="tpu_custom_call", output_to_operand_aliasing={{}: (5, {})} | custom-call | flops 12079595520 | bytes 31195136 | tf_op jit(solution)/shard_map/cast_inner/pallas_call | solution.py:25
  526.4 15.4 %cast_outer.2.refs_10_ = f32[3072,1536]{1,0:T(8,128)} custom-call(s32[6,5]{1,0:T(8,128)} %concatenate.11.table, f32[512,512]{1,0:T(8,128)} %copy-done.29, f32[512,512]{1,0:T(8,128)} %map_outer.8.refs_1_, f32[512,512]{1,0:T(8,128)} %map_outer.6.refs_2_.refs_0_, f32[512,512]{1,0:T(8,128)} %map_outer.7.refs_3_.refs_1_, ...), custom_call_target="tpu_custom_call", output_to_operand_aliasing={{}: (13, {})} | custom-call | flops 6039797760 | bytes 30408704 | tf_op jit(solution)/shard_map/cast_outer/pallas_call | solution.py:25
  541.8 14.2 %cast_outer.3 = f32[3072,1536]{1,0:T(8,128)} custom-call(s32[6,5]{1,0:T(8,128)} %concatenate.10.table, f32[512,512]{1,0:T(8,128)} %map_outer.6.refs_2_.refs_0_, f32[512,512]{1,0:T(8,128)} %map_outer.7.refs_3_.refs_1_, f32[512,512]{1,0:T(8,128)} %map_outer.10.refs_2_, f32[512,512]{1,0:T(8,128)} %map_outer.11.refs_4_.refs_3_, ...), custom_call_target="tpu_custom_call", output_to_operand_aliasing={{}: (11, {})} | custom-call | flops 6039797760 | bytes 29360128 | tf_op jit(solution)/shard_map/cast_outer/pallas_call | solution.py:25
  (189 shorter events, 73.1 us)
Async XLA Ops:
  3.8 23.5 %collective-permute-start = (f32[6,5,32,256]{3,2,1,0:T(8,128)S(1)}, f32[6,5,32,256]{3,2,1,0:T(8,128)S(1)}, u32[]{:S(2)}, u32[]{:S(2)}) collective-permute-start(f32[6,5,32,256]{3,2,1,0:T(8,128)S(1)} %get-tuple-element.124), channel_id=1, source_target_pairs={{0,4},{4,0},{8,12},{12,8},{16,20},{20,16},{24,28},{28,24},{1,5},{5... | collective-permute-start | bytes 2949128 | tf_op jit(solution)/shard_map/ppermute | solution.py:340
  28.9 45.8 %collective-permute-start.1 = (f32[2,6,5,32,256]{4,3,2,1,0:T(8,128)}, f32[2,6,5,32,256]{4,3,2,1,0:T(8,128)S(1)}, u32[]{:S(2)}, u32[]{:S(2)}) collective-permute-start(f32[2,6,5,32,256]{4,3,2,1,0:T(8,128)} %pad_maximum_fusion.refs_0_), channel_id=1, source_target_pairs={{0,8},{8,16},{16,24},{12,4},{20,12},{28,20},{1,9},{9,17},{17,25},{... | collective-permute-start | bytes 5898248 | tf_op jit(solution)/shard_map/ppermute | solution.py:335
  30.2 45.8 %collective-permute-start.2 = (f32[2,6,5,32,256]{4,3,2,1,0:T(8,128)}, f32[2,6,5,32,256]{4,3,2,1,0:T(8,128)}, u32[]{:S(2)}, u32[]{:S(2)}) collective-permute-start(f32[2,6,5,32,256]{4,3,2,1,0:T(8,128)} %pad_maximum_fusion.refs_0_), channel_id=1, source_target_pairs={{4,12},{12,20},{20,28},{8,0},{16,8},{24,16},{5,13},{13,21},{21,29}... | collective-permute-start | bytes 5898248 | tf_op jit(solution)/shard_map/ppermute | solution.py:335
  36.1 39.9 %collective-permute-start.4 = (f32[2,6,5,32,256]{4,3,2,1,0:T(8,128)}, f32[2,6,5,32,256]{4,3,2,1,0:T(8,128)}, u32[]{:S(2)}, u32[]{:S(2)}) collective-permute-start(f32[2,6,5,32,256]{4,3,2,1,0:T(8,128)} %pad_maximum_fusion.refs_0_), channel_id=1, source_target_pairs={{0,2},{4,6},{9,11},{13,15},{18,16},{22,20},{27,25},{31,29}} | collective-permute-start | bytes 5898248 | tf_op jit(solution)/shard_map/ppermute | solution.py:335
  38.0 25.0 %collective-permute-start.3 = (f32[6,5,32,256]{3,2,1,0:T(8,128)}, f32[6,5,32,256]{3,2,1,0:T(8,128)}, u32[]{:S(2)}, u32[]{:S(2)}) collective-permute-start(f32[6,5,32,256]{3,2,1,0:T(8,128)} %get-tuple-element.71), channel_id=1, source_target_pairs={{0,4},{4,0},{8,12},{12,8},{16,20},{20,16},{24,28},{28,24},{1,5},{5... | collective-permute-start | bytes 2949128 | tf_op jit(solution)/shard_map/ppermute | solution.py:335
  46.7 35.5 %collective-permute-start.10 = (f32[512,512]{1,0:T(8,128)}, f32[512,512]{1,0:T(8,128)S(1)}, u32[]{:S(2)}, u32[]{:S(2)}) collective-permute-start(f32[512,512]{1,0:T(8,128)} %get-tuple-element.78), channel_id=1, source_target_pairs={{0,4},{4,0},{8,12},{12,8},{16,20},{20,16},{24,28},{28,24},{1,5},{5... | collective-permute-start | bytes 3145736 | tf_op jit(solution)/shard_map/ppermute | solution.py:335
  76.0 45.2 %collective-permute-start.5 = (f32[2,6,5,32,256]{4,3,2,1,0:T(8,128)S(1)}, f32[2,6,5,32,256]{4,3,2,1,0:T(8,128)}, u32[]{:S(2)}, u32[]{:S(2)}) collective-permute-start(f32[2,6,5,32,256]{4,3,2,1,0:T(8,128)S(1)} %collective-permute-done.1.refs_1_.refs_3_), channel_id=1, source_target_pairs={{8,16},{16,24},{12,4},{20,12},{9,17},{17,25},{13,5},{21,13},{10,18... | collective-permute-start | bytes 5898248 | tf_op jit(solution)/shard_map/ppermute | solution.py:335
  77.3 43.9 %collective-permute-start.6 = (f32[2,6,5,32,256]{4,3,2,1,0:T(8,128)}, f32[2,6,5,32,256]{4,3,2,1,0:T(8,128)S(1)}, u32[]{:S(2)}, u32[]{:S(2)}) collective-permute-start(f32[2,6,5,32,256]{4,3,2,1,0:T(8,128)} %collective-permute-done.2.refs_2_.refs_6_), channel_id=1, source_target_pairs={{12,20},{20,28},{8,0},{16,8},{13,21},{21,29},{9,1},{17,9},{14,22},... | collective-permute-start | bytes 5898248 | tf_op jit(solution)/shard_map/ppermute | solution.py:335
  78.1 43.1 %collective-permute-start.8 = (f32[2,6,5,32,256]{4,3,2,1,0:T(8,128)S(1)}, f32[2,6,5,32,256]{4,3,2,1,0:T(8,128)S(1)}, u32[]{:S(2)}, u32[]{:S(2)}) collective-permute-start(f32[2,6,5,32,256]{4,3,2,1,0:T(8,128)S(1)} %collective-permute-done.1.refs_1_.refs_3_), channel_id=1, source_target_pairs={{4,6},{9,11},{13,15},{18,16},{22,20},{27,25}} | collective-permute-start | bytes 5898248 | tf_op jit(solution)/shard_map/ppermute | solution.py:335
  78.9 42.4 %collective-permute-start.9 = (f32[2,6,5,32,256]{4,3,2,1,0:T(8,128)}, f32[2,6,5,32,256]{4,3,2,1,0:T(8,128)S(1)}, u32[]{:S(2)}, u32[]{:S(2)}) collective-permute-start(f32[2,6,5,32,256]{4,3,2,1,0:T(8,128)} %collective-permute-done.2.refs_2_.refs_6_), channel_id=1, source_target_pairs={{0,2},{9,11},{13,15},{18,16},{22,20},{31,29}} | collective-permute-start | bytes 5898248 | tf_op jit(solution)/shard_map/ppermute | solution.py:335
  82.2 23.1 %collective-permute-start.7 = (f32[512,512]{1,0:T(8,128)}, f32[512,512]{1,0:T(8,128)S(1)}, u32[]{:S(2)}, u32[]{:S(2)}) collective-permute-start(f32[512,512]{1,0:T(8,128)} %get-tuple-element.75), channel_id=1, source_target_pairs={{0,4},{4,0},{8,12},{12,8},{16,20},{20,16},{24,28},{28,24},{1,5},{5... | collective-permute-start | bytes 3145736 | tf_op jit(solution)/shard_map/ppermute | solution.py:335
  84.9 90.7 %copy-start.10 = (f32[2,6,5,32,256]{4,3,2,1,0:T(8,128)}, f32[2,6,5,32,256]{4,3,2,1,0:T(8,128)S(1)}, u32[]{:S(2)}) copy-start(f32[2,6,5,32,256]{4,3,2,1,0:T(8,128)S(1)} %pad_maximum_fusion.1.refs_0_) | copy-start | bytes 5898244
  105.3 70.2 %copy-start.44 = (f32[512,512]{1,0:T(8,128)}, f32[512,512]{1,0:T(8,128)S(1)}, u32[]{:S(2)}) copy-start(f32[512,512]{1,0:T(8,128)S(1)} %collective-permute-done.7.refs_1_) | copy-start | bytes 3145732
  105.3 32.2 %collective-permute-start.17 = (f32[512,512]{1,0:T(8,128)S(1)}, f32[512,512]{1,0:T(8,128)}, u32[]{:S(2)}, u32[]{:S(2)}) collective-permute-start(f32[512,512]{1,0:T(8,128)S(1)} %get-tuple-element.85), channel_id=1, source_target_pairs={{0,4},{4,0},{8,12},{12,8},{16,20},{20,16},{24,28},{28,24},{1,5},{5... | collective-permute-start | bytes 3145736 | tf_op jit(solution)/shard_map/ppermute | solution.py:335
  121.3 29.1 %collective-permute-start.14 = (f32[512,512]{1,0:T(8,128)S(1)}, f32[512,512]{1,0:T(8,128)}, u32[]{:S(2)}, u32[]{:S(2)}) collective-permute-start(f32[512,512]{1,0:T(8,128)S(1)} %get-tuple-element.82), channel_id=1, source_target_pairs={{0,4},{4,0},{8,12},{12,8},{16,20},{20,16},{24,28},{28,24},{1,5},{5... | collective-permute-start | bytes 3145736 | tf_op jit(solution)/shard_map/ppermute | solution.py:335
  125.2 42.2 %collective-permute-start.11 = (f32[2,6,5,32,256]{4,3,2,1,0:T(8,128)S(1)}, f32[2,6,5,32,256]{4,3,2,1,0:T(8,128)S(1)}, u32[]{:S(2)}, u32[]{:S(2)}) collective-permute-start(f32[2,6,5,32,256]{4,3,2,1,0:T(8,128)S(1)} %pad_maximum_fusion.1.refs_0_), channel_id=1, source_target_pairs={{4,12},{12,20},{16,8},{24,16},{5,13},{13,21},{17,9},{25,17},{6,14}... | collective-permute-start | bytes 5898248 | tf_op jit(solution)/shard_map/ppermute | solution.py:335
  135.4 40.1 %collective-permute-start.12 = (f32[2,6,5,32,256]{4,3,2,1,0:T(8,128)}, f32[2,6,5,32,256]{4,3,2,1,0:T(8,128)S(1)}, u32[]{:S(2)}, u32[]{:S(2)}) collective-permute-start(f32[2,6,5,32,256]{4,3,2,1,0:T(8,128)} %collective-permute-done.5.refs_3_.refs_9_), channel_id=1, source_target_pairs={{16,24},{12,4},{17,25},{13,5},{18,26},{14,6},{19,27},{15,7}} | collective-permute-start | bytes 5898248 | tf_op jit(solution)/shard_map/ppermute | solution.py:335
  136.7 38.8 %collective-permute-start.13 = (f32[2,6,5,32,256]{4,3,2,1,0:T(8,128)S(1)}, f32[2,6,5,32,256]{4,3,2,1,0:T(8,128)S(1)}, u32[]{:S(2)}, u32[]{:S(2)}) collective-permute-start(f32[2,6,5,32,256]{4,3,2,1,0:T(8,128)S(1)} %collective-permute-done.6.refs_4_.refs_12_), channel_id=1, source_target_pairs={{20,28},{8,0},{21,29},{9,1},{22,30},{10,2},{23,31},{11,3}} | collective-permute-start | bytes 5898248 | tf_op jit(solution)/shard_map/ppermute | solution.py:335
  137.5 38.0 %collective-permute-start.15 = (f32[2,6,5,32,256]{4,3,2,1,0:T(8,128)}, f32[2,6,5,32,256]{4,3,2,1,0:T(8,128)S(1)}, u32[]{:S(2)}, u32[]{:S(2)}) collective-permute-start(f32[2,6,5,32,256]{4,3,2,1,0:T(8,128)} %collective-permute-done.5.refs_3_.refs_9_), channel_id=1, source_target_pairs={{4,6},{13,15},{18,16},{27,25}} | collective-permute-start | bytes 5898248 | tf_op jit(solution)/shard_map/ppermute | solution.py:335
  150.4 25.2 %collective-permute-start.16 = (f32[2,6,5,32,256]{4,3,2,1,0:T(8,128)S(1)}, f32[2,6,5,32,256]{4,3,2,1,0:T(8,128)S(1)}, u32[]{:S(2)}, u32[]{:S(2)}) collective-permute-start(f32[2,6,5,32,256]{4,3,2,1,0:T(8,128)S(1)} %collective-permute-done.6.refs_4_.refs_12_), channel_id=1, source_target_pairs={{0,2},{9,11},{22,20},{31,29}} | collective-permute-start | bytes 5898248 | tf_op jit(solution)/shard_map/ppermute | solution.py:335
  178.1 13.5 %collective-permute-start.21 = (f32[2,6,5,32,256]{4,3,2,1,0:T(8,128)S(1)}, f32[2,6,5,32,256]{4,3,2,1,0:T(8,128)}, u32[]{:S(2)}, u32[]{:S(2)}) collective-permute-start(f32[2,6,5,32,256]{4,3,2,1,0:T(8,128)S(1)} %collective-permute-done.12.refs_5_.refs_15_), channel_id=1, source_target_pairs={{4,6},{27,25}} | collective-permute-start | bytes 5898248 | tf_op jit(solution)/shard_map/ppermute | solution.py:335
  181.8 14.0 %collective-permute-start.23 = (f32[2,6,5,32,256]{4,3,2,1,0:T(8,128)S(1)}, f32[2,6,5,32,256]{4,3,2,1,0:T(8,128)S(1)}, u32[]{:S(2)}, u32[]{:S(2)}) collective-permute-start(f32[2,6,5,32,256]{4,3,2,1,0:T(8,128)S(1)} %broadcast_select_fusion.6), channel_id=1, source_target_pairs={{0,1},{2,3},{4,5},{6,7},{9,8},{11,10},{13,12},{15,14},{16,17},{18,... | collective-permute-start | bytes 5898248 | tf_op jit(solution)/shard_map/ppermute | solution.py:370
  183.3 30.4 %collective-permute-start.22 = (f32[2,6,5,32,256]{4,3,2,1,0:T(8,128)S(1)}, f32[2,6,5,32,256]{4,3,2,1,0:T(8,128)S(1)}, u32[]{:S(2)}, u32[]{:S(2)}) collective-permute-start(f32[2,6,5,32,256]{4,3,2,1,0:T(8,128)S(1)} %copy-done.8), channel_id=1, source_target_pairs={{0,2},{31,29}} | collective-permute-start | bytes 5898248 | tf_op jit(solution)/shard_map/ppermute | solution.py:335
  184.7 32.0 %collective-permute-start.24 = (f32[2,6,5,32,256]{4,3,2,1,0:T(8,128)S(1)}, f32[2,6,5,32,256]{4,3,2,1,0:T(8,128)S(1)}, u32[]{:S(2)}, u32[]{:S(2)}) collective-permute-start(f32[2,6,5,32,256]{4,3,2,1,0:T(8,128)S(1)} %broadcast_select_fusion.5), channel_id=1, source_target_pairs={{4,5},{6,7},{9,8},{11,10},{13,12},{15,14},{16,17},{18,19},{20,21},... | collective-permute-start | bytes 5898248 | tf_op jit(solution)/shard_map/ppermute | solution.py:370
  186.0 25.8 %collective-permute-start.30 = (f32[512,512]{1,0:T(8,128)S(1)}, f32[512,512]{1,0:T(8,128)S(1)}, u32[]{:S(2)}, u32[]{:S(2)}) collective-permute-start(f32[512,512]{1,0:T(8,128)S(1)} %copy-done.34), channel_id=1, source_target_pairs={{0,4},{4,0},{8,12},{12,8},{16,20},{20,16},{24,28},{28,24},{1,5},{5... | collective-permute-start | bytes 3145736 | tf_op jit(solution)/shard_map/ppermute | solution.py:335
  191.6 27.1 %collective-permute-start.25 = (f32[2,6,5,32,256]{4,3,2,1,0:T(8,128)S(1)}, f32[2,6,5,32,256]{4,3,2,1,0:T(8,128)S(1)}, u32[]{:S(2)}, u32[]{:S(2)}) collective-permute-start(f32[2,6,5,32,256]{4,3,2,1,0:T(8,128)S(1)} %broadcast_select_fusion.4), channel_id=1, source_target_pairs={{0,1},{2,3},{9,8},{11,10},{13,12},{15,14},{16,17},{18,19},{20,21},... | collective-permute-start | bytes 5898248 | tf_op jit(solution)/shard_map/ppermute | solution.py:370
  195.8 26.3 %collective-permute-start.26 = (f32[2,6,5,32,256]{4,3,2,1,0:T(8,128)}, f32[2,6,5,32,256]{4,3,2,1,0:T(8,128)}, u32[]{:S(2)}, u32[]{:S(2)}) collective-permute-start(f32[2,6,5,32,256]{4,3,2,1,0:T(8,128)} %broadcast_select_fusion.3), channel_id=1, source_target_pairs={{4,5},{6,7},{13,12},{15,14},{16,17},{18,19},{25,24},{27,26}} | collective-permute-start | bytes 5898248 | tf_op jit(solution)/shard_map/ppermute | solution.py:370
  211.8 12.3 %collective-permute-start.27 = (f32[2,6,5,32,256]{4,3,2,1,0:T(8,128)}, f32[2,6,5,32,256]{4,3,2,1,0:T(8,128)}, u32[]{:S(2)}, u32[]{:S(2)}) collective-permute-start(f32[2,6,5,32,256]{4,3,2,1,0:T(8,128)} %broadcast_select_fusion.2), channel_id=1, source_target_pairs={{0,1},{2,3},{9,8},{11,10},{20,21},{22,23},{29,28},{31,30}} | collective-permute-start | bytes 5898248 | tf_op jit(solution)/shard_map/ppermute | solution.py:370
  213.7 11.6 %collective-permute-start.28 = (f32[2,6,5,32,256]{4,3,2,1,0:T(8,128)}, f32[2,6,5,32,256]{4,3,2,1,0:T(8,128)}, u32[]{:S(2)}, u32[]{:S(2)}) collective-permute-start(f32[2,6,5,32,256]{4,3,2,1,0:T(8,128)} %broadcast_select_fusion.1), channel_id=1, source_target_pairs={{4,5},{6,7},{25,24},{27,26}} | collective-permute-start | bytes 5898248 | tf_op jit(solution)/shard_map/ppermute | solution.py:370
  216.7 14.2 %collective-permute-start.29 = (f32[2,6,5,32,256]{4,3,2,1,0:T(8,128)}, f32[2,6,5,32,256]{4,3,2,1,0:T(8,128)}, u32[]{:S(2)}, u32[]{:S(2)}) collective-permute-start(f32[2,6,5,32,256]{4,3,2,1,0:T(8,128)} %broadcast_select_fusion), channel_id=1, source_target_pairs={{0,1},{2,3},{29,28},{31,30}} | collective-permute-start | bytes 5898248 | tf_op jit(solution)/shard_map/ppermute | solution.py:370
  220.0 47.3 %collective-permute-start.18 = (f32[512,512]{1,0:T(8,128)}, f32[512,512]{1,0:T(8,128)}, u32[]{:S(2)}, u32[]{:S(2)}) collective-permute-start(f32[512,512]{1,0:T(8,128)} %get-tuple-element.86), channel_id=1, source_target_pairs={{0,4},{4,0},{8,12},{12,8},{16,20},{20,16},{24,28},{28,24},{1,5},{5... | collective-permute-start | bytes 3145736 | tf_op jit(solution)/shard_map/ppermute | solution.py:335
  222.1 102.4 %collective-permute-start.19 = (f32[2,6,5,32,256]{4,3,2,1,0:T(8,128)}, f32[2,6,5,32,256]{4,3,2,1,0:T(8,128)}, u32[]{:S(2)}, u32[]{:S(2)}) collective-permute-start(f32[2,6,5,32,256]{4,3,2,1,0:T(8,128)} %copy-done.23), channel_id=1, source_target_pairs={{12,20},{16,8},{13,21},{17,9},{14,22},{18,10},{15,23},{19,11}} | collective-permute-start | bytes 5898248 | tf_op jit(solution)/shard_map/ppermute | solution.py:335
  224.0 100.4 %collective-permute-start.20 = (f32[2,6,5,32,256]{4,3,2,1,0:T(8,128)S(1)}, f32[2,6,5,32,256]{4,3,2,1,0:T(8,128)}, u32[]{:S(2)}, u32[]{:S(2)}) collective-permute-start(f32[2,6,5,32,256]{4,3,2,1,0:T(8,128)S(1)} %copy-done.11), channel_id=1, source_target_pairs={{0,8},{8,16},{16,24},{12,4},{20,12},{28,20},{1,9},{9,17},{17,25},{... | collective-permute-start | bytes 5898248 | tf_op jit(solution)/shard_map/ppermute | solution.py:335
  225.3 102.7 %collective-permute-start.31 = (f32[512,512]{1,0:T(8,128)S(1)}, f32[512,512]{1,0:T(8,128)}, u32[]{:S(2)}, u32[]{:S(2)}) collective-permute-start(f32[512,512]{1,0:T(8,128)S(1)} %copy-done.33), channel_id=1, source_target_pairs={{4,8},{12,16},{20,24},{8,4},{16,12},{24,20},{5,9},{13,17},{21,25},... | collective-permute-start | bytes 3145736 | tf_op jit(solution)/shard_map/ppermute | solution.py:335
  307.3 71.8 %collective-permute-start.40 = (f32[512,1024]{1,0:T(8,128)}, f32[512,1024]{1,0:T(8,128)}, u32[]{:S(2)}, u32[]{:S(2)}) collective-permute-start(f32[512,1024]{1,0:T(8,128)} %slice.46), channel_id=1, source_target_pairs={{0,1},{1,2},{2,3},{4,5},{5,6},{6,7},{8,9},{9,10},{10,11},{12,13},{... | collective-permute-start | bytes 6291464 | tf_op jit(solution)/shard_map/ppermute | solution.py:440
  324.5 53.3 %collective-permute-start.34 = (f32[2,6,5,32,256]{4,3,2,1,0:T(8,128)}, f32[2,6,5,32,256]{4,3,2,1,0:T(8,128)}, u32[]{:S(2)}, u32[]{:S(2)}) collective-permute-start(f32[2,6,5,32,256]{4,3,2,1,0:T(8,128)} %collective-permute-done.20.refs_1_), channel_id=1, source_target_pairs={{8,16},{16,24},{12,4},{20,12},{9,17},{17,25},{13,5},{21,13},{10,18... | collective-permute-start | bytes 5898248 | tf_op jit(solution)/shard_map/ppermute | solution.py:335
  325.8 52.0 %collective-permute-start.35 = (f32[2,6,5,32,256]{4,3,2,1,0:T(8,128)S(1)}, f32[2,6,5,32,256]{4,3,2,1,0:T(8,128)S(1)}, u32[]{:S(2)}, u32[]{:S(2)}) collective-permute-start(f32[2,6,5,32,256]{4,3,2,1,0:T(8,128)S(1)} %copy-done.4), channel_id=1, source_target_pairs={{4,0},{24,28},{5,1},{25,29},{6,2},{26,30},{7,3},{27,31}} | collective-permute-start | bytes 5898248 | tf_op jit(solution)/shard_map/ppermute | solution.py:335
  328.1 28.9 %collective-permute-start.32 = (f32[512,512]{1,0:T(8,128)S(1)}, f32[512,512]{1,0:T(8,128)S(1)}, u32[]{:S(2)}, u32[]{:S(2)}) collective-permute-start(f32[512,512]{1,0:T(8,128)S(1)} %copy-done.32), channel_id=1, source_target_pairs={{4,8},{12,16},{20,24},{8,4},{16,12},{24,20},{5,9},{13,17},{21,25},... | collective-permute-start | bytes 3145736 | tf_op jit(solution)/shard_map/ppermute | solution.py:335
  330.2 47.6 %collective-permute-start.33 = (f32[512,512]{1,0:T(8,128)S(1)}, f32[512,512]{1,0:T(8,128)S(1)}, u32[]{:S(2)}, u32[]{:S(2)}) collective-permute-start(f32[512,512]{1,0:T(8,128)S(1)} %copy-done.31), channel_id=1, source_target_pairs={{4,8},{12,16},{20,24},{8,4},{16,12},{24,20},{5,9},{13,17},{21,25},... | collective-permute-start | bytes 3145736 | tf_op jit(solution)/shard_map/ppermute | solution.py:335
  383.9 22.0 %collective-permute-start.41 = (f32[512,1024]{1,0:T(8,128)}, f32[512,1024]{1,0:T(8,128)S(1)}, u32[]{:S(2)}, u32[]{:S(2)}) collective-permute-start(f32[512,1024]{1,0:T(8,128)} %get-tuple-element.121), channel_id=1, source_target_pairs={{1,0},{2,1},{3,2},{5,4},{6,5},{7,6},{9,8},{10,9},{11,10},{13,12},{... | collective-permute-start | bytes 6291464 | tf_op jit(solution)/shard_map/ppermute | solution.py:441
  385.2 47.7 %collective-permute-start.38 = (f32[2,6,5,32,256]{4,3,2,1,0:T(8,128)}, f32[2,6,5,32,256]{4,3,2,1,0:T(8,128)}, u32[]{:S(2)}, u32[]{:S(2)}) collective-permute-start(f32[2,6,5,32,256]{4,3,2,1,0:T(8,128)} %collective-permute-done.34.refs_4_), channel_id=1, source_target_pairs={{16,24},{12,4},{17,25},{13,5},{18,26},{14,6},{19,27},{15,7}} | collective-permute-start | bytes 5898248 | tf_op jit(solution)/shard_map/ppermute | solution.py:335
  386.5 46.5 %collective-permute-start.39 = (f32[2,6,5,32,256]{4,3,2,1,0:T(8,128)}, f32[2,6,5,32,256]{4,3,2,1,0:T(8,128)}, u32[]{:S(2)}, u32[]{:S(2)}) collective-permute-start(f32[2,6,5,32,256]{4,3,2,1,0:T(8,128)} %collective-permute-done.5.refs_3_.refs_9_), channel_id=1, source_target_pairs={{4,0},{24,28},{5,1},{25,29},{6,2},{26,30},{7,3},{27,31}} | collective-permute-start | bytes 5898248 | tf_op jit(solution)/shard_map/ppermute | solution.py:335
  403.7 28.7 %collective-permute-start.37 = (f32[512,512]{1,0:T(8,128)S(1)}, f32[512,512]{1,0:T(8,128)S(1)}, u32[]{:S(2)}, u32[]{:S(2)}) collective-permute-start(f32[512,512]{1,0:T(8,128)S(1)} %copy-done.30), channel_id=1, source_target_pairs={{4,8},{12,16},{20,24},{8,4},{16,12},{24,20},{5,9},{13,17},{21,25},... | collective-permute-start | bytes 3145736 | tf_op jit(solution)/shard_map/ppermute | solution.py:335
  433.0 60.9 %collective-permute-start.43 = (f32[2,6,5,32,256]{4,3,2,1,0:T(8,128)S(1)}, f32[2,6,5,32,256]{4,3,2,1,0:T(8,128)}, u32[]{:S(2)}, u32[]{:S(2)}) collective-permute-start(f32[2,6,5,32,256]{4,3,2,1,0:T(8,128)S(1)} %copy-done.1), channel_id=1, source_target_pairs={{4,0},{24,28},{5,1},{25,29},{6,2},{26,30},{7,3},{27,31}} | collective-permute-start | bytes 5898248 | tf_op jit(solution)/shard_map/ppermute | solution.py:335
  436.7 30.6 %collective-permute-start.36 = (f32[512,512]{1,0:T(8,128)}, f32[512,512]{1,0:T(8,128)}, u32[]{:S(2)}, u32[]{:S(2)}) collective-permute-start(f32[512,512]{1,0:T(8,128)} %get-tuple-element.100), channel_id=1, source_target_pairs={{4,8},{12,16},{20,24},{8,4},{16,12},{24,20},{5,9},{13,17},{21,25},... | collective-permute-start | bytes 3145736 | tf_op jit(solution)/shard_map/ppermute | solution.py:335
  438.6 48.6 %collective-permute-start.42 = (f32[512,512]{1,0:T(8,128)}, f32[512,512]{1,0:T(8,128)}, u32[]{:S(2)}, u32[]{:S(2)}) collective-permute-start(f32[512,512]{1,0:T(8,128)} %get-tuple-element.105), channel_id=1, source_target_pairs={{4,8},{12,16},{20,24},{8,4},{16,12},{24,20},{5,9},{13,17},{21,25},... | collective-permute-start | bytes 3145736 | tf_op jit(solution)/shard_map/ppermute | solution.py:335
  449.4 75.0 %collective-permute-start.45 = (f32[512,512]{1,0:T(8,128)}, f32[512,512]{1,0:T(8,128)S(1)}, u32[]{:S(2)}, u32[]{:S(2)}) collective-permute-start(f32[512,512]{1,0:T(8,128)} %map_outer.8.refs_1_), channel_id=1, source_target_pairs={{1,0},{2,1},{3,2},{5,4},{6,5},{7,6},{9,8},{10,9},{11,10},{13,12},{... | collective-permute-start | bytes 3145736 | tf_op jit(solution)/shard_map/ppermute | solution.py:445
  450.7 73.7 %collective-permute-start.44 = (f32[512,512]{1,0:T(8,128)S(1)}, f32[512,512]{1,0:T(8,128)S(1)}, u32[]{:S(2)}, u32[]{:S(2)}) collective-permute-start(f32[512,512]{1,0:T(8,128)S(1)} %copy-done.9), channel_id=1, source_target_pairs={{0,1},{1,2},{2,3},{4,5},{5,6},{6,7},{8,9},{9,10},{10,11},{12,13},{... | collective-permute-start | bytes 3145736 | tf_op jit(solution)/shard_map/ppermute | solution.py:444
  (44 other events, 720.6 us)

commit v2 on v0

--- a/solution.py
+++ b/solution.py
@@ -1,7 +1,285 @@
+import functools
+import itertools
+
 import jax
 import jax.numpy as jnp
 from jax import lax
+from jax.experimental import pallas as pl
+from jax.experimental.pallas import tpu as pltpu
 from jax.sharding import PartitionSpec as P
+
+F32 = jnp.float32
+BF16 = jnp.bfloat16
+BS = 256
+MARGIN = 2 * BS
+WIDE = 5 * BS
+N = MARGIN
+PLACED = 1
+VMEM_BYTES = 56 * 2**20
+
+
+def after(values, others):
+    return lax.optimization_barrier((tuple(values), tuple(others)))[0]
+
+
+def call(kernel, name, prefetch, grid, in_specs, out_specs, out_shape, scratch, args, flops, alias=None):
+    moved = sum(a.size * a.dtype.itemsize for a in args) // 2
+    return pl.pallas_call(
+        kernel,
+        grid_spec=pltpu.PrefetchScalarGridSpec(
+            num_scalar_prefetch=len(prefetch), grid=grid, in_specs=in_specs, out_specs=out_specs, scratch_shapes=scratch
+        ),
+        out_shape=out_shape,
+        input_output_aliases=alias or {},
+        compiler_params=pltpu.CompilerParams(vmem_limit_bytes=VMEM_BYTES),
+        cost_estimate=pl.CostEstimate(flops=flops, bytes_accessed=moved, transcendentals=0),
+        name=name,
+    )(*prefetch, *args)
+
+
+def split_into(high_ref, low_ref, rows, value):
+    high = value.astype(BF16)
+    high_ref[rows, :] = high
+    low_ref[rows, :] = (value - high.astype(F32)).astype(BF16)
+
+
+def dot3(a_high, a_low, b_high, b_low):
+    dot = functools.partial(jnp.dot, preferred_element_type=F32)
+    return dot(a_high, b_high) + (dot(a_high, b_low) + dot(a_low, b_high))
+
+
+def place_kernel(count, use, source, first, flags, *refs):
+    pieces, outs = refs[:count], refs[count:]
+    block = pl.program_id(0) * PLACED
+    slab = pieces[0].shape[3]
+
+    for i, piece in enumerate(pieces):
+
+        @pl.when(use[i] != 0)
+        def _(i=i, piece=piece):
+            for slot in range(2):
+                side = first[i] if slot == 0 else 1 - first[i]
+                rows = pl.ds(pl.multiple_of((source[i] * 2 + side) * slab, slab), slab)
+                for b, d in itertools.product(range(PLACED), range(5)):
+                    columns = pl.ds(d * BS, BS)
+                    live = piece[slot, b, d] * flags[(block + b) * 5 + d].astype(F32)
+                    high = live.astype(BF16)
+                    outs[0][b, rows, columns] = high
+                    outs[1][b, rows, columns] = (live - high.astype(F32)).astype(BF16)
+
+
+def place(candidates, flags):
+    pieces = [a for (a, _), _, _, _ in candidates]
+    table = [jnp.stack([jnp.asarray(c[k], jnp.int32) for c in candidates]) for k in (1, 2, 3)]
+    _, blocks, _, slab, _ = pieces[0].shape
+
+    def spec(i):
+        pair = candidates[i][0][1]
+        return pl.BlockSpec((2, PLACED, 5, slab, BS), lambda b, use, *_: (pair, b * use[i], 0, 0, 0))
+
+    out = pl.BlockSpec((PLACED, BS, WIDE), lambda b, *_: (b, 0, 0))
+    return call(
+        functools.partial(place_kernel, len(pieces)), "place_slabs", table + [flags], (blocks // PLACED,),
+        [spec(i) for i in range(len(pieces))], [out] * 2,
+        [jax.ShapeDtypeStruct((blocks, BS, WIDE), BF16)] * 2, [], pieces, 0,
+    )
+
+
+def inner_kernel(count, y, own, *refs):
+    nears, (high_a, low_a, high_b, low_b, out, head, tail, b_high, b_low) = refs[:count], refs[count:]
+    step = pl.program_id(0)
+    rows = own.shape[0]
+    split_into(b_high, b_low, pl.ds(pl.multiple_of(y[0] * MARGIN, MARGIN), rows), own[...])
+    at = pl.ds(pl.multiple_of((1 - y[0]) * rows, MARGIN), MARGIN)
+    for i, near in enumerate(nears):
+
+        @pl.when(step == i)
+        def _(near=near):
+            split_into(b_high, b_low, at, near[...])
+
+    for j in range(4):
+        high, low = (high_a, low_a) if j < 2 else (high_b, low_b)
+        window = pl.ds(j * BS, WIDE)
+        out[:, j * BS : (j + 1) * BS] = dot3(high[j % 2], low[j % 2], b_high[window, :], b_low[window, :]).T
+
+    @pl.when(step == 0)
+    def _():
+        head[...] = out[...]
+
+    @pl.when(step == count - 1)
+    def _():
+        tail[...] = out[...]
+
+
+def map_inner(y, covariance, nears, row_high, row_low):
+    rows, columns = covariance.shape
+    pair_a = pl.BlockSpec((2, BS, WIDE), lambda s, y: (1 - y[0], 0, 0))
+    pair_b = pl.BlockSpec((2, BS, WIDE), lambda s, y: (2 - y[0], 0, 0))
+    edge = pl.BlockSpec((N, 4 * BS), lambda s, y: (0, 0))
+    return call(
+        functools.partial(inner_kernel, len(nears)), "map_inner", [y], (columns // N,),
+        [pl.BlockSpec((rows, N), lambda s, y: (0, s))]
+        + [pl.BlockSpec((MARGIN, N), lambda s, y, at=at: (0, at)) for _, at in nears]
+        + [pair_a, pair_a, pair_b, pair_b],
+        [pl.BlockSpec((N, 4 * BS), lambda s, y: (s, 0)), edge, edge],
+        [jax.ShapeDtypeStruct((columns, 4 * BS), F32)] + [jax.ShapeDtypeStruct((N, 4 * BS), F32)] * 2,
+        [pltpu.VMEM((rows + MARGIN, N), BF16)] * 2,
+        [covariance, *[near for near, _ in nears], row_high, row_low, row_high, row_low], 6 * 4 * BS * WIDE * columns,
+    )
+
+
+def outer_kernel(count, y, chunks, own_a, own_b, *refs):
+    fars, (high, low), outs, (b_high, b_low) = refs[:count], refs[count : count + 2], refs[count + 2 : -2], refs[-2:]
+    at = lambda k: pl.ds(pl.multiple_of(k * MARGIN, MARGIN), MARGIN)
+    split_into(b_high, b_low, at(1 - y[0]), own_a[...])
+    split_into(b_high, b_low, at(2 - y[0]), own_b[...])
+    for i, far in enumerate(fars):
+
+        @pl.when(pl.program_id(0) == i)
+        def _(far=far):
+            split_into(b_high, b_low, at(2 * y[0]), far[...])
+
+    for j in range(2):
+        window = pl.ds(j * BS, WIDE)
+        mapped = dot3(high[j], low[j], b_high[window, :], b_low[window, :]).T
+        for i, out in enumerate(outs):
+
+            @pl.when(pl.program_id(0) == i)
+            def _(out=out):
+                out[:, j * BS : (j + 1) * BS] = mapped
+
+
+def map_outer(y, covariance, fars, row_high, row_low, chunks):
+    pair = pl.BlockSpec((2, BS, WIDE), lambda s, y, c: (2 * y[0], 0, 0))
+    return call(
+        functools.partial(outer_kernel, len(fars)), "map_outer", [y, jnp.array(chunks, jnp.int32)], (len(chunks),),
+        [
+            pl.BlockSpec((MARGIN, N), lambda s, y, c: (y[0], c[s])),
+            pl.BlockSpec((MARGIN, N), lambda s, y, c: (y[0] + 1, c[s])),
+        ]
+        + [pl.BlockSpec((MARGIN, N), lambda s, y, c, at=at: (0, at)) for _, at in fars]
+        + [pair, pair],
+        [pl.BlockSpec((N, 2 * BS), lambda s, y, c: (0, 0))] * len(chunks),
+        [jax.ShapeDtypeStruct((N, 2 * BS), F32)] * len(chunks),
+        [pltpu.VMEM((3 * MARGIN, N), BF16)] * 2,
+        [covariance, covariance, *[far for far, _ in fars], row_high, row_low], 6 * 2 * BS * WIDE * N * len(chunks),
+    )
+
+
+def split_next(count, at, parts, high_ref, low_ref):
+    rows = pl.ds(pl.multiple_of(pl.program_id(0) * BS, BS), BS)
+    for part, here in zip(parts, (at < 2, (at >= 2) & (at < count + 2), at >= count + 2)):
+
+        @pl.when(here)
+        def _(part=part):
+            split_into(high_ref, low_ref, rows, part[...])
+
+
+def streams(count, width):
+    def spec(first, blocks):
+        return pl.BlockSpec((BS, width), lambda s, t: (jnp.clip(t[0] + s - first, 0, blocks - 1), 0))
+
+    return [spec(0, 2), spec(2, count), spec(count + 2, 2)]
+
+
+def cast_inner_kernel(count, aliased, table, below, mid, above, high, low, noise, *rest):
+    out, b_high, b_low = rest[aliased:]
+    step = pl.program_id(0)
+    split_next(count, table[0] + step, (below, mid, above), b_high, b_low)
+
+    @pl.when(step >= 4)
+    def _():
+        window = pl.ds(pl.multiple_of((step - 4) * BS, BS), WIDE)
+        out[...] = noise[...] + dot3(high[0], low[0], b_high[window, :], b_low[window, :])
+
+
+def cast_inner(table, padded, high, low, noise, forecast):
+    blocks, (length, width) = high.shape[0], padded[1].shape
+    row = lambda s: jnp.maximum(s - 4, 0)
+    place = pl.BlockSpec(
+        (pl.Element(BS), pl.Element(width)), lambda s, t: (pl.multiple_of((t[0] + row(s)) * BS, BS), pl.multiple_of(t[1], N))
+    )
+    band = pl.BlockSpec((1, BS, WIDE), lambda s, t: (row(s), 0, 0))
+    aliased = forecast is not None
+    return call(
+        functools.partial(cast_inner_kernel, length // BS, int(aliased)), "cast_inner", [table], (blocks + 4,),
+        [*streams(length // BS, width), band, band, place]
+        + [pl.BlockSpec(memory_space=pl.ANY)] * aliased,
+        place, jax.ShapeDtypeStruct(noise.shape, F32), [pltpu.VMEM(((blocks + 4) * BS, width), BF16)] * 2,
+        [*padded, high, low, noise] + [forecast] * aliased, 6 * blocks * BS * WIDE * width,
+        {7: 0} if aliased else None,
+    )
+
+
+def cast_outer_kernel(count, held, table, *refs):
+    parts, (high, low, noise, _, out, b_high, b_low) = refs[:count], refs[count:]
+    step = pl.program_id(0)
+
+    @pl.when(step == 0)
+    def _():
+        for i, part in enumerate(parts):
+
+            @pl.when((i >= table[1]) & (i < table[1] + held))
+            def _(i=i, part=part):
+                split_into(b_high, b_low, pl.ds(pl.multiple_of((i - table[1]) * MARGIN, MARGIN), MARGIN), part[...])
+
+    window = pl.ds(pl.multiple_of(step * BS, BS), WIDE)
+    out[...] = noise[...] + dot3(high[0], low[0], b_high[window, :], b_low[window, :])
+
+
+def cast_outer(table, parts, high, low, noise, forecast):
+    blocks = high.shape[0]
+    held = blocks // 2 + 2
+    place = pl.BlockSpec((BS, N), lambda s, t: (t[0] + s, t[2]))
+    band = pl.BlockSpec((1, BS, WIDE), lambda s, t: (s, 0, 0))
+    return call(
+        functools.partial(cast_outer_kernel, len(parts), held), "cast_outer", [table], (blocks,),
+        [pl.BlockSpec((MARGIN, N), lambda s, t, at=at: (at, 0)) for _, at in parts]
+        + [band, band, place, pl.BlockSpec(memory_space=pl.ANY)],
+        place, jax.ShapeDtypeStruct(noise.shape, F32), [pltpu.VMEM((held * MARGIN, N), BF16)] * 2,
+        [*[part for part, _ in parts], high, low, noise, forecast], 6 * blocks * BS * WIDE * N, {len(parts) + 4: 0},
+    )
+
+
+def cast_rest_kernel(blocks, count, held, table, below, mid, above, *refs):
+    parts, (high, low, noise, _, out, in_high, in_low, out_high, out_low) = refs[:count], refs[count:]
+    step = pl.program_id(0)
+    split_next(blocks, table[0] + step, (below, mid, above), in_high, in_low)
+
+    @pl.when(step == 0)
+    def _():
+        for i, part in enumerate(parts):
+
+            @pl.when((i >= table[1]) & (i < table[1] + held))
+            def _(i=i, part=part):
+                split_into(out_high, out_low, pl.ds(pl.multiple_of((i - table[1]) * MARGIN, MARGIN), MARGIN), part[...])
+
+    @pl.when(step >= 4)
+    def _():
+        window = pl.ds(pl.multiple_of((step - 4) * BS, BS), WIDE)
+        inner = pl.ds(pl.multiple_of(table[2], N), mid.shape[1])
+        outer = pl.ds(pl.multiple_of(table[3], N), N)
+        out[:, inner] = noise[:, inner] + dot3(high[0], low[0], in_high[window, :], in_low[window, :])
+        out[:, outer] = noise[:, outer] + dot3(high[0], low[0], out_high[window, :], out_low[window, :])
+
+
+def cast_rest(table, padded, parts, high, low, noise, forecast):
+    blocks, (length, width) = high.shape[0], padded[1].shape
+    held = blocks // 2 + 2
+    row = lambda s: jnp.maximum(s - 4, 0)
+    place = pl.BlockSpec((BS, noise.shape[1]), lambda s, t: (t[0] + row(s), 0))
+    band = pl.BlockSpec((1, BS, WIDE), lambda s, t: (row(s), 0, 0))
+    rows = (blocks + 4) * BS
+    return call(
+        functools.partial(cast_rest_kernel, length // BS, len(parts), held), "cast_rest", [table], (blocks + 4,),
+        streams(length // BS, width)
+        + [pl.BlockSpec((MARGIN, N), lambda s, t, at=at: (at, 0)) for _, at in parts]
+        + [band, band, place, pl.BlockSpec(memory_space=pl.ANY)],
+        place, jax.ShapeDtypeStruct(noise.shape, F32),
+        [pltpu.VMEM((rows, width), BF16)] * 2 + [pltpu.VMEM((rows, N), BF16)] * 2,
+        [*padded, *[part for part, _ in parts], high, low, noise, forecast], 6 * blocks * BS * WIDE * noise.shape[1],
+        {len(parts) + 7: 0},
+    )
 
 
 def spread(array, axis, root):
@@ -50,7 +328,7 @@
     return band_apply(live_band, halo_fn(field))
 
 
-def body(covariance, blocks, present, model_noise):
+def plain_body(covariance, blocks, present, model_noise):
     row_index = lax.axis_index("row")
     col_index = lax.axis_index("col")
     ratio = lax.axis_size("row") // lax.axis_size("col")
@@ -77,7 +355,228 @@
     return second + model_noise
 
 
+def body(covariance, blocks, present, model_noise):
+    rows, cols = lax.axis_size("row"), lax.axis_size("col")
+    r, c = lax.axis_index("row"), lax.axis_index("col")
+    z, y = r // 2, r % 2
+    depth = rows // 2
+    col_blocks, _, slab, _ = blocks.shape
+    part_blocks = col_blocks // 2
+    swap = [(i, i ^ 1) for i in range(rows)]
+    permute = lax.ppermute
+    y_table = jnp.reshape(y, (1,)).astype(jnp.int32)
+
+    sliced = blocks.reshape(2, part_blocks, 5, slab, BS)
+    pick = lambda part: lax.dynamic_index_in_dim(sliced, part % 2, 0, False)
+
+    def along(k, long, ends=True):
+        hops = []
+        for i in range(k - 1, depth - 1):
+            hops.append((2 * i, 2 * i + 2) if long else (2 * i + 1, 2 * i + 3))
+        for i in range(0, depth - k):
+            hops.append((2 * i + 3, 2 * i + 1) if long else (2 * i + 2, 2 * i))
+        return [(a, b) for a, b in hops if ends or b not in (0, rows - 1)]
+
+    home = r // 2
+    bits = [1 << b for b in reversed(range(cols.bit_length() - 1))]
+
+    def senders(missing, bit, keep):
+        pairs_of = [(i, a) for i in range(rows) if keep(i) for a in range(cols) if ((a ^ (i // 2)) & missing) == 0]
+        return [(i * cols + a, i * cols + (a ^ bit)) for i, a in pairs_of]
+
+    def keeps(k, long):
+        def keep(i):
+            up = (i % 2 == 0) == long
+            return i // 2 >= k if up else i // 2 + k < depth
+
+        return keep
+
+    axes = ("row", "col")
+    at_home, at_mate = c == home, c == home ^ bits[0]
+
+    extra = covariance.shape[0] - MARGIN
+    count = covariance.shape[1] // N
+    chunks = sorted(range(count), key=lambda s: min(s, count - 1 - s))
+    hops = [(i, i + 1) for i in range(1, rows - 1, 2)] + [(i + 1, i) for i in range(1, rows - 1, 2)]
+    spans = [(0, 1), (1, 2), (3, 2), (5, 1)]
+    near_trips = [
+        (lax.dynamic_slice(covariance, (extra * (1 - y), at * N), (MARGIN, n * N)), "row", swap) for at, n in spans
+    ]
+    far_spans = [chunks[:1], chunks[1:3], chunks[3:5], chunks[5:]]
+    far_trips = []
+    for span in far_spans:
+        pieces = [lax.dynamic_slice(covariance, (extra * y, i * N), (MARGIN, N)) for i in span]
+        far_trips.append((jnp.concatenate(pieces, axis=1), "row", hops))
+
+    def send(jobs, *others):
+        values = after([job[0] for job in jobs], others)
+        return [permute(value, axis, perm) for value, (_, axis, perm) in zip(values, jobs)]
+
+    def pass_x(k, long):
+        return senders(cols - 1, bits[0], keeps(k, long))
+
+    def pass_core(k, long):
+        return senders(cols - 1 - bits[0], bits[1], keeps(k, long))
+
+    def join(*lists):
+        return [pair for pairs in lists for pair in pairs]
+
+    def whole(hops):
+        return [(i * cols + a, j * cols + a) for i, j in hops for a in range(cols)]
+
+    def among(hops):
+        return functools.reduce(jnp.logical_or, [r == i for i, _ in hops])
+
+    def core(value, passed, k, long):
+        return permute(jnp.where(at_mate, passed, value), axes, pass_core(k, long))
+
+    over = [(1, 0), (rows - 2, rows - 1)]
+    ends_hops, inside_hops = along(3, False), along(1, False, False)
+    trade0 = permute(pick(1 - y), "row", swap)
+    pair0 = jnp.stack([pick(y), trade0])
+    main = send(
+        [(pick(1 - y + 1), "row", swap), near_trips[0], (pair0, "row", along(1, True)), (pair0, "row", along(1, False))], trade0
+    )
+    trade1, near0, long01, short01 = main
+    (x0,) = send([(pair0, axes, pass_x(0, True))], trade1)
+    pair1 = jnp.stack([pick(y + 1), trade1])
+    stage = main + [x0] + [value for value, _, _ in near_trips[1:]]
+    main = send([near_trips[1], (long01, "row", along(2, True)), (short01, "row", along(2, False))], *stage)
+    near1, long02, short02 = main
+    x1a, core0 = send(
+        [(long01, axes, pass_x(1, True)), (jnp.where(at_mate, x0, pair0), axes, pass_core(0, True))], *stage, pair1
+    )
+    climbs = lambda k: jnp.where(y == 0, z >= k, z + k < depth)
+    stage = main + [x1a, core0] + [value for value, _, _ in far_trips]
+    last_hops = along(3, True) + along(3, False)
+    value2 = jnp.where(climbs(2), long02, short02)
+    near2, ends3, short11, x2, x1b = main = send(
+        [
+            near_trips[2], (value2, "row", last_hops), (pair1, "row", along(1, False, False)),
+            (value2, axes, senders(cols - 1, bits[0], lambda i: True)), (short01, axes, pass_x(1, False)),
+        ],
+        *stage,
+    )
+    (core1a,) = send([(jnp.where(at_mate, x1a, long01), axes, pass_core(1, True))], x2)
+    stage = main + [core1a]
+    inside2 = along(2, False, False)
+    x3_keep = lambda i: i // 2 in (0, depth - 1)
+    near3, far0, long11, mixed4, core12 = stage = send(
+        [
+            near_trips[3], far_trips[0], (pair1, "row", along(1, True)),
+            (jnp.where(among(inside2), short11, ends3), axes, whole(inside2) + senders(cols - 1, bits[0], x3_keep)),
+            (
+                jnp.concatenate([jnp.where(at_mate, x1b, short01), jnp.where(at_mate, x2, value2)]),
+                axes, senders(cols - 1 - bits[0], bits[1], lambda i: True),
+            ),
+        ],
+        *stage,
+    )
+
+    def climbed(k, up):
+        return jnp.where(up, z >= k, z + k < depth), jnp.where(up, z - k, z + k)
+
+    def entry(value, k, up, when, first=y):
+        held, source = climbed(k, up)
+        value = value if isinstance(value, tuple) else (value, 0)
+        return value, held & when, jnp.clip(source, 0, depth - 1), first
+
+    def either(value, k, when):
+        value, _, below, first = entry(value, k, False, when)
+        _, _, above, _ = entry(value, k, True, when)
+        held = ((z >= k) | (z + k < depth)) & when
+        return value, held, jnp.where(z >= k, above, below), first
+
+    end = ((y == 0) & (z == 0)) | ((y == 1) & (z == depth - 1))
+    always = z >= 0
+    row_flags = lax.dynamic_slice_in_dim(present, r * part_blocks, part_blocks, 0).reshape(-1)
+
+    def part_flags(phase):
+        base = c * col_blocks + (y + phase) % 2 * part_blocks
+        return lax.dynamic_slice_in_dim(present, base, part_blocks, 0).reshape(-1)
+
+    longs, shorts = y == 0, y == 1
+    at_other = ~(at_home | at_mate)
+    columns0 = [
+        entry(pair0, 0, True, always), entry(long01, 1, longs, always), entry(short01, 1, shorts, always),
+        either(value2, 2, always), either(ends3, 3, always),
+    ]
+    bands = [place(columns0, part_flags(0))]
+    stage = list(stage) + [bands[0][0]]
+
+    def inner_table(phase):
+        return jnp.stack([(y + phase) % 2 * part_blocks, (1 - y) * N]).astype(jnp.int32)
+
+    def outer_table(phase):
+        half = (y + phase) % 2
+        return jnp.stack([half * part_blocks, half * (part_blocks // 2), 2 * y]).astype(jnp.int32)
+
+    def outer(first, number):
+        picked = list(range(first, first + number))
+        outs = map_outer(y_table, covariance, [fars[i] for i in picked], row_high, row_low, [chunks[i] for i in picked])
+        mapped.update((chunks[i], (out, 0)) for i, out in zip(picked, outs))
+        return outs
+
+    up, down = [(i, i + 1) for i in range(cols - 1)], [(i + 1, i) for i in range(cols - 1)]
+    mapped, fars = {}, [(far0, 0)]
+    stage4 = stage
+    far12, long12, over1 = stage = send(
+        [far_trips[1], (long11, "row", along(2, True)), (long01, "row", over)], *stage
+    )
+    (core3,) = send(
+        [(jnp.where(at_mate, mixed4, ends3), axes, senders(cols - 1 - bits[0], bits[1], x3_keep))], *stage4
+    )
+    core1b, core2 = (core12, 0), (core12, 1)
+    row_table = [entry(pair0, 0, True, at_home), entry(x0, 0, True, at_mate), entry(core0, 0, True, at_other)]
+    for k, way, values in (
+        (1, longs, (long01, x1a, core1a)), (1, shorts, (short01, x1b, core1b)),
+    ):
+        row_table += [entry(value, k, way, when) for value, when in zip(values, (at_home, at_mate, at_other))]
+    for k, values in ((2, (value2, x2, core2)), (3, (ends3, mixed4, core3))):
+        row_table += [either(value, k, when) for value, when in zip(values, (at_home, at_mate, at_other))]
+    row_high, row_low = place(row_table, row_flags)
+    near_blocks = [(near, i) for near, (_, n) in zip((near0, near1, near2, near3), spans) for i in range(n)]
+    inner, inner_head, inner_tail = map_inner(y_table, covariance, near_blocks, row_high, row_low)
+    far34, long13, over2, below, above = stage = send(
+        [
+            far_trips[2], (long12, "row", along(3, True)), (long02, "row", over),
+            (inner_tail, "col", up), (inner_head, "col", down),
+        ],
+        *stage, inner,
+    )
+    fars += [(far12, 0), (far12, 1), (far34, 0), (far34, 1)]
+    first_mapped = outer(0, 3)
+    padded = (below, inner, above)
+    forecast = cast_inner(inner_table(0), padded, *bands[0], model_noise, None)
+    far5, last_over, outer_below, outer_above = send(
+        [far_trips[3], (ends3, "row", over), (mapped[count - 1][0], "col", up), (mapped[0][0], "col", down)],
+        *stage, *first_mapped, forecast,
+    )
+    fars.append((far5, 0))
+    mapped[-1], mapped[count] = (outer_below, 0), (outer_above, 0)
+    outer(3, 2)
+    outer(5, 1)
+    parts = [mapped[i] for i in range(-1, count + 1)]
+    forecast = cast_outer(outer_table(0), parts, *bands[0], model_noise, forecast)
+    columns1 = [
+        entry(pair1, 0, True, always), entry(long11, 1, longs, always), entry(short11, 1, shorts, ~end),
+        entry(long12, 2, longs, always), entry(mixed4, 2, shorts, ~end), entry(long13, 3, longs, always),
+        entry(over1, 1, shorts, end, 1 - y), entry(over2, 2, shorts, end, 1 - y), entry(last_over, 3, shorts, end, 1 - y),
+    ]
+    bands.append(place(columns1, part_flags(1)))
+    half = 1 - y
+    table = jnp.stack([half * part_blocks, half * (part_blocks // 2), (1 - y) * N, 2 * y * N]).astype(jnp.int32)
+    return cast_rest(table, padded, parts, *bands[1], model_noise, forecast)
+
+
 def solution(mesh):
+    rows, cols = mesh.shape["row"], mesh.shape["col"]
     in_specs = (P("row", "col"), P("col", None, "row", None), P(), P("col", "row"))
-    out_specs = P("col", "row")
-    return jax.shard_map(body, mesh=mesh, in_specs=in_specs, out_specs=out_specs, check_vma=False)
+
+    def step(covariance, blocks, present, model_noise):
+        fits = rows == 8 and cols == 4 and blocks.shape[0] == 12 * cols
+        chosen = body if fits and blocks.shape[3] == BS else plain_body
+        inner = jax.shard_map(chosen, mesh=mesh, in_specs=in_specs, out_specs=P("col", "row"), check_vma=False)
+        return inner(covariance, blocks, present, model_noise)
+
+    return step

time: 1060 us -> 480 us (0.45)
  waiting for transfers between devices: 468 us -> 153 us
  matrix products: 270 us -> 0 us
  local copies, waits for them, and re-layouts: 199 us -> 26.1 us
  Pallas kernels: 0 us -> 168 us
  starting transfers between devices: 9.68 us -> 103 us
  other arithmetic: 90.9 us -> 28 us
  between operations: 14.1 us -> 0.63 us
    dot_general x10 -> x0, matrix products: 270 us -> none  [band_apply(): jnp.einsum('bij,bjw->biw', live_band[:, diagonal], window, precision=lax....]
    ppermute x4 -> x35, waiting for transfers between devices: 345 us -> 153 us  [the longest x34 138 us: send(): permute(value, axis, perm)]
    pallas_call x0 -> x10, Pallas kernels: none -> 168 us  [call(): pl.pallas_call(kernel, grid_spec=pltpu.PrefetchScalarGridSpec(num_scalar_...]
    slice x8 -> x0, local copies, waits for them, and re-layouts: 146 us -> none  [the longest x6 128 us: band_apply(): padded[diagonal * block_size:(diagonal + blocks_here) * block_size]]
    ppermute x4 -> x35, starting transfers between devices: 9.64 us -> 103 us  [the longest x34 101 us: send(): permute(value, axis, perm)]
    psum x1 -> x0, waiting for transfers between devices: 92.8 us -> none  [spread(): return lax.psum(jnp.where(mine, array, jnp.zeros_like(array)), axis)]
    concatenate x1 -> x3, other arithmetic: 48.1 us -> 6.95 us  [the longest x2 4.72 us: body(): far_trips.append((jnp.concatenate(pieces, axis=1), 'row', hops))]
    all_gather x1 -> x0, waiting for transfers between devices: 30.5 us -> none  [body(): column_band = lax.all_gather(blocks, 'row', axis=2, tiled=True)]
  transfers between devices with their start and end apart: 6 -> 35, of which waited for: 4 -> 12; matrix products, arithmetic and copies ran while one was open for 14% -> 9% of each run, Pallas kernels for 0% -> 27%
where the time goes in v2:
time: 480 us; the launch traced here: 479 us
  Pallas kernels  168 us (35%)
  waiting for transfers between devices  153 us (32%)
  starting transfers between devices  103 us (21%)
  other arithmetic  28 us (6%)
  local copies, waits for them, and re-layouts  26.1 us (5%)
    pallas_call x10, Pallas kernels, call(): pl.pallas_call(kernel, grid_spec=pltpu.PrefetchScalarGridSpec(num_scalar_...  168 us
    ppermute x34, waiting for transfers between devices, send(): permute(value, axis, perm)  138 us
    ppermute x34, starting transfers between devices, send(): permute(value, axis, perm)  101 us
    ppermute x1, waiting for transfers between devices, body(): trade0 = permute(pick(1 - y), 'row', swap)  15 us
  transfers between devices with their start and end apart: 35, of which 12 were waited for; matrix products, arithmetic and copies ran while one was open for 9% of the time, Pallas kernels for 27%

profile of v2, /device:TPU:24, one launch (start us, length us, event | category | flops | bytes accessed | tf_op | source)
XLA Modules:
  0.0 478.7 jit_solution(12861678968286084896)
XLA Ops:
  0.0 3.9 constant_dynamic-slice_fusion.5
  5.5 6.9 %constant_dynamic-slice_fusion.10 = (f32[512,512]{1,0:T(8,128)}, f32[512,512]{1,0:T(8,128)}, f32[512,512]{1,0:T(8,128)}, f32[512,512]{1,0:T(8,128)}, f32[512,512...) fusion(f32[1536,3072]{1,0:T(8,128)} %own_b.5, s32[]{:T(128)S(6)} %select_n.207, ...), kind=kLoop, calls=%fused_computation.27 | loop fusion | bytes 16777224 | tf_op jit(solution)/shard_map/dynamic_slice | solution.py:408
  12.4 15.0 %collective-permute-done = f32[6,5,32,256]{3,2,1,0:T(8,128)S(1)} collective-permute-done((f32[6,5,32,256]{3,2,1,0:T(8,128)S(1)}, f32[6,5,32,256]{3,2,1,0:T(8,128)S(1)}, u32[]{:S(2)}, u32[]{:S(2)}) %collective-permute-start) | collective-permute-done | bytes 983072 | tf_op jit(solution)/shard_map/ppermute | solution.py:435
  31.9 5.8 %collective-permute-start.3 = (f32[2,6,5,32,256]{4,3,2,1,0:T(8,128)}, f32[2,6,5,32,256]{4,3,2,1,0:T(8,128)}, u32[]{:S(2)}, u32[]{:S(2)}) collective-permute-start(f32[2,6,5,32,256]{4,3,2,1,0:T(8,128)} %pad_maximum_fusion.3.refs_0_), channel_id=1, source_target_pairs={{4,12},{12,20},{20,28},{8,0},{16,8},{24,16},{5,13},{13,21},{21,29}... | collective-permute-start | bytes 5898248 | tf_op jit(solution)/shard_map/ppermute | solution.py:413
  37.7 14.3 %collective-permute-done.1 = f32[6,5,32,256]{3,2,1,0:T(8,128)} collective-permute-done((f32[6,5,32,256]{3,2,1,0:T(8,128)}, f32[6,5,32,256]{3,2,1,0:T(8,128)}, u32[]{:S(2)}, u32[]{:S(2)}) %collective-permute-start.1) | collective-permute-done | bytes 983072 | tf_op jit(solution)/shard_map/ppermute | solution.py:413
  52.0 1.9 collective-permute-start.5
  55.5 4.9 %constant_dynamic-slice_fusion.12 = (f32[512,1024]{1,0:T(8,128)}, f32[512,1024]{1,0:T(8,128)}) fusion(f32[1536,3072]{1,0:T(8,128)} %own_b.5, s32[]{:T(128)S(6)} %select_n.208), kind=kLoop, calls=%fused_computation.29 | loop fusion | bytes 8388612 | tf_op jit(solution)/shard_map/dynamic_slice | solution.py:403
  60.4 16.4 %collective-permute-done.4.refs_0_ = f32[512,512]{1,0:T(8,128)} collective-permute-done((f32[512,512]{1,0:T(8,128)}, f32[512,512]{1,0:T(8,128)}, u32[]{:S(2)}, u32[]{:S(2)}) %collective-permute-start.4) | collective-permute-done | bytes 1048608 | tf_op jit(solution)/shard_map/ppermute | solution.py:413
  78.7 2.0 collective-permute-start.7
  80.7 2.7 pad_maximum_fusion.4.refs_0_
  86.6 2.0 collective-permute-start.9
  89.9 3.3 pad_maximum_fusion.1
  94.6 28.1 %collective-permute-done.6 = f32[2,6,5,32,256]{4,3,2,1,0:T(8,128)} collective-permute-done((f32[2,6,5,32,256]{4,3,2,1,0:T(8,128)S(1)}, f32[2,6,5,32,256]{4,3,2,1,0:T(8,128)}, u32[]{:S(2)}, u32[]{:S(2)}) %collective-permute-start.6) | collective-permute-done | bytes 1966112 | tf_op jit(solution)/shard_map/ppermute | solution.py:413
  122.7 3.4 broadcast_select_fusion.5.refs_3_.refs_9_
  126.1 3.8 collective-permute-done.8.refs_1_.refs_2_
  129.8 1.9 collective-permute-start.14
  131.8 1.9 collective-permute-start.13
  133.7 8.6 %collective-permute-start.11 = (f32[2,6,5,32,256]{4,3,2,1,0:T(8,128)}, f32[2,6,5,32,256]{4,3,2,1,0:T(8,128)}, u32[]{:S(2)}, u32[]{:S(2)}) collective-permute-start(f32[2,6,5,32,256]{4,3,2,1,0:T(8,128)} %pad_maximum_fusion.4.refs_0_), channel_id=1, source_target_pairs={{4,12},{12,20},{16,8},{24,16},{5,13},{13,21},{17,9},{25,17},{6,14}... | collective-permute-start | bytes 5898248 | tf_op jit(solution)/shard_map/ppermute | solution.py:413
  146.7 1.9 broadcast_select_fusion.2
  148.6 1.9 broadcast_select_fusion.3
  150.6 2.2 pad_maximum_fusion
  152.8 28.7 %collective-permute-done.11.refs_2_ = f32[2,6,5,32,256]{4,3,2,1,0:T(8,128)} collective-permute-done((f32[2,6,5,32,256]{4,3,2,1,0:T(8,128)}, f32[2,6,5,32,256]{4,3,2,1,0:T(8,128)}, u32[]{:S(2)}, u32[]{:S(2)}) %collective-permute-start.11) | collective-permute-done | bytes 1966112 | tf_op jit(solution)/shard_map/ppermute | solution.py:413
  181.5 6.9 %collective-permute-done.12.refs_4_.refs_12_ = f32[2,6,5,32,256]{4,3,2,1,0:T(8,128)S(1)} collective-permute-done((f32[2,6,5,32,256]{4,3,2,1,0:T(8,128)}, f32[2,6,5,32,256]{4,3,2,1,0:T(8,128)S(1)}, u32[]{:S(2)}, u32[]{:S(2)}) %collective-permute-start.12) | collective-permute-done | bytes 1966112 | tf_op jit(solution)/shard_map/ppermute | solution.py:413
  188.5 1.9 broadcast_select_fusion.6
  191.7 1.9 collective-permute-start.20
  194.9 6.4 %collective-permute-start.18 = (f32[512,512]{1,0:T(8,128)}, f32[512,512]{1,0:T(8,128)}, u32[]{:S(2)}, u32[]{:S(2)}) collective-permute-start(f32[512,512]{1,0:T(8,128)} %get-tuple-element.70), channel_id=1, source_target_pairs={{0,4},{4,0},{8,12},{12,8},{16,20},{20,16},{24,28},{28,24},{1,5},{5... | collective-permute-start | bytes 3145736 | tf_op jit(solution)/shard_map/ppermute | solution.py:413
  201.3 5.2 %collective-permute-start.19 = (f32[512,512]{1,0:T(8,128)S(1)}, f32[512,512]{1,0:T(8,128)}, u32[]{:S(2)}, u32[]{:S(2)}) collective-permute-start(f32[512,512]{1,0:T(8,128)S(1)} %copy-done.15), channel_id=1, source_target_pairs={{4,8},{12,16},{20,24},{8,4},{16,12},{24,20},{5,9},{13,17},{21,25},... | collective-permute-start | bytes 3145736 | tf_op jit(solution)/shard_map/ppermute | solution.py:413
  209.3 9.1 %place_slabs.3 = (bf16[6,256,1280]{2,1,0:T(8,128)(2,1)}, bf16[6,256,1280]{2,1,0:T(8,128)(2,1)}) custom-call(s32[5]{0:T(128)} %stack.308.use, s32[5]{0:T(128)} %stack.314.source, s32[5]{0:T(128)} %stack.315.first, s32[30]{0:T(128)} %reshape.18.flags, f32[2,6,5,32,256]{4,3,2,1,0:T(8,128)} %pad_maximum_fusion.3.refs_0_, f32[2,6,5,32,256]{4,3,2,1,0:T(8,128)} %copy-done.3, ...), custom_call_target="tpu_custom_call" | custom-call | bytes 4915200 | tf_op jit(solution)/shard_map/place_slabs/pallas_call | solution.py:27
  218.4 1.8 broadcast_select_fusion
  220.3 24.9 %collective-permute-done.18.refs_5_ = f32[512,512]{1,0:T(8,128)} collective-permute-done((f32[512,512]{1,0:T(8,128)}, f32[512,512]{1,0:T(8,128)}, u32[]{:S(2)}, u32[]{:S(2)}) %collective-permute-start.18) | collective-permute-done | bytes 1048608 | tf_op jit(solution)/shard_map/ppermute | solution.py:413
  249.9 26.4 %collective-permute-start.24 = (f32[512,1024]{1,0:T(8,128)}, f32[512,1024]{1,0:T(8,128)S(1)}, u32[]{:S(2)}, u32[]{:S(2)}) collective-permute-start(f32[512,1024]{1,0:T(8,128)} %pad_maximum_fusion.2), channel_id=1, source_target_pairs={{4,8},{12,16},{20,24},{8,4},{16,12},{24,20},{5,9},{13,17},{21,25},... | collective-permute-start | bytes 6291464 | tf_op jit(solution)/shard_map/ppermute | solution.py:413
  278.4 10.1 %place_slabs.4 = (bf16[6,256,1280]{2,1,0:T(8,128)(2,1)}, bf16[6,256,1280]{2,1,0:T(8,128)(2,1)}) custom-call(s32[15]{0:T(128)} %stack.333.use, s32[15]{0:T(128)} %stack.334.source, s32[15]{0:T(128)} %stack.335.first, s32[30]{0:T(128)} %reshape.19.flags, f32[2,6,5,32,256]{4,3,2,1,0:T(8,128)} %pad_maximum_fusion.3.refs_0_, ...), custom_call_target="tpu_custom_call" | custom-call | bytes 16711680 | tf_op jit(solution)/shard_map/place_slabs/pallas_call | solution.py:27
  288.5 38.6 %map_inner.1 = (f32[3072,1024]{1,0:T(8,128)}, f32[512,1024]{1,0:T(8,128)}, f32[512,1024]{1,0:T(8,128)}) custom-call(s32[1]{0:T(128)} %bitcast.19.y, f32[1536,3072]{1,0:T(8,128)} %own_b.5, f32[512,512]{1,0:T(8,128)} %collective-permute-done.4.refs_0_, f32[512,1024]{1,0:T(8,128)} %collective-permute-done.8.refs_1_.refs_2_, ...), custom_call_target="tpu_custom_call" | custom-call | flops 24159191040 | bytes 22544384 | tf_op jit(solution)/shard_map/map_inner/pallas_call | solution.py:27
  329.0 3.4 collective-permute-start.26
  333.7 1.9 collective-permute-start.28
  337.0 2.6 collective-permute-start.30
  340.2 15.2 %map_outer.3 = (f32[512,512]{1,0:T(8,128)}, f32[512,512]{1,0:T(8,128)}, f32[512,512]{1,0:T(8,128)}) custom-call(s32[1]{0:T(128)} %bitcast.19.y, s32[3]{0:T(128)} %constant.106.clone.chunks, f32[1536,3072]{1,0:T(8,128)} %own_b.5, f32[1536,3072]{1,0:T(8,128)} %own_b.5, f32[512,512]{1,0:T(8,128)} %collective-permute-done.19.refs_0_, f32[512,1024]{1,0:T(8,128)} %copy-done.7, ...), custom_call_target="tpu_custom_call" | custom-call | flops 6039797760 | bytes 25427968 | tf_op jit(solution)/shard_map/map_outer/pallas_call | solution.py:27
  356.7 21.3 %cast_inner.1.refs_11_ = f32[3072,1536]{1,0:T(8,128)} custom-call(s32[2]{0:T(128)} %pad_add_fusion.1.table, f32[512,1024]{1,0:T(8,128)} %copy-done.6, f32[3072,1024]{1,0:T(8,128)} %get-tuple-element.83.mid, f32[512,1024]{1,0:T(8,128)} %collective-permute-done.27.above, bf16[6,256,1280]{2,1,0:T(8,128)(2,1)} %get-tuple-element.74.high.refs_8_, ...), custom_call_target="tpu_custom_call" | custom-call | flops 12079595520 | bytes 21757952 | tf_op jit(solution)/shard_map/cast_inner/pallas_call | solution.py:27
  378.0 5.5 %collective-permute-done.29.refs_5_ = f32[2,6,5,32,256]{4,3,2,1,0:T(8,128)} collective-permute-done((f32[2,6,5,32,256]{4,3,2,1,0:T(8,128)}, f32[2,6,5,32,256]{4,3,2,1,0:T(8,128)}, u32[]{:S(2)}, u32[]{:S(2)}) %collective-permute-start.29) | collective-permute-done | bytes 1966112 | tf_op jit(solution)/shard_map/ppermute | solution.py:413
  385.2 2.6 collective-permute-start.34
  387.8 1.9 collective-permute-start.32
  389.7 3.0 collective-permute-start.31
  398.1 11.3 %map_outer.4 = (f32[512,512]{1,0:T(8,128)}, f32[512,512]{1,0:T(8,128)}) custom-call(s32[1]{0:T(128)} %bitcast.19.y, s32[2]{0:T(128)} %constant.107.clone.chunks, f32[1536,3072]{1,0:T(8,128)} %own_b.5, f32[1536,3072]{1,0:T(8,128)} %own_b.5, f32[512,1024]{1,0:T(8,128)} %collective-permute-done.28.refs_0_.refs_1_, ...), custom_call_target="tpu_custom_call" | custom-call | flops 4026531840 | bytes 24903680 | tf_op jit(solution)/shard_map/map_outer/pallas_call | solution.py:27
  409.4 6.7 %collective-permute-done.32.refs_0_ = f32[512,512]{1,0:T(8,128)} collective-permute-done((f32[512,512]{1,0:T(8,128)}, f32[512,512]{1,0:T(8,128)}, u32[]{:S(2)}, u32[]{:S(2)}) %collective-permute-start.32) | collective-permute-done | bytes 1048608 | tf_op jit(solution)/shard_map/ppermute | solution.py:413
  416.1 6.7 %map_outer.5.refs_4_ = f32[512,512]{1,0:T(8,128)} custom-call(s32[1]{0:T(128)} %bitcast.19.y, s32[1]{0:T(128)} %constant.108.clone.chunks, f32[1536,3072]{1,0:T(8,128)} %own_b.5, f32[1536,3072]{1,0:T(8,128)} %own_b.5, f32[512,512]{1,0:T(8,128)} %collective-permute-done.32.refs_0_, ...), custom_call_target="tpu_custom_call" | custom-call | flops 2013265920 | bytes 23330816 | tf_op jit(solution)/shard_map/map_outer/pallas_call | solution.py:27
  422.8 14.6 %cast_outer.1.refs_11_ = f32[3072,1536]{1,0:T(8,128)} custom-call(s32[3]{0:T(128)} %pad_add_fusion.2.table, f32[512,512]{1,0:T(8,128)} %collective-permute-done.31.refs_0_, f32[512,512]{1,0:T(8,128)} %get-tuple-element.97.refs_1_, f32[512,512]{1,0:T(8,128)} %get-tuple-element.91.refs_2_, ...), custom_call_target="tpu_custom_call", output_to_operand_aliasing={{}: (12, {})} | custom-call | flops 6039797760 | bytes 27000832 | tf_op jit(solution)/shard_map/cast_outer/pallas_call | solution.py:27
  437.4 9.5 %place_slabs.5 = (bf16[6,256,1280]{2,1,0:T(8,128)(2,1)}, bf16[6,256,1280]{2,1,0:T(8,128)(2,1)}) custom-call(s32[9]{0:T(128)} %stack.352.use, s32[9]{0:T(128)} %stack.357.source, s32[9]{0:T(128)} %stack.359.first, s32[30]{0:T(128)} %reshape.20.flags, f32[2,6,5,32,256]{4,3,2,1,0:T(8,128)} %pad_maximum_fusion.4.refs_0_, ...), custom_call_target="tpu_custom_call" | custom-call | bytes 8847360 | tf_op jit(solution)/shard_map/place_slabs/pallas_call | solution.py:27
  447.0 31.7 %cast_rest.1 = f32[3072,1536]{1,0:T(8,128)} custom-call(s32[4]{0:T(128)} %pad_add_fusion.table, f32[512,1024]{1,0:T(8,128)} %copy-done.6, f32[3072,1024]{1,0:T(8,128)} %get-tuple-element.83.mid, f32[512,1024]{1,0:T(8,128)} %collective-permute-done.27.above, f32[512,512]{1,0:T(8,128)} %collective-permute-done.31.refs_0_, ...), custom_call_target="tpu_custom_call", output_to_operand_aliasing={{}: (15, {})} | custom-call | flops 18119393280 | bytes 35389440 | tf_op jit(solution)/shard_map/cast_rest/pallas_call | solution.py:27
  (101 shorter events, 45.2 us)
Async XLA Ops:
  3.9 23.5 %collective-permute-start = (f32[6,5,32,256]{3,2,1,0:T(8,128)S(1)}, f32[6,5,32,256]{3,2,1,0:T(8,128)S(1)}, u32[]{:S(2)}, u32[]{:S(2)}) collective-permute-start(f32[6,5,32,256]{3,2,1,0:T(8,128)S(1)} %get-tuple-element.112), channel_id=1, source_target_pairs={{0,4},{4,0},{8,12},{12,8},{16,20},{20,16},{24,28},{28,24},{1,5},{5... | collective-permute-start | bytes 2949128 | tf_op jit(solution)/shard_map/ppermute | solution.py:435
  29.0 22.9 %collective-permute-start.1 = (f32[6,5,32,256]{3,2,1,0:T(8,128)}, f32[6,5,32,256]{3,2,1,0:T(8,128)}, u32[]{:S(2)}, u32[]{:S(2)}) collective-permute-start(f32[6,5,32,256]{3,2,1,0:T(8,128)} %get-tuple-element.53), channel_id=1, source_target_pairs={{0,4},{4,0},{8,12},{12,8},{16,20},{20,16},{24,28},{28,24},{1,5},{5... | collective-permute-start | bytes 2949128 | tf_op jit(solution)/shard_map/ppermute | solution.py:413
  30.6 46.1 %collective-permute-start.2 = (f32[2,6,5,32,256]{4,3,2,1,0:T(8,128)}, f32[2,6,5,32,256]{4,3,2,1,0:T(8,128)S(1)}, u32[]{:S(2)}, u32[]{:S(2)}) collective-permute-start(f32[2,6,5,32,256]{4,3,2,1,0:T(8,128)} %pad_maximum_fusion.3.refs_0_), channel_id=1, source_target_pairs={{0,8},{8,16},{16,24},{12,4},{20,12},{28,20},{1,9},{9,17},{17,25},{... | collective-permute-start | bytes 5898248 | tf_op jit(solution)/shard_map/ppermute | solution.py:413
  31.9 45.5 %collective-permute-start.3 = (f32[2,6,5,32,256]{4,3,2,1,0:T(8,128)}, f32[2,6,5,32,256]{4,3,2,1,0:T(8,128)}, u32[]{:S(2)}, u32[]{:S(2)}) collective-permute-start(f32[2,6,5,32,256]{4,3,2,1,0:T(8,128)} %pad_maximum_fusion.3.refs_0_), channel_id=1, source_target_pairs={{4,12},{12,20},{20,28},{8,0},{16,8},{24,16},{5,13},{13,21},{21,29}... | collective-permute-start | bytes 5898248 | tf_op jit(solution)/shard_map/ppermute | solution.py:413
  52.0 25.4 %collective-permute-start.5 = (f32[2,6,5,32,256]{4,3,2,1,0:T(8,128)}, f32[2,6,5,32,256]{4,3,2,1,0:T(8,128)}, u32[]{:S(2)}, u32[]{:S(2)}) collective-permute-start(f32[2,6,5,32,256]{4,3,2,1,0:T(8,128)} %pad_maximum_fusion.3.refs_0_), channel_id=1, source_target_pairs={{0,2},{4,6},{9,11},{13,15},{18,16},{22,20},{27,25},{31,29}} | collective-permute-start | bytes 5898248 | tf_op jit(solution)/shard_map/ppermute | solution.py:413
  53.9 22.9 %collective-permute-start.4 = (f32[512,512]{1,0:T(8,128)}, f32[512,512]{1,0:T(8,128)}, u32[]{:S(2)}, u32[]{:S(2)}) collective-permute-start(f32[512,512]{1,0:T(8,128)} %get-tuple-element.56), channel_id=1, source_target_pairs={{0,4},{4,0},{8,12},{12,8},{16,20},{20,16},{24,28},{28,24},{1,5},{5... | collective-permute-start | bytes 3145736 | tf_op jit(solution)/shard_map/ppermute | solution.py:413
  55.5 25.2 %copy-start.11 = (f32[1,6,5,32,256]{4,3,2,1,0:T(8,128)S(1)}, f32[1,6,5,32,256]{4,3,2,1,0:T(8,128)}, u32[]{:S(2)}) copy-start(f32[1,6,5,32,256]{4,3,2,1,0:T(8,128)} %get-tuple-element.111) | copy-start | bytes 2949124
  76.7 9.9 %copy-start.3 = (f32[2,6,5,32,256]{4,3,2,1,0:T(8,128)}, f32[2,6,5,32,256]{4,3,2,1,0:T(8,128)S(1)}, u32[]{:S(2)}) copy-start(f32[2,6,5,32,256]{4,3,2,1,0:T(8,128)S(1)} %collective-permute-done.2.refs_1_.refs_3_) | copy-start | bytes 5898244
  77.4 45.3 %collective-permute-start.6 = (f32[2,6,5,32,256]{4,3,2,1,0:T(8,128)S(1)}, f32[2,6,5,32,256]{4,3,2,1,0:T(8,128)}, u32[]{:S(2)}, u32[]{:S(2)}) collective-permute-start(f32[2,6,5,32,256]{4,3,2,1,0:T(8,128)S(1)} %collective-permute-done.2.refs_1_.refs_3_), channel_id=1, source_target_pairs={{8,16},{16,24},{12,4},{20,12},{9,17},{17,25},{13,5},{21,13},{10,18... | collective-permute-start | bytes 5898248 | tf_op jit(solution)/shard_map/ppermute | solution.py:413
  78.7 44.0 %collective-permute-start.7 = (f32[2,6,5,32,256]{4,3,2,1,0:T(8,128)}, f32[2,6,5,32,256]{4,3,2,1,0:T(8,128)}, u32[]{:S(2)}, u32[]{:S(2)}) collective-permute-start(f32[2,6,5,32,256]{4,3,2,1,0:T(8,128)} %collective-permute-done.3.refs_2_.refs_6_), channel_id=1, source_target_pairs={{12,20},{20,28},{8,0},{16,8},{13,21},{21,29},{9,1},{17,9},{14,22},... | collective-permute-start | bytes 5898248 | tf_op jit(solution)/shard_map/ppermute | solution.py:413
  80.7 4.2 copy-start.13
  83.4 46.4 %collective-permute-start.8 = (f32[512,1024]{1,0:T(8,128)}, f32[512,1024]{1,0:T(8,128)}, u32[]{:S(2)}, u32[]{:S(2)}) collective-permute-start(f32[512,1024]{1,0:T(8,128)} %get-tuple-element.60), channel_id=1, source_target_pairs={{0,4},{4,0},{8,12},{12,8},{16,20},{20,16},{24,28},{28,24},{1,5},{5... | collective-permute-start | bytes 6291464 | tf_op jit(solution)/shard_map/ppermute | solution.py:413
  86.6 39.5 %collective-permute-start.9 = (f32[2,6,5,32,256]{4,3,2,1,0:T(8,128)S(1)}, f32[2,6,5,32,256]{4,3,2,1,0:T(8,128)}, u32[]{:S(2)}, u32[]{:S(2)}) collective-permute-start(f32[2,6,5,32,256]{4,3,2,1,0:T(8,128)S(1)} %collective-permute-done.2.refs_1_.refs_3_), channel_id=1, source_target_pairs={{4,6},{9,11},{13,15},{18,16},{22,20},{27,25}} | collective-permute-start | bytes 5898248 | tf_op jit(solution)/shard_map/ppermute | solution.py:413
  88.6 37.5 %collective-permute-start.10 = (f32[2,6,5,32,256]{4,3,2,1,0:T(8,128)}, f32[2,6,5,32,256]{4,3,2,1,0:T(8,128)}, u32[]{:S(2)}, u32[]{:S(2)}) collective-permute-start(f32[2,6,5,32,256]{4,3,2,1,0:T(8,128)} %broadcast_select_fusion.4), channel_id=1, source_target_pairs={{0,1},{2,3},{4,5},{6,7},{9,8},{11,10},{13,12},{15,14},{16,17},{18,... | collective-permute-start | bytes 5898248 | tf_op jit(solution)/shard_map/ppermute | solution.py:413
  89.9 3.3 copy-start.9
  89.9 3.3 copy-start.10
  94.6 49.1 %copy-start.4 = (f32[2,6,5,32,256]{4,3,2,1,0:T(8,128)S(1)}, f32[2,6,5,32,256]{4,3,2,1,0:T(8,128)}, u32[]{:S(2)}) copy-start(f32[2,6,5,32,256]{4,3,2,1,0:T(8,128)} %copy-done.3) | copy-start | bytes 5898244
  129.8 15.6 %collective-permute-start.14 = (f32[2,6,5,32,256]{4,3,2,1,0:T(8,128)}, f32[2,6,5,32,256]{4,3,2,1,0:T(8,128)}, u32[]{:S(2)}, u32[]{:S(2)}) collective-permute-start(f32[2,6,5,32,256]{4,3,2,1,0:T(8,128)} %broadcast_select_fusion.5.refs_3_.refs_9_), channel_id=1, source_target_pairs={{0,2},{4,6},{9,11},{13,15},{18,16},{22,20},{27,25},{31,29}} | collective-permute-start | bytes 5898248 | tf_op jit(solution)/shard_map/ppermute | solution.py:413
  131.8 16.8 %collective-permute-start.13 = (f32[2,6,5,32,256]{4,3,2,1,0:T(8,128)}, f32[2,6,5,32,256]{4,3,2,1,0:T(8,128)}, u32[]{:S(2)}, u32[]{:S(2)}) collective-permute-start(f32[2,6,5,32,256]{4,3,2,1,0:T(8,128)} %collective-permute-done.3.refs_2_.refs_6_), channel_id=1, source_target_pairs={{0,2},{9,11},{13,15},{18,16},{22,20},{31,29}} | collective-permute-start | bytes 5898248 | tf_op jit(solution)/shard_map/ppermute | solution.py:413
  133.7 47.8 %collective-permute-start.11 = (f32[2,6,5,32,256]{4,3,2,1,0:T(8,128)}, f32[2,6,5,32,256]{4,3,2,1,0:T(8,128)}, u32[]{:S(2)}, u32[]{:S(2)}) collective-permute-start(f32[2,6,5,32,256]{4,3,2,1,0:T(8,128)} %pad_maximum_fusion.4.refs_0_), channel_id=1, source_target_pairs={{4,12},{12,20},{16,8},{24,16},{5,13},{13,21},{17,9},{25,17},{6,14}... | collective-permute-start | bytes 5898248 | tf_op jit(solution)/shard_map/ppermute | solution.py:413
  142.3 46.1 %collective-permute-start.12 = (f32[2,6,5,32,256]{4,3,2,1,0:T(8,128)}, f32[2,6,5,32,256]{4,3,2,1,0:T(8,128)S(1)}, u32[]{:S(2)}, u32[]{:S(2)}) collective-permute-start(f32[2,6,5,32,256]{4,3,2,1,0:T(8,128)} %broadcast_select_fusion.5.refs_3_.refs_9_), channel_id=1, source_target_pairs={{16,24},{12,4},{20,28},{8,0},{17,25},{13,5},{21,29},{9,1},{18,26},... | collective-permute-start | bytes 5898248 | tf_op jit(solution)/shard_map/ppermute | solution.py:413
  143.6 46.8 %collective-permute-start.15 = (f32[512,1024]{1,0:T(8,128)}, f32[512,1024]{1,0:T(8,128)}, u32[]{:S(2)}, u32[]{:S(2)}) collective-permute-start(f32[512,1024]{1,0:T(8,128)} %get-tuple-element.67), channel_id=1, source_target_pairs={{0,4},{4,0},{8,12},{12,8},{16,20},{20,16},{24,28},{28,24},{1,5},{5... | collective-permute-start | bytes 6291464 | tf_op jit(solution)/shard_map/ppermute | solution.py:413
  145.4 45.0 %collective-permute-start.16 = (f32[2,6,5,32,256]{4,3,2,1,0:T(8,128)}, f32[2,6,5,32,256]{4,3,2,1,0:T(8,128)}, u32[]{:S(2)}, u32[]{:S(2)}) collective-permute-start(f32[2,6,5,32,256]{4,3,2,1,0:T(8,128)} %broadcast_select_fusion.1), channel_id=1, source_target_pairs={{4,5},{6,7},{9,8},{11,10},{13,12},{15,14},{16,17},{18,19},{20,21},... | collective-permute-start | bytes 5898248 | tf_op jit(solution)/shard_map/ppermute | solution.py:413
  152.8 48.5 %copy-start.15 = (f32[512,512]{1,0:T(8,128)S(1)}, f32[512,512]{1,0:T(8,128)}, u32[]{:S(2)}) copy-start(f32[512,512]{1,0:T(8,128)} %get-tuple-element.71) | copy-start | bytes 3145732
  152.8 53.9 %copy-start.16 = (s32[48,5]{0,1:T(8,128)S(1)}, s32[48,5]{0,1:T(8,128)}, u32[]{:S(2)}) copy-start(s32[48,5]{0,1:T(8,128)} %param.9) | copy-start | bytes 2884
  190.4 54.8 %collective-permute-start.21 = (f32[4,6,5,32,256]{4,3,2,1,0:T(8,128)}, f32[4,6,5,32,256]{4,3,2,1,0:T(8,128)}, u32[]{:S(2)}, u32[]{:S(2)}) collective-permute-start(f32[4,6,5,32,256]{4,3,2,1,0:T(8,128)} %pad_maximum_fusion), channel_id=1, source_target_pairs={{0,1},{2,3},{4,5},{6,7},{9,8},{11,10},{13,12},{15,14},{16,17},{18,... | collective-permute-start | bytes 11796488 | tf_op jit(solution)/shard_map/ppermute | solution.py:413
  191.7 26.7 %collective-permute-start.20 = (f32[2,6,5,32,256]{4,3,2,1,0:T(8,128)}, f32[2,6,5,32,256]{4,3,2,1,0:T(8,128)}, u32[]{:S(2)}, u32[]{:S(2)}) collective-permute-start(f32[2,6,5,32,256]{4,3,2,1,0:T(8,128)} %broadcast_select_fusion.6), channel_id=1, source_target_pairs={{12,20},{13,21},{14,22},{15,23},{16,8},{17,9},{18,10},{19,11},{0,2... | collective-permute-start | bytes 5898248 | tf_op jit(solution)/shard_map/ppermute | solution.py:413
  193.6 51.6 %collective-permute-start.17 = (f32[2,6,5,32,256]{4,3,2,1,0:T(8,128)}, f32[2,6,5,32,256]{4,3,2,1,0:T(8,128)}, u32[]{:S(2)}, u32[]{:S(2)}) collective-permute-start(f32[2,6,5,32,256]{4,3,2,1,0:T(8,128)} %pad_maximum_fusion.4.refs_0_), channel_id=1, source_target_pairs={{0,8},{8,16},{16,24},{12,4},{20,12},{28,20},{1,9},{9,17},{17,25},{... | collective-permute-start | bytes 5898248 | tf_op jit(solution)/shard_map/ppermute | solution.py:413
  194.9 50.3 %collective-permute-start.18 = (f32[512,512]{1,0:T(8,128)}, f32[512,512]{1,0:T(8,128)}, u32[]{:S(2)}, u32[]{:S(2)}) collective-permute-start(f32[512,512]{1,0:T(8,128)} %get-tuple-element.70), channel_id=1, source_target_pairs={{0,4},{4,0},{8,12},{12,8},{16,20},{20,16},{24,28},{28,24},{1,5},{5... | collective-permute-start | bytes 3145736 | tf_op jit(solution)/shard_map/ppermute | solution.py:413
  201.3 43.9 %collective-permute-start.19 = (f32[512,512]{1,0:T(8,128)S(1)}, f32[512,512]{1,0:T(8,128)}, u32[]{:S(2)}, u32[]{:S(2)}) collective-permute-start(f32[512,512]{1,0:T(8,128)S(1)} %copy-done.15), channel_id=1, source_target_pairs={{4,8},{12,16},{20,24},{8,4},{16,12},{24,20},{5,9},{13,17},{21,25},... | collective-permute-start | bytes 3145736 | tf_op jit(solution)/shard_map/ppermute | solution.py:413
  209.3 9.2 %copy-start.1 = (f32[2,6,5,32,256]{4,3,2,1,0:T(8,128)S(1)}, f32[2,6,5,32,256]{4,3,2,1,0:T(8,128)}, u32[]{:S(2)}) copy-start(f32[2,6,5,32,256]{4,3,2,1,0:T(8,128)} %copy-done) | copy-start | bytes 5898244
  218.4 57.8 %copy-start.5 = (f32[2,6,5,32,256]{4,3,2,1,0:T(8,128)S(1)}, f32[2,6,5,32,256]{4,3,2,1,0:T(8,128)}, u32[]{:S(2)}) copy-start(f32[2,6,5,32,256]{4,3,2,1,0:T(8,128)} %copy-done.3) | copy-start | bytes 5898244
  245.2 32.6 %collective-permute-start.23 = (f32[2,6,5,32,256]{4,3,2,1,0:T(8,128)}, f32[2,6,5,32,256]{4,3,2,1,0:T(8,128)}, u32[]{:S(2)}, u32[]{:S(2)}) collective-permute-start(f32[2,6,5,32,256]{4,3,2,1,0:T(8,128)} %broadcast_select_fusion), channel_id=1, source_target_pairs={{0,1},{2,3},{4,5},{6,7},{25,24},{27,26},{29,28},{31,30}} | collective-permute-start | bytes 5898248 | tf_op jit(solution)/shard_map/ppermute | solution.py:413
  248.6 78.5 %collective-permute-start.22 = (f32[2,6,5,32,256]{4,3,2,1,0:T(8,128)}, f32[2,6,5,32,256]{4,3,2,1,0:T(8,128)}, u32[]{:S(2)}, u32[]{:S(2)}) collective-permute-start(f32[2,6,5,32,256]{4,3,2,1,0:T(8,128)} %collective-permute-done.17.refs_1_), channel_id=1, source_target_pairs={{8,16},{16,24},{12,4},{20,12},{9,17},{17,25},{13,5},{21,13},{10,18... | collective-permute-start | bytes 5898248 | tf_op jit(solution)/shard_map/ppermute | solution.py:413
  249.9 77.3 %collective-permute-start.24 = (f32[512,1024]{1,0:T(8,128)}, f32[512,1024]{1,0:T(8,128)S(1)}, u32[]{:S(2)}, u32[]{:S(2)}) collective-permute-start(f32[512,1024]{1,0:T(8,128)} %pad_maximum_fusion.2), channel_id=1, source_target_pairs={{4,8},{12,16},{20,24},{8,4},{16,12},{24,20},{5,9},{13,17},{21,25},... | collective-permute-start | bytes 6291464 | tf_op jit(solution)/shard_map/ppermute | solution.py:413
  276.2 50.9 %collective-permute-start.25 = (f32[2,6,5,32,256]{4,3,2,1,0:T(8,128)S(1)}, f32[2,6,5,32,256]{4,3,2,1,0:T(8,128)S(1)}, u32[]{:S(2)}, u32[]{:S(2)}) collective-permute-start(f32[2,6,5,32,256]{4,3,2,1,0:T(8,128)S(1)} %copy-done.5), channel_id=1, source_target_pairs={{4,0},{24,28},{5,1},{25,29},{6,2},{26,30},{7,3},{27,31}} | collective-permute-start | bytes 5898248 | tf_op jit(solution)/shard_map/ppermute | solution.py:413
  327.1 1.9 copy-start.14
  329.0 26.3 %collective-permute-start.26 = (f32[512,1024]{1,0:T(8,128)}, f32[512,1024]{1,0:T(8,128)S(1)}, u32[]{:S(2)}, u32[]{:S(2)}) collective-permute-start(f32[512,1024]{1,0:T(8,128)} %get-tuple-element.84), channel_id=1, source_target_pairs={{0,1},{1,2},{2,3},{4,5},{5,6},{6,7},{8,9},{9,10},{10,11},{12,13},{... | collective-permute-start | bytes 6291464 | tf_op jit(solution)/shard_map/ppermute | solution.py:413
  332.4 22.9 %collective-permute-start.27 = (f32[512,1024]{1,0:T(8,128)}, f32[512,1024]{1,0:T(8,128)}, u32[]{:S(2)}, u32[]{:S(2)}) collective-permute-start(f32[512,1024]{1,0:T(8,128)} %get-tuple-element.85), channel_id=1, source_target_pairs={{1,0},{2,1},{3,2},{5,4},{6,5},{7,6},{9,8},{10,9},{11,10},{13,12},{... | collective-permute-start | bytes 6291464 | tf_op jit(solution)/shard_map/ppermute | solution.py:413
  333.7 51.5 %collective-permute-start.28 = (f32[512,1024]{1,0:T(8,128)}, f32[512,1024]{1,0:T(8,128)}, u32[]{:S(2)}, u32[]{:S(2)}) collective-permute-start(f32[512,1024]{1,0:T(8,128)} %pad_maximum_fusion.1), channel_id=1, source_target_pairs={{4,8},{12,16},{20,24},{8,4},{16,12},{24,20},{5,9},{13,17},{21,25},... | collective-permute-start | bytes 6291464 | tf_op jit(solution)/shard_map/ppermute | solution.py:413
  335.7 47.7 %collective-permute-start.29 = (f32[2,6,5,32,256]{4,3,2,1,0:T(8,128)}, f32[2,6,5,32,256]{4,3,2,1,0:T(8,128)}, u32[]{:S(2)}, u32[]{:S(2)}) collective-permute-start(f32[2,6,5,32,256]{4,3,2,1,0:T(8,128)} %collective-permute-done.22.refs_3_), channel_id=1, source_target_pairs={{16,24},{12,4},{17,25},{13,5},{18,26},{14,6},{19,27},{15,7}} | collective-permute-start | bytes 5898248 | tf_op jit(solution)/shard_map/ppermute | solution.py:413
  337.0 46.5 %collective-permute-start.30 = (f32[2,6,5,32,256]{4,3,2,1,0:T(8,128)}, f32[2,6,5,32,256]{4,3,2,1,0:T(8,128)}, u32[]{:S(2)}, u32[]{:S(2)}) collective-permute-start(f32[2,6,5,32,256]{4,3,2,1,0:T(8,128)} %collective-permute-done.6), channel_id=1, source_target_pairs={{4,0},{24,28},{5,1},{25,29},{6,2},{26,30},{7,3},{27,31}} | collective-permute-start | bytes 5898248 | tf_op jit(solution)/shard_map/ppermute | solution.py:413
  356.7 28.5 %copy-start.2 = (f32[2,6,5,32,256]{4,3,2,1,0:T(8,128)S(1)}, f32[2,6,5,32,256]{4,3,2,1,0:T(8,128)}, u32[]{:S(2)}) copy-start(f32[2,6,5,32,256]{4,3,2,1,0:T(8,128)} %copy-done) | copy-start | bytes 5898244
  356.7 36.0 %copy-start.8 = (f32[512,512]{1,0:T(8,128)S(1)}, f32[512,512]{1,0:T(8,128)}, u32[]{:S(2)}) copy-start(f32[512,512]{1,0:T(8,128)} %get-tuple-element.97.refs_1_) | copy-start | bytes 3145732
  385.2 52.2 %collective-permute-start.34 = (f32[2,6,5,32,256]{4,3,2,1,0:T(8,128)S(1)}, f32[2,6,5,32,256]{4,3,2,1,0:T(8,128)}, u32[]{:S(2)}, u32[]{:S(2)}) collective-permute-start(f32[2,6,5,32,256]{4,3,2,1,0:T(8,128)S(1)} %copy-done.2), channel_id=1, source_target_pairs={{4,0},{24,28},{5,1},{25,29},{6,2},{26,30},{7,3},{27,31}} | collective-permute-start | bytes 5898248 | tf_op jit(solution)/shard_map/ppermute | solution.py:413
  387.8 28.3 %collective-permute-start.32 = (f32[512,512]{1,0:T(8,128)}, f32[512,512]{1,0:T(8,128)}, u32[]{:S(2)}, u32[]{:S(2)}) collective-permute-start(f32[512,512]{1,0:T(8,128)} %get-tuple-element.95), channel_id=1, source_target_pairs={{4,8},{12,16},{20,24},{8,4},{16,12},{24,20},{5,9},{13,17},{21,25},... | collective-permute-start | bytes 3145736 | tf_op jit(solution)/shard_map/ppermute | solution.py:413
  389.7 33.1 %collective-permute-start.31 = (f32[512,512]{1,0:T(8,128)}, f32[512,512]{1,0:T(8,128)}, u32[]{:S(2)}, u32[]{:S(2)}) collective-permute-start(f32[512,512]{1,0:T(8,128)} %get-tuple-element.93.refs_6_), channel_id=1, source_target_pairs={{0,1},{1,2},{2,3},{4,5},{5,6},{6,7},{8,9},{9,10},{10,11},{12,13},{... | collective-permute-start | bytes 3145736 | tf_op jit(solution)/shard_map/ppermute | solution.py:413
  392.7 30.1 %collective-permute-start.33 = (f32[512,512]{1,0:T(8,128)S(1)}, f32[512,512]{1,0:T(8,128)}, u32[]{:S(2)}, u32[]{:S(2)}) collective-permute-start(f32[512,512]{1,0:T(8,128)S(1)} %copy-done.8), channel_id=1, source_target_pairs={{1,0},{2,1},{3,2},{5,4},{6,5},{7,6},{9,8},{10,9},{11,10},{13,12},{... | collective-permute-start | bytes 3145736 | tf_op jit(solution)/shard_map/ppermute | solution.py:413
  (4 other events, 6.2 us)

commit v3 on v2

--- a/solution.py
+++ b/solution.py
@@ -48,11 +48,8 @@
     return dot(a_high, b_high) + (dot(a_high, b_low) + dot(a_low, b_high))
 
 
-def place_kernel(count, use, source, first, flags, *refs):
-    pieces, outs = refs[:count], refs[count:]
-    block = pl.program_id(0) * PLACED
+def write_slabs(pieces, use, source, first, flags, block, high_ref, low_ref):
     slab = pieces[0].shape[3]
-
     for i, piece in enumerate(pieces):
 
         @pl.when(use[i] != 0)
@@ -60,28 +57,51 @@
             for slot in range(2):
                 side = first[i] if slot == 0 else 1 - first[i]
                 rows = pl.ds(pl.multiple_of((source[i] * 2 + side) * slab, slab), slab)
-                for b, d in itertools.product(range(PLACED), range(5)):
+                for d in range(5):
                     columns = pl.ds(d * BS, BS)
-                    live = piece[slot, b, d] * flags[(block + b) * 5 + d].astype(F32)
+                    live = piece[slot, 0, d] * flags[block * 5 + d].astype(F32)
                     high = live.astype(BF16)
-                    outs[0][b, rows, columns] = high
-                    outs[1][b, rows, columns] = (live - high.astype(F32)).astype(BF16)
-
-
-def place(candidates, flags):
-    pieces = [a for (a, _), _, _, _ in candidates]
-    table = [jnp.stack([jnp.asarray(c[k], jnp.int32) for c in candidates]) for k in (1, 2, 3)]
-    _, blocks, _, slab, _ = pieces[0].shape
-
-    def spec(i):
-        pair = candidates[i][0][1]
-        return pl.BlockSpec((2, PLACED, 5, slab, BS), lambda b, use, *_: (pair, b * use[i], 0, 0, 0))
-
-    out = pl.BlockSpec((PLACED, BS, WIDE), lambda b, *_: (b, 0, 0))
+                    high_ref[rows, columns] = high
+                    low_ref[rows, columns] = (live - high.astype(F32)).astype(BF16)
+
+
+def slab_specs(pieces, row, at):
+    def spec(i, piece, pair):
+        return pl.BlockSpec((2, 1, 5, piece.shape[3], BS), lambda s, *tables: (pair, row(s) * tables[at][i], 0, 0, 0))
+
+    return [spec(i, piece, pair) for i, (piece, pair) in enumerate(pieces)]
+
+
+def place_kernel(count, use, source, first, flags, *refs):
+    pieces, (high, low) = refs[:count], refs[count:]
+    write_slabs(pieces, use, source, first, flags, pl.program_id(0), high.at[0], low.at[0])
+
+
+def place(pieces, tables):
+    blocks = pieces[0][0].shape[1]
+    out = pl.BlockSpec((1, BS, WIDE), lambda b, *_: (b, 0, 0))
     return call(
-        functools.partial(place_kernel, len(pieces)), "place_slabs", table + [flags], (blocks // PLACED,),
-        [spec(i) for i in range(len(pieces))], [out] * 2,
-        [jax.ShapeDtypeStruct((blocks, BS, WIDE), BF16)] * 2, [], pieces, 0,
+        functools.partial(place_kernel, len(pieces)), "place_slabs", tables, (blocks,),
+        slab_specs(pieces, lambda b: b, 0), [out] * 2,
+        [jax.ShapeDtypeStruct((blocks, BS, WIDE), BF16)] * 2, [], [piece for piece, _ in pieces], 0,
+    )
+
+
+def place_last_kernel(count, use, source, first, flags, group, *refs):
+    pieces, (high_before, low_before, high, low) = refs[:count], refs[count:]
+    high[...] = high_before[...]
+    low[...] = low_before[...]
+    write_slabs(pieces, use, [0] * count, first, flags, pl.program_id(0), high.at[0], low.at[0])
+
+
+def place_last(pieces, tables, high, low):
+    blocks, _, slab = pieces[0][0].shape[1:4]
+    group = pl.BlockSpec((1, 2 * slab, WIDE), lambda b, *t: (b, t[4][0], 0))
+    return call(
+        functools.partial(place_last_kernel, len(pieces)), "place_last", tables, (blocks,),
+        slab_specs(pieces, lambda b: b, 0) + [group] * 2, [group] * 2,
+        [jax.ShapeDtypeStruct(high.shape, BF16)] * 2, [], [piece for piece, _ in pieces] + [high, low], 0,
+        {5 + len(pieces): 0, 6 + len(pieces): 1},
     )
 
 
@@ -177,7 +197,7 @@
 
 def streams(count, width):
     def spec(first, blocks):
-        return pl.BlockSpec((BS, width), lambda s, t: (jnp.clip(t[0] + s - first, 0, blocks - 1), 0))
+        return pl.BlockSpec((BS, width), lambda s, t, *_: (jnp.clip(t[0] + s - first, 0, blocks - 1), 0))
 
     return [spec(0, 2), spec(2, count), spec(count + 2, 2)]
 
@@ -241,10 +261,11 @@
     )
 
 
-def cast_rest_kernel(blocks, count, held, table, below, mid, above, *refs):
-    parts, (high, low, noise, _, out, in_high, in_low, out_high, out_low) = refs[:count], refs[count:]
+def cast_rest_kernel(length, count, held, slabs, table, use, source, first, flags, below, mid, above, *refs):
+    parts, pieces, rest = refs[:count], refs[count : count + slabs], refs[count + slabs :]
+    noise, _, out, in_high, in_low, out_high, out_low, high, low = rest
     step = pl.program_id(0)
-    split_next(blocks, table[0] + step, (below, mid, above), in_high, in_low)
+    split_next(length, table[0] + step, (below, mid, above), in_high, in_low)
 
     @pl.when(step == 0)
     def _():
@@ -256,29 +277,31 @@
 
     @pl.when(step >= 4)
     def _():
+        write_slabs(pieces, use, source, first, flags, step - 4, high, low)
         window = pl.ds(pl.multiple_of((step - 4) * BS, BS), WIDE)
         inner = pl.ds(pl.multiple_of(table[2], N), mid.shape[1])
         outer = pl.ds(pl.multiple_of(table[3], N), N)
-        out[:, inner] = noise[:, inner] + dot3(high[0], low[0], in_high[window, :], in_low[window, :])
-        out[:, outer] = noise[:, outer] + dot3(high[0], low[0], out_high[window, :], out_low[window, :])
-
-
-def cast_rest(table, padded, parts, high, low, noise, forecast):
-    blocks, (length, width) = high.shape[0], padded[1].shape
+        out[:, inner] = noise[:, inner] + dot3(high[...], low[...], in_high[window, :], in_low[window, :])
+        out[:, outer] = noise[:, outer] + dot3(high[...], low[...], out_high[window, :], out_low[window, :])
+
+
+def cast_rest(table, padded, parts, pieces, tables, noise, forecast):
+    blocks, (length, width) = pieces[0][0].shape[1], padded[1].shape
     held = blocks // 2 + 2
     row = lambda s: jnp.maximum(s - 4, 0)
-    place = pl.BlockSpec((BS, noise.shape[1]), lambda s, t: (t[0] + row(s), 0))
-    band = pl.BlockSpec((1, BS, WIDE), lambda s, t: (row(s), 0, 0))
+    place = pl.BlockSpec((BS, noise.shape[1]), lambda s, t, *_: (t[0] + row(s), 0))
     rows = (blocks + 4) * BS
+    operands = [*padded, *[part for part, _ in parts], *[piece for piece, _ in pieces], noise, forecast]
     return call(
-        functools.partial(cast_rest_kernel, length // BS, len(parts), held), "cast_rest", [table], (blocks + 4,),
+        functools.partial(cast_rest_kernel, length // BS, len(parts), held, len(pieces)), "cast_rest", [table, *tables],
+        (blocks + 4,),
         streams(length // BS, width)
-        + [pl.BlockSpec((MARGIN, N), lambda s, t, at=at: (at, 0)) for _, at in parts]
-        + [band, band, place, pl.BlockSpec(memory_space=pl.ANY)],
+        + [pl.BlockSpec((MARGIN, N), lambda s, *_, at=at: (at, 0)) for _, at in parts]
+        + slab_specs(pieces, row, 1)
+        + [place, pl.BlockSpec(memory_space=pl.ANY)],
         place, jax.ShapeDtypeStruct(noise.shape, F32),
-        [pltpu.VMEM((rows, width), BF16)] * 2 + [pltpu.VMEM((rows, N), BF16)] * 2,
-        [*padded, *[part for part, _ in parts], high, low, noise, forecast], 6 * blocks * BS * WIDE * noise.shape[1],
-        {len(parts) + 7: 0},
+        [pltpu.VMEM((rows, width), BF16)] * 2 + [pltpu.VMEM((rows, N), BF16)] * 2 + [pltpu.VMEM((BS, WIDE), BF16)] * 2,
+        operands, 6 * blocks * BS * WIDE * noise.shape[1], {5 + len(operands) - 1: 0},
     )
 
 
@@ -430,6 +453,54 @@
     def core(value, passed, k, long):
         return permute(jnp.where(at_mate, passed, value), axes, pass_core(k, long))
 
+    def climbed(k, up):
+        return jnp.where(up, z >= k, z + k < depth), jnp.where(up, z - k, z + k)
+
+    def entry(k, up, when, first=y):
+        held, source = climbed(k, up)
+        return held & when, jnp.clip(source, 0, depth - 1), first
+
+    def either(k, when):
+        above, below = entry(k, True, when), entry(k, False, when)
+        return above[0] | below[0], jnp.where(z >= k, above[1], below[1]), y
+
+    end = ((y == 0) & (z == 0)) | ((y == 1) & (z == depth - 1))
+    always = z >= 0
+    longs, shorts = y == 0, y == 1
+    spots = (at_home, at_mate, ~(at_home | at_mate))
+
+    def tables_of(entries, flags):
+        return [jnp.stack([jnp.asarray(e[k], jnp.int32) for e in entries]) for k in range(3)] + [flags.reshape(-1)]
+
+    def part_flags(phase):
+        base = c * col_blocks + (y + phase) % 2 * part_blocks
+        return lax.dynamic_slice_in_dim(present, base, part_blocks, 0)
+
+    tables0 = tables_of(
+        [entry(0, True, always), entry(1, longs, always), entry(1, shorts, always), either(2, always), either(3, always)],
+        part_flags(0),
+    )
+    tables1 = tables_of(
+        [
+            entry(0, True, always), entry(1, longs, always), entry(1, shorts, ~end), entry(2, longs, always),
+            entry(2, shorts, ~end), entry(3, longs, always), entry(1, shorts, end, 1 - y), entry(2, shorts, end, 1 - y),
+            entry(3, shorts, end, 1 - y),
+        ],
+        part_flags(1),
+    )
+    row_flags = lax.dynamic_slice_in_dim(present, r * part_blocks, part_blocks, 0)
+    row_tables = tables_of(
+        [entry(0, True, spot) for spot in spots] + [entry(1, longs, spot) for spot in spots]
+        + [entry(1, shorts, spot) for spot in spots] + [either(2, spot) for spot in spots], row_flags
+    )
+    last_tables = tables_of([either(3, spot) for spot in spots], row_flags)
+    last_tables.append(jnp.reshape(either(3, always)[1], (1,)).astype(jnp.int32))
+    half = 1 - y
+    inner_table = jnp.stack([y * part_blocks, half * N]).astype(jnp.int32)
+    outer_table = jnp.stack([y * part_blocks, y * (part_blocks // 2), 2 * y]).astype(jnp.int32)
+    rest_table = jnp.stack([half * part_blocks, half * (part_blocks // 2), half * N, 2 * y * N]).astype(jnp.int32)
+    all_tables = [*tables0, *tables1, *row_tables, *last_tables, inner_table, outer_table, rest_table, y_table]
+
     over = [(1, 0), (rows - 2, rows - 1)]
     ends_hops, inside_hops = along(3, False), along(1, False, False)
     trade0 = permute(pick(1 - y), "row", swap)
@@ -440,7 +511,7 @@
     trade1, near0, long01, short01 = main
     (x0,) = send([(pair0, axes, pass_x(0, True))], trade1)
     pair1 = jnp.stack([pick(y + 1), trade1])
-    stage = main + [x0] + [value for value, _, _ in near_trips[1:]]
+    stage = main + [x0] + [value for value, _, _ in near_trips[1:]] + all_tables
     main = send([near_trips[1], (long01, "row", along(2, True)), (short01, "row", along(2, False))], *stage)
     near1, long02, short02 = main
     x1a, core0 = send(
@@ -473,43 +544,13 @@
         *stage,
     )
 
-    def climbed(k, up):
-        return jnp.where(up, z >= k, z + k < depth), jnp.where(up, z - k, z + k)
-
-    def entry(value, k, up, when, first=y):
-        held, source = climbed(k, up)
-        value = value if isinstance(value, tuple) else (value, 0)
-        return value, held & when, jnp.clip(source, 0, depth - 1), first
-
-    def either(value, k, when):
-        value, _, below, first = entry(value, k, False, when)
-        _, _, above, _ = entry(value, k, True, when)
-        held = ((z >= k) | (z + k < depth)) & when
-        return value, held, jnp.where(z >= k, above, below), first
-
-    end = ((y == 0) & (z == 0)) | ((y == 1) & (z == depth - 1))
-    always = z >= 0
-    row_flags = lax.dynamic_slice_in_dim(present, r * part_blocks, part_blocks, 0).reshape(-1)
-
-    def part_flags(phase):
-        base = c * col_blocks + (y + phase) % 2 * part_blocks
-        return lax.dynamic_slice_in_dim(present, base, part_blocks, 0).reshape(-1)
-
-    longs, shorts = y == 0, y == 1
-    at_other = ~(at_home | at_mate)
-    columns0 = [
-        entry(pair0, 0, True, always), entry(long01, 1, longs, always), entry(short01, 1, shorts, always),
-        either(value2, 2, always), either(ends3, 3, always),
-    ]
-    bands = [place(columns0, part_flags(0))]
-    stage = list(stage) + [bands[0][0]]
-
-    def inner_table(phase):
-        return jnp.stack([(y + phase) % 2 * part_blocks, (1 - y) * N]).astype(jnp.int32)
-
-    def outer_table(phase):
-        half = (y + phase) % 2
-        return jnp.stack([half * part_blocks, half * (part_blocks // 2), 2 * y]).astype(jnp.int32)
+    plain = lambda *values: [value if isinstance(value, tuple) else (value, 0) for value in values]
+    bands = [place(plain(pair0, long01, short01, value2, ends3), tables0)]
+    core1b, core2 = (core12, 0), (core12, 1)
+    row_parts = place(
+        plain(pair0, x0, core0, long01, x1a, core1a, short01, x1b, core1b, value2, x2, core2), row_tables
+    )
+    stage = list(stage) + [bands[0][0], row_parts[0]]
 
     def outer(first, number):
         picked = list(range(first, first + number))
@@ -526,15 +567,7 @@
     (core3,) = send(
         [(jnp.where(at_mate, mixed4, ends3), axes, senders(cols - 1 - bits[0], bits[1], x3_keep))], *stage4
     )
-    core1b, core2 = (core12, 0), (core12, 1)
-    row_table = [entry(pair0, 0, True, at_home), entry(x0, 0, True, at_mate), entry(core0, 0, True, at_other)]
-    for k, way, values in (
-        (1, longs, (long01, x1a, core1a)), (1, shorts, (short01, x1b, core1b)),
-    ):
-        row_table += [entry(value, k, way, when) for value, when in zip(values, (at_home, at_mate, at_other))]
-    for k, values in ((2, (value2, x2, core2)), (3, (ends3, mixed4, core3))):
-        row_table += [either(value, k, when) for value, when in zip(values, (at_home, at_mate, at_other))]
-    row_high, row_low = place(row_table, row_flags)
+    row_high, row_low = place_last(plain(ends3, mixed4, core3), last_tables, *row_parts)
     near_blocks = [(near, i) for near, (_, n) in zip((near0, near1, near2, near3), spans) for i in range(n)]
     inner, inner_head, inner_tail = map_inner(y_table, covariance, near_blocks, row_high, row_low)
     far34, long13, over2, below, above = stage = send(
@@ -547,7 +580,7 @@
     fars += [(far12, 0), (far12, 1), (far34, 0), (far34, 1)]
     first_mapped = outer(0, 3)
     padded = (below, inner, above)
-    forecast = cast_inner(inner_table(0), padded, *bands[0], model_noise, None)
+    forecast = cast_inner(inner_table, padded, *bands[0], model_noise, None)
     far5, last_over, outer_below, outer_above = send(
         [far_trips[3], (ends3, "row", over), (mapped[count - 1][0], "col", up), (mapped[0][0], "col", down)],
         *stage, *first_mapped, forecast,
@@ -557,16 +590,9 @@
     outer(3, 2)
     outer(5, 1)
     parts = [mapped[i] for i in range(-1, count + 1)]
-    forecast = cast_outer(outer_table(0), parts, *bands[0], model_noise, forecast)
-    columns1 = [
-        entry(pair1, 0, True, always), entry(long11, 1, longs, always), entry(short11, 1, shorts, ~end),
-        entry(long12, 2, longs, always), entry(mixed4, 2, shorts, ~end), entry(long13, 3, longs, always),
-        entry(over1, 1, shorts, end, 1 - y), entry(over2, 2, shorts, end, 1 - y), entry(last_over, 3, shorts, end, 1 - y),
-    ]
-    bands.append(place(columns1, part_flags(1)))
-    half = 1 - y
-    table = jnp.stack([half * part_blocks, half * (part_blocks // 2), (1 - y) * N, 2 * y * N]).astype(jnp.int32)
-    return cast_rest(table, padded, parts, *bands[1], model_noise, forecast)
+    forecast = cast_outer(outer_table, parts, *bands[0], model_noise, forecast)
+    pieces1 = plain(pair1, long11, short11, long12, mixed4, long13, over1, over2, last_over)
+    return cast_rest(rest_table, padded, parts, pieces1, tables1, model_noise, forecast)
 
 
 def solution(mesh):

time: 480 us -> 468 us (0.975)
  waiting for transfers between devices: 153 us -> 145 us
  starting transfers between devices: 103 us -> 96.6 us
  local copies, waits for them, and re-layouts: 26.1 us -> 32 us
    ppermute x34, waiting for transfers between devices: 138 us -> 130 us  [send(): permute(value, axis, perm)]
    ppermute x34, starting transfers between devices: 101 us -> 95 us  [send(): permute(value, axis, perm)]
    unnamed x34 -> x60, local copies, waits for them, and re-layouts: 3.29 us -> 8.63 us
  transfers between devices with their start and end apart: 35 -> 35, of which waited for: 12 -> 15; matrix products, arithmetic and copies ran while one was open for 9% -> 9% of each run, Pallas kernels for 27% -> 28%
where the time goes in v3:
time: 468 us; the launch traced here: 467 us
  Pallas kernels  168 us (36%)
  waiting for transfers between devices  145 us (31%)
  starting transfers between devices  96.6 us (21%)
  local copies, waits for them, and re-layouts  32 us (7%)
  other arithmetic  24.2 us (5%)
    pallas_call x10, Pallas kernels, call(): pl.pallas_call(kernel, grid_spec=pltpu.PrefetchScalarGridSpec(num_scalar_...  168 us
    ppermute x34, waiting for transfers between devices, send(): permute(value, axis, perm)  130 us
    ppermute x34, starting transfers between devices, send(): permute(value, axis, perm)  95 us
    ppermute x1, waiting for transfers between devices, body(): trade0 = permute(pick(1 - y), 'row', swap)  15 us
  transfers between devices with their start and end apart: 35, of which 15 were waited for; matrix products, arithmetic and copies ran while one was open for 9% of the time, Pallas kernels for 28%

profile of v3, /device:TPU:24, one launch (start us, length us, event | category | flops | bytes accessed | tf_op | source)
XLA Modules:
  0.0 466.6 jit_solution(5653109863373975642)
XLA Ops:
  0.0 3.9 constant_dynamic-slice_fusion.4
  5.5 6.9 %constant_dynamic-slice_fusion.10 = (f32[512,512]{1,0:T(8,128)}, f32[512,512]{1,0:T(8,128)}, f32[512,512]{1,0:T(8,128)}, f32[512,512]{1,0:T(8,128)}, f32[512,512...) fusion(f32[1536,3072]{1,0:T(8,128)} %own_b.5, s32[]{:T(128)S(6)} %select_n.237, ...), kind=kLoop, calls=%fused_computation.28 | loop fusion | bytes 16777224 | tf_op jit(solution)/shard_map/dynamic_slice | solution.py:431
  12.4 15.0 %collective-permute-done = f32[6,5,32,256]{3,2,1,0:T(8,128)S(1)} collective-permute-done((f32[6,5,32,256]{3,2,1,0:T(8,128)S(1)}, f32[6,5,32,256]{3,2,1,0:T(8,128)S(1)}, u32[]{:S(2)}, u32[]{:S(2)}) %collective-permute-start) | collective-permute-done | bytes 983072 | tf_op jit(solution)/shard_map/ppermute | solution.py:506
  27.4 1.6 pad_maximum_fusion.3.refs_0_
  31.9 5.9 %collective-permute-start.3 = (f32[2,6,5,32,256]{4,3,2,1,0:T(8,128)}, f32[2,6,5,32,256]{4,3,2,1,0:T(8,128)}, u32[]{:S(2)}, u32[]{:S(2)}) collective-permute-start(f32[2,6,5,32,256]{4,3,2,1,0:T(8,128)} %pad_maximum_fusion.3.refs_0_), channel_id=1, source_target_pairs={{4,12},{12,20},{20,28},{8,0},{16,8},{24,16},{5,13},{13,21},{21,29}... | collective-permute-start | bytes 5898248 | tf_op jit(solution)/shard_map/ppermute | solution.py:436
  37.8 14.2 %collective-permute-done.1 = f32[6,5,32,256]{3,2,1,0:T(8,128)} collective-permute-done((f32[6,5,32,256]{3,2,1,0:T(8,128)}, f32[6,5,32,256]{3,2,1,0:T(8,128)}, u32[]{:S(2)}, u32[]{:S(2)}) %collective-permute-start.1) | collective-permute-done | bytes 983072 | tf_op jit(solution)/shard_map/ppermute | solution.py:436
  52.0 2.0 collective-permute-start.5
  64.8 4.1 constant_dynamic-slice_fusion.12
  68.9 7.9 %collective-permute-done.4.refs_0_ = f32[512,512]{1,0:T(8,128)} collective-permute-done((f32[512,512]{1,0:T(8,128)}, f32[512,512]{1,0:T(8,128)}, u32[]{:S(2)}, u32[]{:S(2)}) %collective-permute-start.4) | collective-permute-done | bytes 1048608 | tf_op jit(solution)/shard_map/ppermute | solution.py:436
  81.7 2.8 pad_maximum_fusion.4.refs_8_
  92.3 32.5 %collective-permute-done.6 = f32[2,6,5,32,256]{4,3,2,1,0:T(8,128)S(1)} collective-permute-done((f32[2,6,5,32,256]{4,3,2,1,0:T(8,128)S(1)}, f32[2,6,5,32,256]{4,3,2,1,0:T(8,128)S(1)}, u32[]{:S(2)}, u32[]{:S(2)}) %collective-permute-start.6) | collective-permute-done | bytes 1966112 | tf_op jit(solution)/shard_map/ppermute | solution.py:436
  124.8 1.9 broadcast_select_fusion.5.refs_3_.refs_9_
  126.7 3.9 collective-permute-done.8.refs_1_.refs_2_
  130.6 1.9 collective-permute-start.14
  132.5 2.0 collective-permute-start.13
  134.5 7.9 %collective-permute-start.11 = (f32[2,6,5,32,256]{4,3,2,1,0:T(8,128)}, f32[2,6,5,32,256]{4,3,2,1,0:T(8,128)}, u32[]{:S(2)}, u32[]{:S(2)}) collective-permute-start(f32[2,6,5,32,256]{4,3,2,1,0:T(8,128)} %pad_maximum_fusion.4.refs_8_), channel_id=1, source_target_pairs={{4,12},{12,20},{16,8},{24,16},{5,13},{13,21},{17,9},{25,17},{6,14}... | collective-permute-start | bytes 5898248 | tf_op jit(solution)/shard_map/ppermute | solution.py:436
  143.7 1.6 broadcast_select_fusion.1
  146.7 1.9 broadcast_select_fusion.2
  148.6 1.9 broadcast_select_fusion.3
  150.6 2.2 pad_maximum_fusion
  152.8 29.9 %collective-permute-done.11.refs_10_ = f32[2,6,5,32,256]{4,3,2,1,0:T(8,128)} collective-permute-done((f32[2,6,5,32,256]{4,3,2,1,0:T(8,128)}, f32[2,6,5,32,256]{4,3,2,1,0:T(8,128)}, u32[]{:S(2)}, u32[]{:S(2)}) %collective-permute-start.11) | collective-permute-done | bytes 1966112 | tf_op jit(solution)/shard_map/ppermute | solution.py:436
  182.7 5.5 %collective-permute-done.12.refs_4_.refs_0_ = f32[2,6,5,32,256]{4,3,2,1,0:T(8,128)S(1)} collective-permute-done((f32[2,6,5,32,256]{4,3,2,1,0:T(8,128)}, f32[2,6,5,32,256]{4,3,2,1,0:T(8,128)S(1)}, u32[]{:S(2)}, u32[]{:S(2)}) %collective-permute-start.12) | collective-permute-done | bytes 1966112 | tf_op jit(solution)/shard_map/ppermute | solution.py:436
  188.2 2.0 broadcast_select_fusion.6
  193.9 5.6 %collective-permute-start.18 = (f32[512,512]{1,0:T(8,128)}, f32[512,512]{1,0:T(8,128)}, u32[]{:S(2)}, u32[]{:S(2)}) collective-permute-start(f32[512,512]{1,0:T(8,128)} %get-tuple-element.70), channel_id=1, source_target_pairs={{0,4},{4,0},{8,12},{12,8},{16,20},{20,16},{24,28},{28,24},{1,5},{5... | collective-permute-start | bytes 3145736 | tf_op jit(solution)/shard_map/ppermute | solution.py:436
  199.5 5.8 %collective-permute-start.19 = (f32[512,512]{1,0:T(8,128)}, f32[512,512]{1,0:T(8,128)}, u32[]{:S(2)}, u32[]{:S(2)}) collective-permute-start(f32[512,512]{1,0:T(8,128)} %get-tuple-element.71), channel_id=1, source_target_pairs={{4,8},{12,16},{20,24},{8,4},{16,12},{24,20},{5,9},{13,17},{21,25},... | collective-permute-start | bytes 3145736 | tf_op jit(solution)/shard_map/ppermute | solution.py:436
  205.3 8.9 %place_slabs.2 = (bf16[6,256,1280]{2,1,0:T(8,128)(2,1)}, bf16[6,256,1280]{2,1,0:T(8,128)(2,1)}) custom-call(s32[5]{0:T(128)} %stack.345.use, s32[5]{0:T(128)} %stack.348.source, s32[5]{0:T(128)} %stack.349.first, s32[30]{0:T(128)} %reshape.25.flags, f32[2,6,5,32,256]{4,3,2,1,0:T(8,128)} %pad_maximum_fusion.3.refs_0_, f32[2,6,5,32,256]{4,3,2,1,0:T(8,128)} %copy-done.4, ...), custom_call_target="tpu_custom_call" | custom-call | bytes 4915200 | tf_op jit(solution)/shard_map/place_slabs/pallas_call | solution.py:27
  214.2 1.9 broadcast_select_fusion
  216.1 2.0 copy-done.7
  218.1 9.5 %place_slabs.3 = (bf16[6,256,1280]{2,1,0:T(8,128)(2,1)}, bf16[6,256,1280]{2,1,0:T(8,128)(2,1)}) custom-call(s32[12]{0:T(128)} %stack.363.use, s32[12]{0:T(128)} %stack.364.source, s32[12]{0:T(128)} %stack.365.first, s32[30]{0:T(128)} %reshape.26.flags, f32[2,6,5,32,256]{4,3,2,1,0:T(8,128)} %pad_maximum_fusion.3.refs_0_, ...), custom_call_target="tpu_custom_call" | custom-call | bytes 13762560 | tf_op jit(solution)/shard_map/place_slabs/pallas_call | solution.py:27
  227.6 16.1 %collective-permute-done.18.refs_5_ = f32[512,512]{1,0:T(8,128)} collective-permute-done((f32[512,512]{1,0:T(8,128)}, f32[512,512]{1,0:T(8,128)}, u32[]{:S(2)}, u32[]{:S(2)}) %collective-permute-start.18) | collective-permute-done | bytes 1048608 | tf_op jit(solution)/shard_map/ppermute | solution.py:436
  243.7 1.8 collective-permute-done.17.refs_9_
  249.5 26.2 %collective-permute-start.24 = (f32[512,1024]{1,0:T(8,128)}, f32[512,1024]{1,0:T(8,128)S(1)}, u32[]{:S(2)}, u32[]{:S(2)}) collective-permute-start(f32[512,1024]{1,0:T(8,128)} %pad_maximum_fusion.2), channel_id=1, source_target_pairs={{4,8},{12,16},{20,24},{8,4},{16,12},{24,20},{5,9},{13,17},{21,25},... | collective-permute-start | bytes 6291464 | tf_op jit(solution)/shard_map/ppermute | solution.py:436
  275.7 6.2 %place_last.1 = (bf16[6,256,1280]{2,1,0:T(8,128)(2,1)}, bf16[6,256,1280]{2,1,0:T(8,128)(2,1)}) custom-call(s32[3]{0:T(128)} %add_convert_fusion.use, s32[3]{0:T(128)} %stack.371.source, s32[3]{0:T(128)} %stack.372.first, s32[30]{0:T(128)} %reshape.26.flags, s32[1]{0:T(128)} %bitcast.31.group, ...), custom_call_target="tpu_custom_call", output_to_operand_aliasing={{0}: (8, {}), {1}: (9, {})} | custom-call | bytes 6881280 | tf_op jit(solution)/shard_map/place_last/pallas_call | solution.py:27
  281.9 38.6 %map_inner.1 = (f32[3072,1024]{1,0:T(8,128)}, f32[512,1024]{1,0:T(8,128)}, f32[512,1024]{1,0:T(8,128)}) custom-call(s32[1]{0:T(128)} %bitcast.20.y, f32[1536,3072]{1,0:T(8,128)} %own_b.5, f32[512,512]{1,0:T(8,128)} %collective-permute-done.4.refs_0_, f32[512,1024]{1,0:T(8,128)} %copy-done.29, f32[512,1024]{1,0:T(8,128)} %copy-done.29, ...), custom_call_target="tpu_custom_call" | custom-call | flops 24159191040 | bytes 22544384 | tf_op jit(solution)/shard_map/map_inner/pallas_call | solution.py:27
  322.5 1.6 collective-permute-start.26
  325.4 3.3 collective-permute-start.28
  330.0 2.6 collective-permute-start.30
  332.6 15.1 %map_outer.3 = (f32[512,512]{1,0:T(8,128)}, f32[512,512]{1,0:T(8,128)}, f32[512,512]{1,0:T(8,128)}) custom-call(s32[1]{0:T(128)} %bitcast.20.y, s32[3]{0:T(128)} %constant.102.clone.chunks, f32[1536,3072]{1,0:T(8,128)} %own_b.5, f32[1536,3072]{1,0:T(8,128)} %own_b.5, f32[512,512]{1,0:T(8,128)} %collective-permute-done.19.refs_0_, f32[512,1024]{1,0:T(8,128)} %copy-done.10, ...), custom_call_target="tpu_custom_call" | custom-call | flops 6039797760 | bytes 25427968 | tf_op jit(solution)/shard_map/map_outer/pallas_call | solution.py:27
  349.7 21.6 %cast_inner.1.refs_11_ = f32[3072,1536]{1,0:T(8,128)} custom-call(s32[2]{0:T(128)} %pad_add_fusion.1.table, f32[512,1024]{1,0:T(8,128)} %copy-done.8, f32[3072,1024]{1,0:T(8,128)} %get-tuple-element.85.mid, f32[512,1024]{1,0:T(8,128)} %copy-done.9, bf16[6,256,1280]{2,1,0:T(8,128)(2,1)} %get-tuple-element.74.high.refs_8_, ...), custom_call_target="tpu_custom_call" | custom-call | flops 12079595520 | bytes 21757952 | tf_op jit(solution)/shard_map/cast_inner/pallas_call | solution.py:27
  371.2 5.2 %collective-permute-done.29.refs_13_ = f32[2,6,5,32,256]{4,3,2,1,0:T(8,128)} collective-permute-done((f32[2,6,5,32,256]{4,3,2,1,0:T(8,128)}, f32[2,6,5,32,256]{4,3,2,1,0:T(8,128)}, u32[]{:S(2)}, u32[]{:S(2)}) %collective-permute-start.29) | collective-permute-done | bytes 1966112 | tf_op jit(solution)/shard_map/ppermute | solution.py:436
  376.9 2.3 collective-permute-start.34
  379.1 1.9 collective-permute-start.32
  381.1 1.8 collective-permute-start.31
  384.4 11.4 %map_outer.4 = (f32[512,512]{1,0:T(8,128)}, f32[512,512]{1,0:T(8,128)}) custom-call(s32[1]{0:T(128)} %bitcast.20.y, s32[2]{0:T(128)} %constant.103.clone.chunks, f32[1536,3072]{1,0:T(8,128)} %own_b.5, f32[1536,3072]{1,0:T(8,128)} %own_b.5, f32[512,1024]{1,0:T(8,128)} %collective-permute-done.28.refs_0_.refs_1_, ...), custom_call_target="tpu_custom_call" | custom-call | flops 4026531840 | bytes 24903680 | tf_op jit(solution)/shard_map/map_outer/pallas_call | solution.py:27
  395.8 11.4 %collective-permute-done.32.refs_0_ = f32[512,512]{1,0:T(8,128)} collective-permute-done((f32[512,512]{1,0:T(8,128)}, f32[512,512]{1,0:T(8,128)}, u32[]{:S(2)}, u32[]{:S(2)}) %collective-permute-start.32) | collective-permute-done | bytes 1048608 | tf_op jit(solution)/shard_map/ppermute | solution.py:436
  407.1 6.7 %map_outer.5.refs_4_ = f32[512,512]{1,0:T(8,128)} custom-call(s32[1]{0:T(128)} %bitcast.20.y, s32[1]{0:T(128)} %constant.104.clone.chunks, f32[1536,3072]{1,0:T(8,128)} %own_b.5, f32[1536,3072]{1,0:T(8,128)} %own_b.5, f32[512,512]{1,0:T(8,128)} %collective-permute-done.32.refs_0_, ...), custom_call_target="tpu_custom_call" | custom-call | flops 2013265920 | bytes 23330816 | tf_op jit(solution)/shard_map/map_outer/pallas_call | solution.py:27
  415.2 14.7 %cast_outer.1.refs_18_ = f32[3072,1536]{1,0:T(8,128)} custom-call(s32[3]{0:T(128)} %pad_add_fusion.2.table, f32[512,512]{1,0:T(8,128)} %copy-done.14, f32[512,512]{1,0:T(8,128)} %get-tuple-element.99.refs_1_, f32[512,512]{1,0:T(8,128)} %get-tuple-element.93.refs_2_, f32[512,512]{1,0:T(8,128)} %get-tuple-element.96.refs_3_, ...), custom_call_target="tpu_custom_call", output_to_operand_aliasing={{}: (12, {})} | custom-call | flops 6039797760 | bytes 27000832 | tf_op jit(solution)/shard_map/cast_outer/pallas_call | solution.py:27
  431.1 35.3 %cast_rest.1 = f32[3072,1536]{1,0:T(8,128)} custom-call(s32[4]{0:T(128)} %pad_add_fusion.table, s32[9]{0:T(128)} %stack.323.use, s32[9]{0:T(128)} %stack.331.source, s32[9]{0:T(128)} %stack.334.first, s32[30]{0:T(128)} %reshape.23.flags, f32[512,1024]{1,0:T(8,128)} %copy-done.8, ...), custom_call_target="tpu_custom_call", output_to_operand_aliasing={{}: (26, {})} | custom-call | flops 18119393280 | bytes 40304640 | tf_op jit(solution)/shard_map/cast_rest/pallas_call | solution.py:27
  (130 shorter events, 49.3 us)
Async XLA Ops:
  3.9 23.5 %collective-permute-start = (f32[6,5,32,256]{3,2,1,0:T(8,128)S(1)}, f32[6,5,32,256]{3,2,1,0:T(8,128)S(1)}, u32[]{:S(2)}, u32[]{:S(2)}) collective-permute-start(f32[6,5,32,256]{3,2,1,0:T(8,128)S(1)} %get-tuple-element.112), channel_id=1, source_target_pairs={{0,4},{4,0},{8,12},{12,8},{16,20},{20,16},{24,28},{28,24},{1,5},{5... | collective-permute-start | bytes 2949128 | tf_op jit(solution)/shard_map/ppermute | solution.py:506
  27.4 30.2 %copy-start.28 = (s32[48,5]{0,1:T(8,128)S(1)}, s32[48,5]{0,1:T(8,128)}, u32[]{:S(2)}) copy-start(s32[48,5]{0,1:T(8,128)} %param.9) | copy-start | bytes 2884
  29.1 22.9 %collective-permute-start.1 = (f32[6,5,32,256]{3,2,1,0:T(8,128)}, f32[6,5,32,256]{3,2,1,0:T(8,128)}, u32[]{:S(2)}, u32[]{:S(2)}) collective-permute-start(f32[6,5,32,256]{3,2,1,0:T(8,128)} %get-tuple-element.53), channel_id=1, source_target_pairs={{0,4},{4,0},{8,12},{12,8},{16,20},{20,16},{24,28},{28,24},{1,5},{5... | collective-permute-start | bytes 2949128 | tf_op jit(solution)/shard_map/ppermute | solution.py:436
  30.6 46.1 %collective-permute-start.2 = (f32[2,6,5,32,256]{4,3,2,1,0:T(8,128)}, f32[2,6,5,32,256]{4,3,2,1,0:T(8,128)S(1)}, u32[]{:S(2)}, u32[]{:S(2)}) collective-permute-start(f32[2,6,5,32,256]{4,3,2,1,0:T(8,128)} %pad_maximum_fusion.3.refs_0_), channel_id=1, source_target_pairs={{0,8},{8,16},{16,24},{12,4},{20,12},{28,20},{1,9},{9,17},{17,25},{... | collective-permute-start | bytes 5898248 | tf_op jit(solution)/shard_map/ppermute | solution.py:436
  31.9 45.5 %collective-permute-start.3 = (f32[2,6,5,32,256]{4,3,2,1,0:T(8,128)}, f32[2,6,5,32,256]{4,3,2,1,0:T(8,128)}, u32[]{:S(2)}, u32[]{:S(2)}) collective-permute-start(f32[2,6,5,32,256]{4,3,2,1,0:T(8,128)} %pad_maximum_fusion.3.refs_0_), channel_id=1, source_target_pairs={{4,12},{12,20},{20,28},{8,0},{16,8},{24,16},{5,13},{13,21},{21,29}... | collective-permute-start | bytes 5898248 | tf_op jit(solution)/shard_map/ppermute | solution.py:436
  52.0 25.4 %collective-permute-start.5 = (f32[2,6,5,32,256]{4,3,2,1,0:T(8,128)}, f32[2,6,5,32,256]{4,3,2,1,0:T(8,128)}, u32[]{:S(2)}, u32[]{:S(2)}) collective-permute-start(f32[2,6,5,32,256]{4,3,2,1,0:T(8,128)} %pad_maximum_fusion.3.refs_0_), channel_id=1, source_target_pairs={{0,2},{4,6},{9,11},{13,15},{18,16},{22,20},{27,25},{31,29}} | collective-permute-start | bytes 5898248 | tf_op jit(solution)/shard_map/ppermute | solution.py:436
  54.0 22.8 %collective-permute-start.4 = (f32[512,512]{1,0:T(8,128)}, f32[512,512]{1,0:T(8,128)}, u32[]{:S(2)}, u32[]{:S(2)}) collective-permute-start(f32[512,512]{1,0:T(8,128)} %get-tuple-element.56), channel_id=1, source_target_pairs={{0,4},{4,0},{8,12},{12,8},{16,20},{20,16},{24,28},{28,24},{1,5},{5... | collective-permute-start | bytes 3145736 | tf_op jit(solution)/shard_map/ppermute | solution.py:436
  64.8 16.8 %copy-start.20 = (f32[1,6,5,32,256]{4,3,2,1,0:T(8,128)S(1)}, f32[1,6,5,32,256]{4,3,2,1,0:T(8,128)}, u32[]{:S(2)}) copy-start(f32[1,6,5,32,256]{4,3,2,1,0:T(8,128)} %get-tuple-element.111) | copy-start | bytes 2949124
  76.8 9.6 %copy-start.4 = (f32[2,6,5,32,256]{4,3,2,1,0:T(8,128)}, f32[2,6,5,32,256]{4,3,2,1,0:T(8,128)S(1)}, u32[]{:S(2)}) copy-start(f32[2,6,5,32,256]{4,3,2,1,0:T(8,128)S(1)} %collective-permute-done.2.refs_1_.refs_3_) | copy-start | bytes 5898244
  79.6 45.2 %collective-permute-start.6 = (f32[2,6,5,32,256]{4,3,2,1,0:T(8,128)S(1)}, f32[2,6,5,32,256]{4,3,2,1,0:T(8,128)S(1)}, u32[]{:S(2)}, u32[]{:S(2)}) collective-permute-start(f32[2,6,5,32,256]{4,3,2,1,0:T(8,128)S(1)} %collective-permute-done.2.refs_1_.refs_3_), channel_id=1, source_target_pairs={{8,16},{16,24},{12,4},{20,12},{9,17},{17,25},{13,5},{21,13},{10,18... | collective-permute-start | bytes 5898248 | tf_op jit(solution)/shard_map/ppermute | solution.py:436
  80.9 43.9 %collective-permute-start.7 = (f32[2,6,5,32,256]{4,3,2,1,0:T(8,128)}, f32[2,6,5,32,256]{4,3,2,1,0:T(8,128)S(1)}, u32[]{:S(2)}, u32[]{:S(2)}) collective-permute-start(f32[2,6,5,32,256]{4,3,2,1,0:T(8,128)} %collective-permute-done.3.refs_2_.refs_6_), channel_id=1, source_target_pairs={{12,20},{20,28},{8,0},{16,8},{13,21},{21,29},{9,1},{17,9},{14,22},... | collective-permute-start | bytes 5898248 | tf_op jit(solution)/shard_map/ppermute | solution.py:436
  84.4 46.1 %collective-permute-start.8 = (f32[512,1024]{1,0:T(8,128)S(1)}, f32[512,1024]{1,0:T(8,128)S(1)}, u32[]{:S(2)}, u32[]{:S(2)}) collective-permute-start(f32[512,1024]{1,0:T(8,128)S(1)} %get-tuple-element.60), channel_id=1, source_target_pairs={{0,4},{4,0},{8,12},{12,8},{16,20},{20,16},{24,28},{28,24},{1,5},{5... | collective-permute-start | bytes 6291464 | tf_op jit(solution)/shard_map/ppermute | solution.py:436
  86.4 40.3 %collective-permute-start.9 = (f32[2,6,5,32,256]{4,3,2,1,0:T(8,128)S(1)}, f32[2,6,5,32,256]{4,3,2,1,0:T(8,128)S(1)}, u32[]{:S(2)}, u32[]{:S(2)}) collective-permute-start(f32[2,6,5,32,256]{4,3,2,1,0:T(8,128)S(1)} %collective-permute-done.2.refs_1_.refs_3_), channel_id=1, source_target_pairs={{4,6},{9,11},{13,15},{18,16},{22,20},{27,25}} | collective-permute-start | bytes 5898248 | tf_op jit(solution)/shard_map/ppermute | solution.py:436
  87.2 39.5 %collective-permute-start.10 = (f32[2,6,5,32,256]{4,3,2,1,0:T(8,128)S(1)}, f32[2,6,5,32,256]{4,3,2,1,0:T(8,128)S(1)}, u32[]{:S(2)}, u32[]{:S(2)}) collective-permute-start(f32[2,6,5,32,256]{4,3,2,1,0:T(8,128)S(1)} %broadcast_select_fusion.4), channel_id=1, source_target_pairs={{0,1},{2,3},{4,5},{6,7},{9,8},{11,10},{13,12},{15,14},{16,17},{18,... | collective-permute-start | bytes 5898248 | tf_op jit(solution)/shard_map/ppermute | solution.py:436
  92.3 51.4 %copy-start.5 = (f32[2,6,5,32,256]{4,3,2,1,0:T(8,128)S(1)}, f32[2,6,5,32,256]{4,3,2,1,0:T(8,128)}, u32[]{:S(2)}) copy-start(f32[2,6,5,32,256]{4,3,2,1,0:T(8,128)} %copy-done.4) | copy-start | bytes 5898244
  126.7 18.7 %copy-start.11 = (f32[2,6,5,32,256]{4,3,2,1,0:T(8,128)}, f32[2,6,5,32,256]{4,3,2,1,0:T(8,128)S(1)}, u32[]{:S(2)}) copy-start(f32[2,6,5,32,256]{4,3,2,1,0:T(8,128)S(1)} %collective-permute-done.9.refs_4_) | copy-start | bytes 5898244
  126.7 18.7 %copy-start.27 = (f32[2,6,5,32,256]{4,3,2,1,0:T(8,128)}, f32[2,6,5,32,256]{4,3,2,1,0:T(8,128)S(1)}, u32[]{:S(2)}) copy-start(f32[2,6,5,32,256]{4,3,2,1,0:T(8,128)S(1)} %collective-permute-done.10.refs_2_) | copy-start | bytes 5898244
  130.6 14.8 %copy-start.29 = (f32[512,1024]{1,0:T(8,128)}, f32[512,1024]{1,0:T(8,128)S(1)}, u32[]{:S(2)}) copy-start(f32[512,1024]{1,0:T(8,128)S(1)} %collective-permute-done.8.refs_1_.refs_2_) | copy-start | bytes 6291460
  130.6 14.8 %collective-permute-start.14 = (f32[2,6,5,32,256]{4,3,2,1,0:T(8,128)}, f32[2,6,5,32,256]{4,3,2,1,0:T(8,128)}, u32[]{:S(2)}, u32[]{:S(2)}) collective-permute-start(f32[2,6,5,32,256]{4,3,2,1,0:T(8,128)} %broadcast_select_fusion.5.refs_3_.refs_9_), channel_id=1, source_target_pairs={{0,2},{4,6},{9,11},{13,15},{18,16},{22,20},{27,25},{31,29}} | collective-permute-start | bytes 5898248 | tf_op jit(solution)/shard_map/ppermute | solution.py:436
  132.5 16.1 %collective-permute-start.13 = (f32[2,6,5,32,256]{4,3,2,1,0:T(8,128)}, f32[2,6,5,32,256]{4,3,2,1,0:T(8,128)}, u32[]{:S(2)}, u32[]{:S(2)}) collective-permute-start(f32[2,6,5,32,256]{4,3,2,1,0:T(8,128)} %collective-permute-done.3.refs_2_.refs_6_), channel_id=1, source_target_pairs={{0,2},{9,11},{13,15},{18,16},{22,20},{31,29}} | collective-permute-start | bytes 5898248 | tf_op jit(solution)/shard_map/ppermute | solution.py:436
  134.5 48.2 %collective-permute-start.11 = (f32[2,6,5,32,256]{4,3,2,1,0:T(8,128)}, f32[2,6,5,32,256]{4,3,2,1,0:T(8,128)}, u32[]{:S(2)}, u32[]{:S(2)}) collective-permute-start(f32[2,6,5,32,256]{4,3,2,1,0:T(8,128)} %pad_maximum_fusion.4.refs_8_), channel_id=1, source_target_pairs={{4,12},{12,20},{16,8},{24,16},{5,13},{13,21},{17,9},{25,17},{6,14}... | collective-permute-start | bytes 5898248 | tf_op jit(solution)/shard_map/ppermute | solution.py:436
  142.3 45.8 %collective-permute-start.12 = (f32[2,6,5,32,256]{4,3,2,1,0:T(8,128)}, f32[2,6,5,32,256]{4,3,2,1,0:T(8,128)S(1)}, u32[]{:S(2)}, u32[]{:S(2)}) collective-permute-start(f32[2,6,5,32,256]{4,3,2,1,0:T(8,128)} %broadcast_select_fusion.5.refs_3_.refs_9_), channel_id=1, source_target_pairs={{16,24},{12,4},{20,28},{8,0},{17,25},{13,5},{21,29},{9,1},{18,26},... | collective-permute-start | bytes 5898248 | tf_op jit(solution)/shard_map/ppermute | solution.py:436
  143.6 46.7 %collective-permute-start.15 = (f32[512,1024]{1,0:T(8,128)}, f32[512,1024]{1,0:T(8,128)}, u32[]{:S(2)}, u32[]{:S(2)}) collective-permute-start(f32[512,1024]{1,0:T(8,128)} %get-tuple-element.67), channel_id=1, source_target_pairs={{0,4},{4,0},{8,12},{12,8},{16,20},{20,16},{24,28},{28,24},{1,5},{5... | collective-permute-start | bytes 6291464 | tf_op jit(solution)/shard_map/ppermute | solution.py:436
  145.4 45.0 %collective-permute-start.16 = (f32[2,6,5,32,256]{4,3,2,1,0:T(8,128)}, f32[2,6,5,32,256]{4,3,2,1,0:T(8,128)}, u32[]{:S(2)}, u32[]{:S(2)}) collective-permute-start(f32[2,6,5,32,256]{4,3,2,1,0:T(8,128)} %broadcast_select_fusion.1), channel_id=1, source_target_pairs={{4,5},{6,7},{9,8},{11,10},{13,12},{15,14},{16,17},{18,19},{20,21},... | collective-permute-start | bytes 5898248 | tf_op jit(solution)/shard_map/ppermute | solution.py:436
  190.4 23.8 %copy-start.1 = (f32[2,6,5,32,256]{4,3,2,1,0:T(8,128)S(1)}, f32[2,6,5,32,256]{4,3,2,1,0:T(8,128)}, u32[]{:S(2)}) copy-start(f32[2,6,5,32,256]{4,3,2,1,0:T(8,128)} %copy-done) | copy-start | bytes 5898244
  190.4 25.8 %collective-permute-start.21 = (f32[4,6,5,32,256]{4,3,2,1,0:T(8,128)}, f32[4,6,5,32,256]{4,3,2,1,0:T(8,128)S(1)}, u32[]{:S(2)}, u32[]{:S(2)}) collective-permute-start(f32[4,6,5,32,256]{4,3,2,1,0:T(8,128)} %pad_maximum_fusion), channel_id=1, source_target_pairs={{0,1},{2,3},{4,5},{6,7},{9,8},{11,10},{13,12},{15,14},{16,17},{18,... | collective-permute-start | bytes 11796488 | tf_op jit(solution)/shard_map/ppermute | solution.py:436
  191.8 22.4 %collective-permute-start.20 = (f32[2,6,5,32,256]{4,3,2,1,0:T(8,128)}, f32[2,6,5,32,256]{4,3,2,1,0:T(8,128)S(1)}, u32[]{:S(2)}, u32[]{:S(2)}) collective-permute-start(f32[2,6,5,32,256]{4,3,2,1,0:T(8,128)} %broadcast_select_fusion.6), channel_id=1, source_target_pairs={{12,20},{13,21},{14,22},{15,23},{16,8},{17,9},{18,10},{19,11},{0,2... | collective-permute-start | bytes 5898248 | tf_op jit(solution)/shard_map/ppermute | solution.py:436
  192.6 52.9 %collective-permute-start.17 = (f32[2,6,5,32,256]{4,3,2,1,0:T(8,128)}, f32[2,6,5,32,256]{4,3,2,1,0:T(8,128)}, u32[]{:S(2)}, u32[]{:S(2)}) collective-permute-start(f32[2,6,5,32,256]{4,3,2,1,0:T(8,128)} %pad_maximum_fusion.4.refs_8_), channel_id=1, source_target_pairs={{0,8},{8,16},{16,24},{12,4},{20,12},{28,20},{1,9},{9,17},{17,25},{... | collective-permute-start | bytes 5898248 | tf_op jit(solution)/shard_map/ppermute | solution.py:436
  193.9 49.8 %collective-permute-start.18 = (f32[512,512]{1,0:T(8,128)}, f32[512,512]{1,0:T(8,128)}, u32[]{:S(2)}, u32[]{:S(2)}) collective-permute-start(f32[512,512]{1,0:T(8,128)} %get-tuple-element.70), channel_id=1, source_target_pairs={{0,4},{4,0},{8,12},{12,8},{16,20},{20,16},{24,28},{28,24},{1,5},{5... | collective-permute-start | bytes 3145736 | tf_op jit(solution)/shard_map/ppermute | solution.py:436
  199.5 44.2 %collective-permute-start.19 = (f32[512,512]{1,0:T(8,128)}, f32[512,512]{1,0:T(8,128)}, u32[]{:S(2)}, u32[]{:S(2)}) collective-permute-start(f32[512,512]{1,0:T(8,128)} %get-tuple-element.71), channel_id=1, source_target_pairs={{4,8},{12,16},{20,24},{8,4},{16,12},{24,20},{5,9},{13,17},{21,25},... | collective-permute-start | bytes 3145736 | tf_op jit(solution)/shard_map/ppermute | solution.py:436
  216.1 31.9 %copy-start.6 = (f32[2,6,5,32,256]{4,3,2,1,0:T(8,128)S(1)}, f32[2,6,5,32,256]{4,3,2,1,0:T(8,128)}, u32[]{:S(2)}) copy-start(f32[2,6,5,32,256]{4,3,2,1,0:T(8,128)} %copy-done.4) | copy-start | bytes 5898244
  245.5 30.3 %collective-permute-start.23 = (f32[2,6,5,32,256]{4,3,2,1,0:T(8,128)}, f32[2,6,5,32,256]{4,3,2,1,0:T(8,128)}, u32[]{:S(2)}, u32[]{:S(2)}) collective-permute-start(f32[2,6,5,32,256]{4,3,2,1,0:T(8,128)} %broadcast_select_fusion), channel_id=1, source_target_pairs={{0,1},{2,3},{4,5},{6,7},{25,24},{27,26},{29,28},{31,30}} | collective-permute-start | bytes 5898248 | tf_op jit(solution)/shard_map/ppermute | solution.py:436
  246.8 73.8 %collective-permute-start.22 = (f32[2,6,5,32,256]{4,3,2,1,0:T(8,128)}, f32[2,6,5,32,256]{4,3,2,1,0:T(8,128)S(1)}, u32[]{:S(2)}, u32[]{:S(2)}) collective-permute-start(f32[2,6,5,32,256]{4,3,2,1,0:T(8,128)} %collective-permute-done.17.refs_9_), channel_id=1, source_target_pairs={{8,16},{16,24},{12,4},{20,12},{9,17},{17,25},{13,5},{21,13},{10,18... | collective-permute-start | bytes 5898248 | tf_op jit(solution)/shard_map/ppermute | solution.py:436
  248.1 72.5 %collective-permute-start.25 = (f32[2,6,5,32,256]{4,3,2,1,0:T(8,128)S(1)}, f32[2,6,5,32,256]{4,3,2,1,0:T(8,128)S(1)}, u32[]{:S(2)}, u32[]{:S(2)}) collective-permute-start(f32[2,6,5,32,256]{4,3,2,1,0:T(8,128)S(1)} %copy-done.6), channel_id=1, source_target_pairs={{4,0},{24,28},{5,1},{25,29},{6,2},{26,30},{7,3},{27,31}} | collective-permute-start | bytes 5898248 | tf_op jit(solution)/shard_map/ppermute | solution.py:436
  249.5 71.9 %collective-permute-start.24 = (f32[512,1024]{1,0:T(8,128)}, f32[512,1024]{1,0:T(8,128)S(1)}, u32[]{:S(2)}, u32[]{:S(2)}) collective-permute-start(f32[512,1024]{1,0:T(8,128)} %pad_maximum_fusion.2), channel_id=1, source_target_pairs={{4,8},{12,16},{20,24},{8,4},{16,12},{24,20},{5,9},{13,17},{21,25},... | collective-permute-start | bytes 6291464 | tf_op jit(solution)/shard_map/ppermute | solution.py:436
  321.4 11.2 %copy-start.10 = (f32[512,1024]{1,0:T(8,128)}, f32[512,1024]{1,0:T(8,128)S(1)}, u32[]{:S(2)}) copy-start(f32[512,1024]{1,0:T(8,128)S(1)} %collective-permute-done.24.refs_1_.refs_2_) | copy-start | bytes 6291460
  322.5 25.2 %collective-permute-start.26 = (f32[512,1024]{1,0:T(8,128)}, f32[512,1024]{1,0:T(8,128)S(1)}, u32[]{:S(2)}, u32[]{:S(2)}) collective-permute-start(f32[512,1024]{1,0:T(8,128)} %get-tuple-element.86), channel_id=1, source_target_pairs={{0,1},{1,2},{2,3},{4,5},{5,6},{6,7},{8,9},{9,10},{10,11},{12,13},{... | collective-permute-start | bytes 6291464 | tf_op jit(solution)/shard_map/ppermute | solution.py:436
  324.1 23.6 %collective-permute-start.27 = (f32[512,1024]{1,0:T(8,128)}, f32[512,1024]{1,0:T(8,128)S(1)}, u32[]{:S(2)}, u32[]{:S(2)}) collective-permute-start(f32[512,1024]{1,0:T(8,128)} %get-tuple-element.87), channel_id=1, source_target_pairs={{1,0},{2,1},{3,2},{5,4},{6,5},{7,6},{9,8},{10,9},{11,10},{13,12},{... | collective-permute-start | bytes 6291464 | tf_op jit(solution)/shard_map/ppermute | solution.py:436
  325.4 51.5 %collective-permute-start.28 = (f32[512,1024]{1,0:T(8,128)}, f32[512,1024]{1,0:T(8,128)}, u32[]{:S(2)}, u32[]{:S(2)}) collective-permute-start(f32[512,1024]{1,0:T(8,128)} %pad_maximum_fusion.1), channel_id=1, source_target_pairs={{4,8},{12,16},{20,24},{8,4},{16,12},{24,20},{5,9},{13,17},{21,25},... | collective-permute-start | bytes 6291464 | tf_op jit(solution)/shard_map/ppermute | solution.py:436
  328.7 47.8 %collective-permute-start.29 = (f32[2,6,5,32,256]{4,3,2,1,0:T(8,128)}, f32[2,6,5,32,256]{4,3,2,1,0:T(8,128)}, u32[]{:S(2)}, u32[]{:S(2)}) collective-permute-start(f32[2,6,5,32,256]{4,3,2,1,0:T(8,128)} %copy-done.24), channel_id=1, source_target_pairs={{16,24},{12,4},{17,25},{13,5},{18,26},{14,6},{19,27},{15,7}} | collective-permute-start | bytes 5898248 | tf_op jit(solution)/shard_map/ppermute | solution.py:436
  330.0 46.5 %collective-permute-start.30 = (f32[2,6,5,32,256]{4,3,2,1,0:T(8,128)}, f32[2,6,5,32,256]{4,3,2,1,0:T(8,128)}, u32[]{:S(2)}, u32[]{:S(2)}) collective-permute-start(f32[2,6,5,32,256]{4,3,2,1,0:T(8,128)} %copy-done.23), channel_id=1, source_target_pairs={{4,0},{24,28},{5,1},{25,29},{6,2},{26,30},{7,3},{27,31}} | collective-permute-start | bytes 5898248 | tf_op jit(solution)/shard_map/ppermute | solution.py:436
  349.7 27.2 %copy-start.2 = (f32[2,6,5,32,256]{4,3,2,1,0:T(8,128)S(1)}, f32[2,6,5,32,256]{4,3,2,1,0:T(8,128)}, u32[]{:S(2)}) copy-start(f32[2,6,5,32,256]{4,3,2,1,0:T(8,128)} %copy-done) | copy-start | bytes 5898244
  349.7 31.4 %copy-start.13 = (f32[512,512]{1,0:T(8,128)S(1)}, f32[512,512]{1,0:T(8,128)}, u32[]{:S(2)}) copy-start(f32[512,512]{1,0:T(8,128)} %get-tuple-element.95.refs_6_) | copy-start | bytes 3145732
  349.7 33.2 %copy-start.12 = (f32[512,512]{1,0:T(8,128)S(1)}, f32[512,512]{1,0:T(8,128)}, u32[]{:S(2)}) copy-start(f32[512,512]{1,0:T(8,128)} %get-tuple-element.99.refs_1_) | copy-start | bytes 3145732
  376.9 53.0 %collective-permute-start.34 = (f32[2,6,5,32,256]{4,3,2,1,0:T(8,128)S(1)}, f32[2,6,5,32,256]{4,3,2,1,0:T(8,128)S(1)}, u32[]{:S(2)}, u32[]{:S(2)}) collective-permute-start(f32[2,6,5,32,256]{4,3,2,1,0:T(8,128)S(1)} %copy-done.2), channel_id=1, source_target_pairs={{4,0},{24,28},{5,1},{25,29},{6,2},{26,30},{7,3},{27,31}} | collective-permute-start | bytes 5898248 | tf_op jit(solution)/shard_map/ppermute | solution.py:436
  379.1 28.0 %collective-permute-start.32 = (f32[512,512]{1,0:T(8,128)}, f32[512,512]{1,0:T(8,128)}, u32[]{:S(2)}, u32[]{:S(2)}) collective-permute-start(f32[512,512]{1,0:T(8,128)} %get-tuple-element.97), channel_id=1, source_target_pairs={{4,8},{12,16},{20,24},{8,4},{16,12},{24,20},{5,9},{13,17},{21,25},... | collective-permute-start | bytes 3145736 | tf_op jit(solution)/shard_map/ppermute | solution.py:436
  381.1 32.7 %collective-permute-start.31 = (f32[512,512]{1,0:T(8,128)S(1)}, f32[512,512]{1,0:T(8,128)S(1)}, u32[]{:S(2)}, u32[]{:S(2)}) collective-permute-start(f32[512,512]{1,0:T(8,128)S(1)} %copy-done.13), channel_id=1, source_target_pairs={{0,1},{1,2},{2,3},{4,5},{5,6},{6,7},{8,9},{9,10},{10,11},{12,13},{... | collective-permute-start | bytes 3145736 | tf_op jit(solution)/shard_map/ppermute | solution.py:436
  382.9 30.9 %collective-permute-start.33 = (f32[512,512]{1,0:T(8,128)S(1)}, f32[512,512]{1,0:T(8,128)S(1)}, u32[]{:S(2)}, u32[]{:S(2)}) collective-permute-start(f32[512,512]{1,0:T(8,128)S(1)} %copy-done.12), channel_id=1, source_target_pairs={{1,0},{2,1},{3,2},{5,4},{6,5},{7,6},{9,8},{10,9},{11,10},{13,12},{... | collective-permute-start | bytes 3145736 | tf_op jit(solution)/shard_map/ppermute | solution.py:436
  (17 other events, 35.8 us)

commit v4 on v3

--- a/solution.py
+++ b/solution.py
@@ -105,15 +105,16 @@
     )
 
 
-def inner_kernel(count, y, own, *refs):
+def inner_kernel(spans, y, own, *refs):
+    count = len(spans)
     nears, (high_a, low_a, high_b, low_b, out, head, tail, b_high, b_low) = refs[:count], refs[count:]
     step = pl.program_id(0)
     rows = own.shape[0]
     split_into(b_high, b_low, pl.ds(pl.multiple_of(y[0] * MARGIN, MARGIN), rows), own[...])
     at = pl.ds(pl.multiple_of((1 - y[0]) * rows, MARGIN), MARGIN)
-    for i, near in enumerate(nears):
-
-        @pl.when(step == i)
+    for (at_step, n), near in zip(spans, nears):
+
+        @pl.when((step >= at_step) & (step < at_step + n))
         def _(near=near):
             split_into(b_high, b_low, at, near[...])
 
@@ -126,25 +127,25 @@
     def _():
         head[...] = out[...]
 
-    @pl.when(step == count - 1)
+    @pl.when(step == pl.num_programs(0) - 1)
     def _():
         tail[...] = out[...]
 
 
-def map_inner(y, covariance, nears, row_high, row_low):
+def map_inner(y, covariance, nears, spans, row_high, row_low):
     rows, columns = covariance.shape
     pair_a = pl.BlockSpec((2, BS, WIDE), lambda s, y: (1 - y[0], 0, 0))
     pair_b = pl.BlockSpec((2, BS, WIDE), lambda s, y: (2 - y[0], 0, 0))
     edge = pl.BlockSpec((N, 4 * BS), lambda s, y: (0, 0))
     return call(
-        functools.partial(inner_kernel, len(nears)), "map_inner", [y], (columns // N,),
+        functools.partial(inner_kernel, spans), "map_inner", [y], (columns // N,),
         [pl.BlockSpec((rows, N), lambda s, y: (0, s))]
-        + [pl.BlockSpec((MARGIN, N), lambda s, y, at=at: (0, at)) for _, at in nears]
+        + [pl.BlockSpec((MARGIN, N), lambda s, y, at=at, n=n: (0, jnp.clip(s - at, 0, n - 1))) for at, n in spans]
         + [pair_a, pair_a, pair_b, pair_b],
         [pl.BlockSpec((N, 4 * BS), lambda s, y: (s, 0)), edge, edge],
         [jax.ShapeDtypeStruct((columns, 4 * BS), F32)] + [jax.ShapeDtypeStruct((N, 4 * BS), F32)] * 2,
         [pltpu.VMEM((rows + MARGIN, N), BF16)] * 2,
-        [covariance, *[near for near, _ in nears], row_high, row_low, row_high, row_low], 6 * 4 * BS * WIDE * columns,
+        [covariance, *nears, row_high, row_low, row_high, row_low], 6 * 4 * BS * WIDE * columns,
     )
 
 
@@ -521,13 +522,15 @@
     stage = main + [x1a, core0] + [value for value, _, _ in far_trips]
     last_hops = along(3, True) + along(3, False)
     value2 = jnp.where(climbs(2), long02, short02)
-    near2, ends3, short11, x2, x1b = main = send(
+    near2, short11 = main = send([near_trips[2], (pair1, "row", along(1, False, False))], *stage)
+    ends3, x2, x1b = rest = send(
         [
-            near_trips[2], (value2, "row", last_hops), (pair1, "row", along(1, False, False)),
-            (value2, axes, senders(cols - 1, bits[0], lambda i: True)), (short01, axes, pass_x(1, False)),
+            (value2, "row", last_hops), (value2, axes, senders(cols - 1, bits[0], lambda i: True)),
+            (short01, axes, pass_x(1, False)),
         ],
         *stage,
     )
+    main = main + rest
     (core1a,) = send([(jnp.where(at_mate, x1a, long01), axes, pass_core(1, True))], x2)
     stage = main + [core1a]
     inside2 = along(2, False, False)
@@ -568,8 +571,7 @@
         [(jnp.where(at_mate, mixed4, ends3), axes, senders(cols - 1 - bits[0], bits[1], x3_keep))], *stage4
     )
     row_high, row_low = place_last(plain(ends3, mixed4, core3), last_tables, *row_parts)
-    near_blocks = [(near, i) for near, (_, n) in zip((near0, near1, near2, near3), spans) for i in range(n)]
-    inner, inner_head, inner_tail = map_inner(y_table, covariance, near_blocks, row_high, row_low)
+    inner, inner_head, inner_tail = map_inner(y_table, covariance, [near0, near1, near2, near3], spans, row_high, row_low)
     far34, long13, over2, below, above = stage = send(
         [
             far_trips[2], (long12, "row", along(3, True)), (long02, "row", over),

time: 468 us -> 468 us (level)
  transfers between devices with their start and end apart: 35 -> 35, of which waited for: 15 -> 14; matrix products, arithmetic and copies ran while one was open for 9% -> 9% of each run, Pallas kernels for 28% -> 28%
where the time goes in v4:
time: 468 us; the launch traced here: 467 us
  Pallas kernels  167 us (36%)
  waiting for transfers between devices  145 us (31%)
  starting transfers between devices  97.5 us (21%)
  local copies, waits for them, and re-layouts  31.5 us (7%)
  other arithmetic  24.2 us (5%)
    pallas_call x10, Pallas kernels, call(): pl.pallas_call(kernel, grid_spec=pltpu.PrefetchScalarGridSpec(num_scalar_...  167 us
    ppermute x34, waiting for transfers between devices, send(): permute(value, axis, perm)  130 us
    ppermute x34, starting transfers between devices, send(): permute(value, axis, perm)  95.9 us
    ppermute x1, waiting for transfers between devices, body(): trade0 = permute(pick(1 - y), 'row', swap)  15 us
  transfers between devices with their start and end apart: 35, of which 14 were waited for; matrix products, arithmetic and copies ran while one was open for 9% of the time, Pallas kernels for 28%

profile of v4, /device:TPU:24, one launch (start us, length us, event | category | flops | bytes accessed | tf_op | source)
XLA Modules:
  0.0 466.6 jit_solution(1391883551195368667)
XLA Ops:
  0.0 3.9 constant_dynamic-slice_fusion.4
  5.5 6.9 %constant_dynamic-slice_fusion.10 = (f32[512,512]{1,0:T(8,128)}, f32[512,512]{1,0:T(8,128)}, f32[512,512]{1,0:T(8,128)}, f32[512,512]{1,0:T(8,128)}, f32[512,512...) fusion(f32[1536,3072]{1,0:T(8,128)} %own_b.5, s32[]{:T(128)S(6)} %select_n.237, ...), kind=kLoop, calls=%fused_computation.28 | loop fusion | bytes 16777224 | tf_op jit(solution)/shard_map/dynamic_slice | solution.py:432
  12.4 15.0 %collective-permute-done = f32[6,5,32,256]{3,2,1,0:T(8,128)S(1)} collective-permute-done((f32[6,5,32,256]{3,2,1,0:T(8,128)S(1)}, f32[6,5,32,256]{3,2,1,0:T(8,128)S(1)}, u32[]{:S(2)}, u32[]{:S(2)}) %collective-permute-start) | collective-permute-done | bytes 983072 | tf_op jit(solution)/shard_map/ppermute | solution.py:507
  27.4 1.6 pad_maximum_fusion.3.refs_0_
  31.9 5.9 %collective-permute-start.3 = (f32[2,6,5,32,256]{4,3,2,1,0:T(8,128)}, f32[2,6,5,32,256]{4,3,2,1,0:T(8,128)}, u32[]{:S(2)}, u32[]{:S(2)}) collective-permute-start(f32[2,6,5,32,256]{4,3,2,1,0:T(8,128)} %pad_maximum_fusion.3.refs_0_), channel_id=1, source_target_pairs={{4,12},{12,20},{20,28},{8,0},{16,8},{24,16},{5,13},{13,21},{21,29}... | collective-permute-start | bytes 5898248 | tf_op jit(solution)/shard_map/ppermute | solution.py:437
  37.8 14.2 %collective-permute-done.1 = f32[6,5,32,256]{3,2,1,0:T(8,128)} collective-permute-done((f32[6,5,32,256]{3,2,1,0:T(8,128)}, f32[6,5,32,256]{3,2,1,0:T(8,128)}, u32[]{:S(2)}, u32[]{:S(2)}) %collective-permute-start.1) | collective-permute-done | bytes 983072 | tf_op jit(solution)/shard_map/ppermute | solution.py:437
  52.0 2.0 collective-permute-start.5
  64.8 4.1 constant_dynamic-slice_fusion.12
  68.9 7.9 %collective-permute-done.4.refs_0_ = f32[512,512]{1,0:T(8,128)} collective-permute-done((f32[512,512]{1,0:T(8,128)}, f32[512,512]{1,0:T(8,128)}, u32[]{:S(2)}, u32[]{:S(2)}) %collective-permute-start.4) | collective-permute-done | bytes 1048608 | tf_op jit(solution)/shard_map/ppermute | solution.py:437
  81.7 2.8 pad_maximum_fusion.4.refs_8_
  92.3 32.5 %collective-permute-done.7 = f32[2,6,5,32,256]{4,3,2,1,0:T(8,128)S(1)} collective-permute-done((f32[2,6,5,32,256]{4,3,2,1,0:T(8,128)S(1)}, f32[2,6,5,32,256]{4,3,2,1,0:T(8,128)S(1)}, u32[]{:S(2)}, u32[]{:S(2)}) %collective-permute-start.7) | collective-permute-done | bytes 1966112 | tf_op jit(solution)/shard_map/ppermute | solution.py:437
  124.8 1.9 broadcast_select_fusion.refs_3_.refs_9_
  126.7 3.9 collective-permute-done.6.refs_1_
  130.6 1.9 collective-permute-start.14
  132.5 2.0 collective-permute-start.13
  134.5 7.9 %collective-permute-start.11 = (f32[2,6,5,32,256]{4,3,2,1,0:T(8,128)}, f32[2,6,5,32,256]{4,3,2,1,0:T(8,128)}, u32[]{:S(2)}, u32[]{:S(2)}) collective-permute-start(f32[2,6,5,32,256]{4,3,2,1,0:T(8,128)} %pad_maximum_fusion.4.refs_8_), channel_id=1, source_target_pairs={{4,12},{12,20},{16,8},{24,16},{5,13},{13,21},{17,9},{25,17},{6,14}... | collective-permute-start | bytes 5898248 | tf_op jit(solution)/shard_map/ppermute | solution.py:437
  143.7 1.6 broadcast_select_fusion.2
  146.7 1.9 broadcast_select_fusion.3
  148.6 1.9 broadcast_select_fusion.4
  150.6 2.2 pad_maximum_fusion
  152.8 29.9 %collective-permute-done.11.refs_10_ = f32[2,6,5,32,256]{4,3,2,1,0:T(8,128)} collective-permute-done((f32[2,6,5,32,256]{4,3,2,1,0:T(8,128)}, f32[2,6,5,32,256]{4,3,2,1,0:T(8,128)}, u32[]{:S(2)}, u32[]{:S(2)}) %collective-permute-start.11) | collective-permute-done | bytes 1966112 | tf_op jit(solution)/shard_map/ppermute | solution.py:437
  182.7 5.5 %collective-permute-done.12.refs_4_.refs_0_ = f32[2,6,5,32,256]{4,3,2,1,0:T(8,128)S(1)} collective-permute-done((f32[2,6,5,32,256]{4,3,2,1,0:T(8,128)}, f32[2,6,5,32,256]{4,3,2,1,0:T(8,128)S(1)}, u32[]{:S(2)}, u32[]{:S(2)}) %collective-permute-start.12) | collective-permute-done | bytes 1966112 | tf_op jit(solution)/shard_map/ppermute | solution.py:437
  188.2 2.0 broadcast_select_fusion.6
  193.9 5.6 %collective-permute-start.18 = (f32[512,512]{1,0:T(8,128)}, f32[512,512]{1,0:T(8,128)}, u32[]{:S(2)}, u32[]{:S(2)}) collective-permute-start(f32[512,512]{1,0:T(8,128)} %get-tuple-element.70), channel_id=1, source_target_pairs={{0,4},{4,0},{8,12},{12,8},{16,20},{20,16},{24,28},{28,24},{1,5},{5... | collective-permute-start | bytes 3145736 | tf_op jit(solution)/shard_map/ppermute | solution.py:437
  199.5 5.8 %collective-permute-start.19 = (f32[512,512]{1,0:T(8,128)}, f32[512,512]{1,0:T(8,128)}, u32[]{:S(2)}, u32[]{:S(2)}) collective-permute-start(f32[512,512]{1,0:T(8,128)} %get-tuple-element.71), channel_id=1, source_target_pairs={{4,8},{12,16},{20,24},{8,4},{16,12},{24,20},{5,9},{13,17},{21,25},... | collective-permute-start | bytes 3145736 | tf_op jit(solution)/shard_map/ppermute | solution.py:437
  205.3 8.9 %place_slabs.2 = (bf16[6,256,1280]{2,1,0:T(8,128)(2,1)}, bf16[6,256,1280]{2,1,0:T(8,128)(2,1)}) custom-call(s32[5]{0:T(128)} %stack.345.use, s32[5]{0:T(128)} %stack.348.source, s32[5]{0:T(128)} %stack.349.first, s32[30]{0:T(128)} %reshape.25.flags, f32[2,6,5,32,256]{4,3,2,1,0:T(8,128)} %pad_maximum_fusion.3.refs_0_, f32[2,6,5,32,256]{4,3,2,1,0:T(8,128)} %copy-done.4, ...), custom_call_target="tpu_custom_call" | custom-call | bytes 4915200 | tf_op jit(solution)/shard_map/place_slabs/pallas_call | solution.py:27
  214.2 1.9 broadcast_select_fusion.1
  216.1 2.0 copy-done.7
  218.1 9.5 %place_slabs.3 = (bf16[6,256,1280]{2,1,0:T(8,128)(2,1)}, bf16[6,256,1280]{2,1,0:T(8,128)(2,1)}) custom-call(s32[12]{0:T(128)} %stack.363.use, s32[12]{0:T(128)} %stack.364.source, s32[12]{0:T(128)} %stack.365.first, s32[30]{0:T(128)} %reshape.26.flags, f32[2,6,5,32,256]{4,3,2,1,0:T(8,128)} %pad_maximum_fusion.3.refs_0_, ...), custom_call_target="tpu_custom_call" | custom-call | bytes 13762560 | tf_op jit(solution)/shard_map/place_slabs/pallas_call | solution.py:27
  227.6 16.1 %collective-permute-done.18.refs_3_ = f32[512,512]{1,0:T(8,128)} collective-permute-done((f32[512,512]{1,0:T(8,128)}, f32[512,512]{1,0:T(8,128)}, u32[]{:S(2)}, u32[]{:S(2)}) %collective-permute-start.18) | collective-permute-done | bytes 1048608 | tf_op jit(solution)/shard_map/ppermute | solution.py:437
  243.7 1.8 collective-permute-done.17.refs_9_
  249.5 26.2 %collective-permute-start.24 = (f32[512,1024]{1,0:T(8,128)}, f32[512,1024]{1,0:T(8,128)S(1)}, u32[]{:S(2)}, u32[]{:S(2)}) collective-permute-start(f32[512,1024]{1,0:T(8,128)} %pad_maximum_fusion.2), channel_id=1, source_target_pairs={{4,8},{12,16},{20,24},{8,4},{16,12},{24,20},{5,9},{13,17},{21,25},... | collective-permute-start | bytes 6291464 | tf_op jit(solution)/shard_map/ppermute | solution.py:437
  275.7 6.2 %place_last.1 = (bf16[6,256,1280]{2,1,0:T(8,128)(2,1)}, bf16[6,256,1280]{2,1,0:T(8,128)(2,1)}) custom-call(s32[3]{0:T(128)} %add_convert_fusion.use, s32[3]{0:T(128)} %stack.371.source, s32[3]{0:T(128)} %stack.372.first, s32[30]{0:T(128)} %reshape.26.flags, s32[1]{0:T(128)} %bitcast.31.group, ...), custom_call_target="tpu_custom_call", output_to_operand_aliasing={{0}: (8, {}), {1}: (9, {})} | custom-call | bytes 6881280 | tf_op jit(solution)/shard_map/place_last/pallas_call | solution.py:27
  281.9 38.1 %map_inner.1 = (f32[3072,1024]{1,0:T(8,128)}, f32[512,1024]{1,0:T(8,128)}, f32[512,1024]{1,0:T(8,128)}) custom-call(s32[1]{0:T(128)} %bitcast.20.y, f32[1536,3072]{1,0:T(8,128)} %own_b.5, f32[512,512]{1,0:T(8,128)} %collective-permute-done.4.refs_0_, f32[512,1024]{1,0:T(8,128)} %copy-done.29, f32[512,1024]{1,0:T(8,128)} %collective-permute-done.15.refs_2_, ...), custom_call_target="tpu_custom_call" | custom-call | flops 24159191040 | bytes 20447232 | tf_op jit(solution)/shard_map/map_inner/pallas_call | solution.py:27
  322.0 1.6 collective-permute-start.26
  324.9 3.7 collective-permute-start.28
  330.0 2.6 collective-permute-start.30
  332.6 15.1 %map_outer.3 = (f32[512,512]{1,0:T(8,128)}, f32[512,512]{1,0:T(8,128)}, f32[512,512]{1,0:T(8,128)}) custom-call(s32[1]{0:T(128)} %bitcast.20.y, s32[3]{0:T(128)} %constant.102.clone.chunks, f32[1536,3072]{1,0:T(8,128)} %own_b.5, f32[1536,3072]{1,0:T(8,128)} %own_b.5, f32[512,512]{1,0:T(8,128)} %collective-permute-done.19.refs_0_, f32[512,1024]{1,0:T(8,128)} %copy-done.10, ...), custom_call_target="tpu_custom_call" | custom-call | flops 6039797760 | bytes 25427968 | tf_op jit(solution)/shard_map/map_outer/pallas_call | solution.py:27
  349.7 21.6 %cast_inner.1.refs_11_ = f32[3072,1536]{1,0:T(8,128)} custom-call(s32[2]{0:T(128)} %pad_add_fusion.1.table, f32[512,1024]{1,0:T(8,128)} %copy-done.8, f32[3072,1024]{1,0:T(8,128)} %get-tuple-element.85.mid, f32[512,1024]{1,0:T(8,128)} %copy-done.9, bf16[6,256,1280]{2,1,0:T(8,128)(2,1)} %get-tuple-element.74.high.refs_8_, ...), custom_call_target="tpu_custom_call" | custom-call | flops 12079595520 | bytes 21757952 | tf_op jit(solution)/shard_map/cast_inner/pallas_call | solution.py:27
  371.2 5.2 %collective-permute-done.29.refs_13_ = f32[2,6,5,32,256]{4,3,2,1,0:T(8,128)} collective-permute-done((f32[2,6,5,32,256]{4,3,2,1,0:T(8,128)}, f32[2,6,5,32,256]{4,3,2,1,0:T(8,128)}, u32[]{:S(2)}, u32[]{:S(2)}) %collective-permute-start.29) | collective-permute-done | bytes 1966112 | tf_op jit(solution)/shard_map/ppermute | solution.py:437
  376.5 2.7 collective-permute-start.34
  379.1 1.9 collective-permute-start.32
  381.1 1.8 collective-permute-start.31
  384.4 11.4 %map_outer.4 = (f32[512,512]{1,0:T(8,128)}, f32[512,512]{1,0:T(8,128)}) custom-call(s32[1]{0:T(128)} %bitcast.20.y, s32[2]{0:T(128)} %constant.103.clone.chunks, f32[1536,3072]{1,0:T(8,128)} %own_b.5, f32[1536,3072]{1,0:T(8,128)} %own_b.5, f32[512,1024]{1,0:T(8,128)} %collective-permute-done.28.refs_0_.refs_1_, ...), custom_call_target="tpu_custom_call" | custom-call | flops 4026531840 | bytes 24903680 | tf_op jit(solution)/shard_map/map_outer/pallas_call | solution.py:27
  395.8 11.4 %collective-permute-done.32.refs_0_ = f32[512,512]{1,0:T(8,128)} collective-permute-done((f32[512,512]{1,0:T(8,128)}, f32[512,512]{1,0:T(8,128)}, u32[]{:S(2)}, u32[]{:S(2)}) %collective-permute-start.32) | collective-permute-done | bytes 1048608 | tf_op jit(solution)/shard_map/ppermute | solution.py:437
  407.1 6.7 %map_outer.5.refs_4_ = f32[512,512]{1,0:T(8,128)} custom-call(s32[1]{0:T(128)} %bitcast.20.y, s32[1]{0:T(128)} %constant.104.clone.chunks, f32[1536,3072]{1,0:T(8,128)} %own_b.5, f32[1536,3072]{1,0:T(8,128)} %own_b.5, f32[512,512]{1,0:T(8,128)} %collective-permute-done.32.refs_0_, ...), custom_call_target="tpu_custom_call" | custom-call | flops 2013265920 | bytes 23330816 | tf_op jit(solution)/shard_map/map_outer/pallas_call | solution.py:27
  415.2 14.7 %cast_outer.1.refs_18_ = f32[3072,1536]{1,0:T(8,128)} custom-call(s32[3]{0:T(128)} %pad_add_fusion.2.table, f32[512,512]{1,0:T(8,128)} %copy-done.14, f32[512,512]{1,0:T(8,128)} %get-tuple-element.99.refs_1_, f32[512,512]{1,0:T(8,128)} %get-tuple-element.93.refs_2_, f32[512,512]{1,0:T(8,128)} %get-tuple-element.96.refs_3_, ...), custom_call_target="tpu_custom_call", output_to_operand_aliasing={{}: (12, {})} | custom-call | flops 6039797760 | bytes 27000832 | tf_op jit(solution)/shard_map/cast_outer/pallas_call | solution.py:27
  431.1 35.3 %cast_rest.1 = f32[3072,1536]{1,0:T(8,128)} custom-call(s32[4]{0:T(128)} %pad_add_fusion.table, s32[9]{0:T(128)} %stack.323.use, s32[9]{0:T(128)} %stack.331.source, s32[9]{0:T(128)} %stack.334.first, s32[30]{0:T(128)} %reshape.23.flags, f32[512,1024]{1,0:T(8,128)} %copy-done.8, ...), custom_call_target="tpu_custom_call", output_to_operand_aliasing={{}: (26, {})} | custom-call | flops 18119393280 | bytes 40304640 | tf_op jit(solution)/shard_map/cast_rest/pallas_call | solution.py:27
  (130 shorter events, 48.9 us)
Async XLA Ops:
  3.9 23.5 %collective-permute-start = (f32[6,5,32,256]{3,2,1,0:T(8,128)S(1)}, f32[6,5,32,256]{3,2,1,0:T(8,128)S(1)}, u32[]{:S(2)}, u32[]{:S(2)}) collective-permute-start(f32[6,5,32,256]{3,2,1,0:T(8,128)S(1)} %get-tuple-element.112), channel_id=1, source_target_pairs={{0,4},{4,0},{8,12},{12,8},{16,20},{20,16},{24,28},{28,24},{1,5},{5... | collective-permute-start | bytes 2949128 | tf_op jit(solution)/shard_map/ppermute | solution.py:507
  27.4 30.2 %copy-start.28 = (s32[48,5]{0,1:T(8,128)S(1)}, s32[48,5]{0,1:T(8,128)}, u32[]{:S(2)}) copy-start(s32[48,5]{0,1:T(8,128)} %param.9) | copy-start | bytes 2884
  29.1 22.9 %collective-permute-start.1 = (f32[6,5,32,256]{3,2,1,0:T(8,128)}, f32[6,5,32,256]{3,2,1,0:T(8,128)}, u32[]{:S(2)}, u32[]{:S(2)}) collective-permute-start(f32[6,5,32,256]{3,2,1,0:T(8,128)} %get-tuple-element.53), channel_id=1, source_target_pairs={{0,4},{4,0},{8,12},{12,8},{16,20},{20,16},{24,28},{28,24},{1,5},{5... | collective-permute-start | bytes 2949128 | tf_op jit(solution)/shard_map/ppermute | solution.py:437
  30.6 46.1 %collective-permute-start.2 = (f32[2,6,5,32,256]{4,3,2,1,0:T(8,128)}, f32[2,6,5,32,256]{4,3,2,1,0:T(8,128)S(1)}, u32[]{:S(2)}, u32[]{:S(2)}) collective-permute-start(f32[2,6,5,32,256]{4,3,2,1,0:T(8,128)} %pad_maximum_fusion.3.refs_0_), channel_id=1, source_target_pairs={{0,8},{8,16},{16,24},{12,4},{20,12},{28,20},{1,9},{9,17},{17,25},{... | collective-permute-start | bytes 5898248 | tf_op jit(solution)/shard_map/ppermute | solution.py:437
  31.9 45.5 %collective-permute-start.3 = (f32[2,6,5,32,256]{4,3,2,1,0:T(8,128)}, f32[2,6,5,32,256]{4,3,2,1,0:T(8,128)}, u32[]{:S(2)}, u32[]{:S(2)}) collective-permute-start(f32[2,6,5,32,256]{4,3,2,1,0:T(8,128)} %pad_maximum_fusion.3.refs_0_), channel_id=1, source_target_pairs={{4,12},{12,20},{20,28},{8,0},{16,8},{24,16},{5,13},{13,21},{21,29}... | collective-permute-start | bytes 5898248 | tf_op jit(solution)/shard_map/ppermute | solution.py:437
  52.0 25.4 %collective-permute-start.5 = (f32[2,6,5,32,256]{4,3,2,1,0:T(8,128)}, f32[2,6,5,32,256]{4,3,2,1,0:T(8,128)}, u32[]{:S(2)}, u32[]{:S(2)}) collective-permute-start(f32[2,6,5,32,256]{4,3,2,1,0:T(8,128)} %pad_maximum_fusion.3.refs_0_), channel_id=1, source_target_pairs={{0,2},{4,6},{9,11},{13,15},{18,16},{22,20},{27,25},{31,29}} | collective-permute-start | bytes 5898248 | tf_op jit(solution)/shard_map/ppermute | solution.py:437
  54.0 22.8 %collective-permute-start.4 = (f32[512,512]{1,0:T(8,128)}, f32[512,512]{1,0:T(8,128)}, u32[]{:S(2)}, u32[]{:S(2)}) collective-permute-start(f32[512,512]{1,0:T(8,128)} %get-tuple-element.56), channel_id=1, source_target_pairs={{0,4},{4,0},{8,12},{12,8},{16,20},{20,16},{24,28},{28,24},{1,5},{5... | collective-permute-start | bytes 3145736 | tf_op jit(solution)/shard_map/ppermute | solution.py:437
  64.8 16.8 %copy-start.20 = (f32[1,6,5,32,256]{4,3,2,1,0:T(8,128)S(1)}, f32[1,6,5,32,256]{4,3,2,1,0:T(8,128)}, u32[]{:S(2)}) copy-start(f32[1,6,5,32,256]{4,3,2,1,0:T(8,128)} %get-tuple-element.111) | copy-start | bytes 2949124
  76.8 9.6 %copy-start.4 = (f32[2,6,5,32,256]{4,3,2,1,0:T(8,128)}, f32[2,6,5,32,256]{4,3,2,1,0:T(8,128)S(1)}, u32[]{:S(2)}) copy-start(f32[2,6,5,32,256]{4,3,2,1,0:T(8,128)S(1)} %collective-permute-done.2.refs_1_.refs_3_) | copy-start | bytes 5898244
  79.6 45.2 %collective-permute-start.7 = (f32[2,6,5,32,256]{4,3,2,1,0:T(8,128)S(1)}, f32[2,6,5,32,256]{4,3,2,1,0:T(8,128)S(1)}, u32[]{:S(2)}, u32[]{:S(2)}) collective-permute-start(f32[2,6,5,32,256]{4,3,2,1,0:T(8,128)S(1)} %collective-permute-done.2.refs_1_.refs_3_), channel_id=1, source_target_pairs={{8,16},{16,24},{12,4},{20,12},{9,17},{17,25},{13,5},{21,13},{10,18... | collective-permute-start | bytes 5898248 | tf_op jit(solution)/shard_map/ppermute | solution.py:437
  80.9 43.9 %collective-permute-start.8 = (f32[2,6,5,32,256]{4,3,2,1,0:T(8,128)}, f32[2,6,5,32,256]{4,3,2,1,0:T(8,128)S(1)}, u32[]{:S(2)}, u32[]{:S(2)}) collective-permute-start(f32[2,6,5,32,256]{4,3,2,1,0:T(8,128)} %collective-permute-done.3.refs_2_.refs_6_), channel_id=1, source_target_pairs={{12,20},{20,28},{8,0},{16,8},{13,21},{21,29},{9,1},{17,9},{14,22},... | collective-permute-start | bytes 5898248 | tf_op jit(solution)/shard_map/ppermute | solution.py:437
  84.4 46.1 %collective-permute-start.6 = (f32[512,1024]{1,0:T(8,128)S(1)}, f32[512,1024]{1,0:T(8,128)S(1)}, u32[]{:S(2)}, u32[]{:S(2)}) collective-permute-start(f32[512,1024]{1,0:T(8,128)S(1)} %get-tuple-element.58), channel_id=1, source_target_pairs={{0,4},{4,0},{8,12},{12,8},{16,20},{20,16},{24,28},{28,24},{1,5},{5... | collective-permute-start | bytes 6291464 | tf_op jit(solution)/shard_map/ppermute | solution.py:437
  86.4 40.3 %collective-permute-start.9 = (f32[2,6,5,32,256]{4,3,2,1,0:T(8,128)S(1)}, f32[2,6,5,32,256]{4,3,2,1,0:T(8,128)S(1)}, u32[]{:S(2)}, u32[]{:S(2)}) collective-permute-start(f32[2,6,5,32,256]{4,3,2,1,0:T(8,128)S(1)} %collective-permute-done.2.refs_1_.refs_3_), channel_id=1, source_target_pairs={{4,6},{9,11},{13,15},{18,16},{22,20},{27,25}} | collective-permute-start | bytes 5898248 | tf_op jit(solution)/shard_map/ppermute | solution.py:437
  87.2 39.5 %collective-permute-start.10 = (f32[2,6,5,32,256]{4,3,2,1,0:T(8,128)S(1)}, f32[2,6,5,32,256]{4,3,2,1,0:T(8,128)S(1)}, u32[]{:S(2)}, u32[]{:S(2)}) collective-permute-start(f32[2,6,5,32,256]{4,3,2,1,0:T(8,128)S(1)} %broadcast_select_fusion.5), channel_id=1, source_target_pairs={{0,1},{2,3},{4,5},{6,7},{9,8},{11,10},{13,12},{15,14},{16,17},{18,... | collective-permute-start | bytes 5898248 | tf_op jit(solution)/shard_map/ppermute | solution.py:437
  92.3 51.4 %copy-start.5 = (f32[2,6,5,32,256]{4,3,2,1,0:T(8,128)S(1)}, f32[2,6,5,32,256]{4,3,2,1,0:T(8,128)}, u32[]{:S(2)}) copy-start(f32[2,6,5,32,256]{4,3,2,1,0:T(8,128)} %copy-done.4) | copy-start | bytes 5898244
  126.7 18.7 %copy-start.11 = (f32[2,6,5,32,256]{4,3,2,1,0:T(8,128)}, f32[2,6,5,32,256]{4,3,2,1,0:T(8,128)S(1)}, u32[]{:S(2)}) copy-start(f32[2,6,5,32,256]{4,3,2,1,0:T(8,128)S(1)} %collective-permute-done.9.refs_4_) | copy-start | bytes 5898244
  126.7 18.7 %copy-start.27 = (f32[2,6,5,32,256]{4,3,2,1,0:T(8,128)}, f32[2,6,5,32,256]{4,3,2,1,0:T(8,128)S(1)}, u32[]{:S(2)}) copy-start(f32[2,6,5,32,256]{4,3,2,1,0:T(8,128)S(1)} %collective-permute-done.10.refs_2_) | copy-start | bytes 5898244
  130.6 14.8 %copy-start.29 = (f32[512,1024]{1,0:T(8,128)}, f32[512,1024]{1,0:T(8,128)S(1)}, u32[]{:S(2)}) copy-start(f32[512,1024]{1,0:T(8,128)S(1)} %collective-permute-done.6.refs_1_) | copy-start | bytes 6291460
  130.6 14.8 %collective-permute-start.14 = (f32[2,6,5,32,256]{4,3,2,1,0:T(8,128)}, f32[2,6,5,32,256]{4,3,2,1,0:T(8,128)}, u32[]{:S(2)}, u32[]{:S(2)}) collective-permute-start(f32[2,6,5,32,256]{4,3,2,1,0:T(8,128)} %broadcast_select_fusion.refs_3_.refs_9_), channel_id=1, source_target_pairs={{0,2},{4,6},{9,11},{13,15},{18,16},{22,20},{27,25},{31,29}} | collective-permute-start | bytes 5898248 | tf_op jit(solution)/shard_map/ppermute | solution.py:437
  132.5 16.1 %collective-permute-start.13 = (f32[2,6,5,32,256]{4,3,2,1,0:T(8,128)}, f32[2,6,5,32,256]{4,3,2,1,0:T(8,128)}, u32[]{:S(2)}, u32[]{:S(2)}) collective-permute-start(f32[2,6,5,32,256]{4,3,2,1,0:T(8,128)} %collective-permute-done.3.refs_2_.refs_6_), channel_id=1, source_target_pairs={{0,2},{9,11},{13,15},{18,16},{22,20},{31,29}} | collective-permute-start | bytes 5898248 | tf_op jit(solution)/shard_map/ppermute | solution.py:437
  134.5 48.2 %collective-permute-start.11 = (f32[2,6,5,32,256]{4,3,2,1,0:T(8,128)}, f32[2,6,5,32,256]{4,3,2,1,0:T(8,128)}, u32[]{:S(2)}, u32[]{:S(2)}) collective-permute-start(f32[2,6,5,32,256]{4,3,2,1,0:T(8,128)} %pad_maximum_fusion.4.refs_8_), channel_id=1, source_target_pairs={{4,12},{12,20},{16,8},{24,16},{5,13},{13,21},{17,9},{25,17},{6,14}... | collective-permute-start | bytes 5898248 | tf_op jit(solution)/shard_map/ppermute | solution.py:437
  142.3 45.8 %collective-permute-start.12 = (f32[2,6,5,32,256]{4,3,2,1,0:T(8,128)}, f32[2,6,5,32,256]{4,3,2,1,0:T(8,128)S(1)}, u32[]{:S(2)}, u32[]{:S(2)}) collective-permute-start(f32[2,6,5,32,256]{4,3,2,1,0:T(8,128)} %broadcast_select_fusion.refs_3_.refs_9_), channel_id=1, source_target_pairs={{16,24},{12,4},{20,28},{8,0},{17,25},{13,5},{21,29},{9,1},{18,26},... | collective-permute-start | bytes 5898248 | tf_op jit(solution)/shard_map/ppermute | solution.py:437
  143.6 46.7 %collective-permute-start.15 = (f32[512,1024]{1,0:T(8,128)}, f32[512,1024]{1,0:T(8,128)}, u32[]{:S(2)}, u32[]{:S(2)}) collective-permute-start(f32[512,1024]{1,0:T(8,128)} %get-tuple-element.67), channel_id=1, source_target_pairs={{0,4},{4,0},{8,12},{12,8},{16,20},{20,16},{24,28},{28,24},{1,5},{5... | collective-permute-start | bytes 6291464 | tf_op jit(solution)/shard_map/ppermute | solution.py:437
  145.4 45.0 %collective-permute-start.16 = (f32[2,6,5,32,256]{4,3,2,1,0:T(8,128)}, f32[2,6,5,32,256]{4,3,2,1,0:T(8,128)}, u32[]{:S(2)}, u32[]{:S(2)}) collective-permute-start(f32[2,6,5,32,256]{4,3,2,1,0:T(8,128)} %broadcast_select_fusion.2), channel_id=1, source_target_pairs={{4,5},{6,7},{9,8},{11,10},{13,12},{15,14},{16,17},{18,19},{20,21},... | collective-permute-start | bytes 5898248 | tf_op jit(solution)/shard_map/ppermute | solution.py:437
  190.4 23.8 %copy-start.1 = (f32[2,6,5,32,256]{4,3,2,1,0:T(8,128)S(1)}, f32[2,6,5,32,256]{4,3,2,1,0:T(8,128)}, u32[]{:S(2)}) copy-start(f32[2,6,5,32,256]{4,3,2,1,0:T(8,128)} %copy-done) | copy-start | bytes 5898244
  190.4 25.8 %collective-permute-start.21 = (f32[4,6,5,32,256]{4,3,2,1,0:T(8,128)}, f32[4,6,5,32,256]{4,3,2,1,0:T(8,128)S(1)}, u32[]{:S(2)}, u32[]{:S(2)}) collective-permute-start(f32[4,6,5,32,256]{4,3,2,1,0:T(8,128)} %pad_maximum_fusion), channel_id=1, source_target_pairs={{0,1},{2,3},{4,5},{6,7},{9,8},{11,10},{13,12},{15,14},{16,17},{18,... | collective-permute-start | bytes 11796488 | tf_op jit(solution)/shard_map/ppermute | solution.py:437
  191.8 22.4 %collective-permute-start.20 = (f32[2,6,5,32,256]{4,3,2,1,0:T(8,128)}, f32[2,6,5,32,256]{4,3,2,1,0:T(8,128)S(1)}, u32[]{:S(2)}, u32[]{:S(2)}) collective-permute-start(f32[2,6,5,32,256]{4,3,2,1,0:T(8,128)} %broadcast_select_fusion.6), channel_id=1, source_target_pairs={{12,20},{13,21},{14,22},{15,23},{16,8},{17,9},{18,10},{19,11},{0,2... | collective-permute-start | bytes 5898248 | tf_op jit(solution)/shard_map/ppermute | solution.py:437
  192.6 52.9 %collective-permute-start.17 = (f32[2,6,5,32,256]{4,3,2,1,0:T(8,128)}, f32[2,6,5,32,256]{4,3,2,1,0:T(8,128)}, u32[]{:S(2)}, u32[]{:S(2)}) collective-permute-start(f32[2,6,5,32,256]{4,3,2,1,0:T(8,128)} %pad_maximum_fusion.4.refs_8_), channel_id=1, source_target_pairs={{0,8},{8,16},{16,24},{12,4},{20,12},{28,20},{1,9},{9,17},{17,25},{... | collective-permute-start | bytes 5898248 | tf_op jit(solution)/shard_map/ppermute | solution.py:437
  193.9 49.8 %collective-permute-start.18 = (f32[512,512]{1,0:T(8,128)}, f32[512,512]{1,0:T(8,128)}, u32[]{:S(2)}, u32[]{:S(2)}) collective-permute-start(f32[512,512]{1,0:T(8,128)} %get-tuple-element.70), channel_id=1, source_target_pairs={{0,4},{4,0},{8,12},{12,8},{16,20},{20,16},{24,28},{28,24},{1,5},{5... | collective-permute-start | bytes 3145736 | tf_op jit(solution)/shard_map/ppermute | solution.py:437
  199.5 44.2 %collective-permute-start.19 = (f32[512,512]{1,0:T(8,128)}, f32[512,512]{1,0:T(8,128)}, u32[]{:S(2)}, u32[]{:S(2)}) collective-permute-start(f32[512,512]{1,0:T(8,128)} %get-tuple-element.71), channel_id=1, source_target_pairs={{4,8},{12,16},{20,24},{8,4},{16,12},{24,20},{5,9},{13,17},{21,25},... | collective-permute-start | bytes 3145736 | tf_op jit(solution)/shard_map/ppermute | solution.py:437
  216.1 31.9 %copy-start.6 = (f32[2,6,5,32,256]{4,3,2,1,0:T(8,128)S(1)}, f32[2,6,5,32,256]{4,3,2,1,0:T(8,128)}, u32[]{:S(2)}) copy-start(f32[2,6,5,32,256]{4,3,2,1,0:T(8,128)} %copy-done.4) | copy-start | bytes 5898244
  245.5 30.3 %collective-permute-start.23 = (f32[2,6,5,32,256]{4,3,2,1,0:T(8,128)}, f32[2,6,5,32,256]{4,3,2,1,0:T(8,128)}, u32[]{:S(2)}, u32[]{:S(2)}) collective-permute-start(f32[2,6,5,32,256]{4,3,2,1,0:T(8,128)} %broadcast_select_fusion.1), channel_id=1, source_target_pairs={{0,1},{2,3},{4,5},{6,7},{25,24},{27,26},{29,28},{31,30}} | collective-permute-start | bytes 5898248 | tf_op jit(solution)/shard_map/ppermute | solution.py:437
  246.8 73.3 %collective-permute-start.22 = (f32[2,6,5,32,256]{4,3,2,1,0:T(8,128)}, f32[2,6,5,32,256]{4,3,2,1,0:T(8,128)S(1)}, u32[]{:S(2)}, u32[]{:S(2)}) collective-permute-start(f32[2,6,5,32,256]{4,3,2,1,0:T(8,128)} %collective-permute-done.17.refs_9_), channel_id=1, source_target_pairs={{8,16},{16,24},{12,4},{20,12},{9,17},{17,25},{13,5},{21,13},{10,18... | collective-permute-start | bytes 5898248 | tf_op jit(solution)/shard_map/ppermute | solution.py:437
  248.1 72.0 %collective-permute-start.25 = (f32[2,6,5,32,256]{4,3,2,1,0:T(8,128)S(1)}, f32[2,6,5,32,256]{4,3,2,1,0:T(8,128)S(1)}, u32[]{:S(2)}, u32[]{:S(2)}) collective-permute-start(f32[2,6,5,32,256]{4,3,2,1,0:T(8,128)S(1)} %copy-done.6), channel_id=1, source_target_pairs={{4,0},{24,28},{5,1},{25,29},{6,2},{26,30},{7,3},{27,31}} | collective-permute-start | bytes 5898248 | tf_op jit(solution)/shard_map/ppermute | solution.py:437
  249.5 71.9 %collective-permute-start.24 = (f32[512,1024]{1,0:T(8,128)}, f32[512,1024]{1,0:T(8,128)S(1)}, u32[]{:S(2)}, u32[]{:S(2)}) collective-permute-start(f32[512,1024]{1,0:T(8,128)} %pad_maximum_fusion.2), channel_id=1, source_target_pairs={{4,8},{12,16},{20,24},{8,4},{16,12},{24,20},{5,9},{13,17},{21,25},... | collective-permute-start | bytes 6291464 | tf_op jit(solution)/shard_map/ppermute | solution.py:437
  321.4 11.2 %copy-start.10 = (f32[512,1024]{1,0:T(8,128)}, f32[512,1024]{1,0:T(8,128)S(1)}, u32[]{:S(2)}) copy-start(f32[512,1024]{1,0:T(8,128)S(1)} %collective-permute-done.24.refs_1_.refs_2_) | copy-start | bytes 6291460
  322.0 25.7 %collective-permute-start.26 = (f32[512,1024]{1,0:T(8,128)}, f32[512,1024]{1,0:T(8,128)S(1)}, u32[]{:S(2)}, u32[]{:S(2)}) collective-permute-start(f32[512,1024]{1,0:T(8,128)} %get-tuple-element.86), channel_id=1, source_target_pairs={{0,1},{1,2},{2,3},{4,5},{5,6},{6,7},{8,9},{9,10},{10,11},{12,13},{... | collective-permute-start | bytes 6291464 | tf_op jit(solution)/shard_map/ppermute | solution.py:437
  323.6 24.1 %collective-permute-start.27 = (f32[512,1024]{1,0:T(8,128)}, f32[512,1024]{1,0:T(8,128)S(1)}, u32[]{:S(2)}, u32[]{:S(2)}) collective-permute-start(f32[512,1024]{1,0:T(8,128)} %get-tuple-element.87), channel_id=1, source_target_pairs={{1,0},{2,1},{3,2},{5,4},{6,5},{7,6},{9,8},{10,9},{11,10},{13,12},{... | collective-permute-start | bytes 6291464 | tf_op jit(solution)/shard_map/ppermute | solution.py:437
  324.9 51.5 %collective-permute-start.28 = (f32[512,1024]{1,0:T(8,128)}, f32[512,1024]{1,0:T(8,128)}, u32[]{:S(2)}, u32[]{:S(2)}) collective-permute-start(f32[512,1024]{1,0:T(8,128)} %pad_maximum_fusion.1), channel_id=1, source_target_pairs={{4,8},{12,16},{20,24},{8,4},{16,12},{24,20},{5,9},{13,17},{21,25},... | collective-permute-start | bytes 6291464 | tf_op jit(solution)/shard_map/ppermute | solution.py:437
  328.7 47.8 %collective-permute-start.29 = (f32[2,6,5,32,256]{4,3,2,1,0:T(8,128)}, f32[2,6,5,32,256]{4,3,2,1,0:T(8,128)}, u32[]{:S(2)}, u32[]{:S(2)}) collective-permute-start(f32[2,6,5,32,256]{4,3,2,1,0:T(8,128)} %copy-done.24), channel_id=1, source_target_pairs={{16,24},{12,4},{17,25},{13,5},{18,26},{14,6},{19,27},{15,7}} | collective-permute-start | bytes 5898248 | tf_op jit(solution)/shard_map/ppermute | solution.py:437
  330.0 46.5 %collective-permute-start.30 = (f32[2,6,5,32,256]{4,3,2,1,0:T(8,128)}, f32[2,6,5,32,256]{4,3,2,1,0:T(8,128)}, u32[]{:S(2)}, u32[]{:S(2)}) collective-permute-start(f32[2,6,5,32,256]{4,3,2,1,0:T(8,128)} %copy-done.23), channel_id=1, source_target_pairs={{4,0},{24,28},{5,1},{25,29},{6,2},{26,30},{7,3},{27,31}} | collective-permute-start | bytes 5898248 | tf_op jit(solution)/shard_map/ppermute | solution.py:437
  349.7 26.8 %copy-start.2 = (f32[2,6,5,32,256]{4,3,2,1,0:T(8,128)S(1)}, f32[2,6,5,32,256]{4,3,2,1,0:T(8,128)}, u32[]{:S(2)}) copy-start(f32[2,6,5,32,256]{4,3,2,1,0:T(8,128)} %copy-done) | copy-start | bytes 5898244
  349.7 31.4 %copy-start.13 = (f32[512,512]{1,0:T(8,128)S(1)}, f32[512,512]{1,0:T(8,128)}, u32[]{:S(2)}) copy-start(f32[512,512]{1,0:T(8,128)} %get-tuple-element.95.refs_6_) | copy-start | bytes 3145732
  349.7 33.2 %copy-start.12 = (f32[512,512]{1,0:T(8,128)S(1)}, f32[512,512]{1,0:T(8,128)}, u32[]{:S(2)}) copy-start(f32[512,512]{1,0:T(8,128)} %get-tuple-element.99.refs_1_) | copy-start | bytes 3145732
  376.5 53.4 %collective-permute-start.34 = (f32[2,6,5,32,256]{4,3,2,1,0:T(8,128)S(1)}, f32[2,6,5,32,256]{4,3,2,1,0:T(8,128)S(1)}, u32[]{:S(2)}, u32[]{:S(2)}) collective-permute-start(f32[2,6,5,32,256]{4,3,2,1,0:T(8,128)S(1)} %copy-done.2), channel_id=1, source_target_pairs={{4,0},{24,28},{5,1},{25,29},{6,2},{26,30},{7,3},{27,31}} | collective-permute-start | bytes 5898248 | tf_op jit(solution)/shard_map/ppermute | solution.py:437
  379.1 28.0 %collective-permute-start.32 = (f32[512,512]{1,0:T(8,128)}, f32[512,512]{1,0:T(8,128)}, u32[]{:S(2)}, u32[]{:S(2)}) collective-permute-start(f32[512,512]{1,0:T(8,128)} %get-tuple-element.97), channel_id=1, source_target_pairs={{4,8},{12,16},{20,24},{8,4},{16,12},{24,20},{5,9},{13,17},{21,25},... | collective-permute-start | bytes 3145736 | tf_op jit(solution)/shard_map/ppermute | solution.py:437
  381.1 32.7 %collective-permute-start.31 = (f32[512,512]{1,0:T(8,128)S(1)}, f32[512,512]{1,0:T(8,128)S(1)}, u32[]{:S(2)}, u32[]{:S(2)}) collective-permute-start(f32[512,512]{1,0:T(8,128)S(1)} %copy-done.13), channel_id=1, source_target_pairs={{0,1},{1,2},{2,3},{4,5},{5,6},{6,7},{8,9},{9,10},{10,11},{12,13},{... | collective-permute-start | bytes 3145736 | tf_op jit(solution)/shard_map/ppermute | solution.py:437
  382.9 30.9 %collective-permute-start.33 = (f32[512,512]{1,0:T(8,128)S(1)}, f32[512,512]{1,0:T(8,128)S(1)}, u32[]{:S(2)}, u32[]{:S(2)}) collective-permute-start(f32[512,512]{1,0:T(8,128)S(1)} %copy-done.12), channel_id=1, source_target_pairs={{1,0},{2,1},{3,2},{5,4},{6,5},{7,6},{9,8},{10,9},{11,10},{13,12},{... | collective-permute-start | bytes 3145736 | tf_op jit(solution)/shard_map/ppermute | solution.py:437
  (17 other events, 35.9 us)
